TPU v7x, 32 devices: a whole 2x2x4 slice. The times are simulated.
32 devices in a mesh: dp: 4 (over z), expert: 8 (over y, x, core).
Axes of the slice: x: 2, y: 2, z: 4, core: 2. Of those that a mesh axis runs over, the one named last changes fastest.
Arguments:
- tokens: bfloat16 [4096, 2048], P(('dp', 'expert')), may hold values from -6 to 6
- attn_query: bfloat16 [2048, 2048], P(('dp', 'expert')), may hold values from -0.125 to 0.125
- attn_key: bfloat16 [2048, 2048], P(('dp', 'expert')), may hold values from -0.125 to 0.125
- attn_value: bfloat16 [2048, 2048], P(('dp', 'expert')), may hold values from -0.125 to 0.125
- attn_output: bfloat16 [2048, 2048], P(('dp', 'expert')), may hold values from -2 to 2
- norm_in: bfloat16 [2048], P(('dp', 'expert')), may hold values from 0.25 to 1.75
- norm_query: bfloat16 [2048], P(('dp', 'expert')), may hold values from 0.25 to 1.75
- norm_key: bfloat16 [2048], P(('dp', 'expert')), may hold values from 0.25 to 1.75
- norm_mid: bfloat16 [2048], P(('dp', 'expert')), may hold values from 0.25 to 1.75
- router: bfloat16 [2048, 16], P(('dp', 'expert')), may hold values from -0.0625 to 0.0625
- expert_gate: bfloat16 [16, 2048, 1024], P('expert'), may hold values from -0.125 to 0.125
- expert_up: bfloat16 [16, 2048, 1024], P('expert'), may hold values from -0.125 to 0.125
- expert_down: bfloat16 [16, 1024, 2048], P('expert'), may hold values from -0.75 to 0.75
- routes: int32 [4096, 8], P(('dp', 'expert')), may hold values from 0 to 15, all different within a row; in each aligned block of 128 rows (0 to 127, 128 to 255, ...) at most 68 rows name the same one
- pieces: int32 [4096], P(('dp', 'expert')), may hold values from 0 to 5, as said below
- cotangent: bfloat16 [4096, 2048], P(('dp', 'expert')), may hold values from -6 to 6
Outputs:
- output: bfloat16 [4096, 2048], P(('dp', 'expert'))
- input_grad: float32 [4096, 2048], P(('dp', 'expert'))
- query_grad: float32 [2048, 2048], P(('dp', 'expert'))
- key_grad: float32 [2048, 2048], P(('dp', 'expert'))
- value_grad: float32 [2048, 2048], P(('dp', 'expert'))
- output_grad: float32 [2048, 2048], P(('dp', 'expert'))
- norm_in_grad: float32 [2048], P(('dp', 'expert'))
- norm_query_grad: float32 [2048], P(('dp', 'expert'))
- norm_key_grad: float32 [2048], P(('dp', 'expert'))
- norm_mid_grad: float32 [2048], P(('dp', 'expert'))
- router_grad: float32 [2048, 16], P(('dp', 'expert'))
- gate_grad: float32 [16, 2048, 1024], P('expert', 'dp')
- up_grad: float32 [16, 2048, 1024], P('expert', 'dp')
- down_grad: float32 [16, 1024, 2048], P('expert', None, 'dp')
Inputs may be any that keep to these rules, and one draw needn't show every extreme that they name: `routes`: each row names 8 different experts. No expert is named by more than 68 of the rows of one device, and in every draw some expert is named by exactly 68 rows of some device. 0 marks text. Tokens of one sequence with the same positive number form one picture piece: consecutive tokens, at most 256 of them, beginning at the sequence's start or at a position p where p + 128 is a multiple of 256. Different pieces of a sequence have different numbers. The last token of every sequence belongs to a picture piece.
All inputs are finite; a program needn't handle non-finite values.
Results may differ from a plain program's by a relative error of at most 0.018.
Values may be sent and summed in bfloat16 or wider, within the bound.
No kernel may reach another device: no remote copies, remote signals or barrier semaphores. Data moves between devices by JAX's collectives and lax.ppermute only.
A program may use at most 320 MiB of HBM per device.

v0:
```python
import math

import jax
import jax.numpy as jnp
from jax import lax
from jax.sharding import PartitionSpec as P

HEADS = 16
HEAD = 128


eps_norm = 1e-05
rope_base = 10000.0


def rms_scale(values, gain_vector):
    return (
        values
        * lax.rsqrt(jnp.mean(values * values, axis=-1, keepdims=True) + eps_norm)
        * gain_vector
    )


def angle_tables(positions, head_size):
    half_size = head_size // 2
    inverse = jnp.exp(
        jnp.arange(half_size, dtype=jnp.float32) * (-2.0 * math.log(rope_base) / head_size)
    )
    angles = positions[:, None] * inverse[None, :]
    return (jnp.cos(angles)[:, None, :], jnp.sin(angles)[:, None, :])


def rotate(values, cosine, sine_table):
    half_size = values.shape[-1] // 2
    first_half = values[..., :half_size]
    second = values[..., half_size:]
    return jnp.concatenate(
        [first_half * cosine - second * sine_table, second * cosine + first_half * sine_table],
        axis=-1,
    )


def softmax_rows(scores):
    highest = jnp.max(scores, axis=-1, keepdims=True)
    exponent = jnp.exp(scores - highest)
    return exponent / jnp.sum(exponent, axis=-1, keepdims=True)


def expert_forward(incoming, expert_gate, expert_up):
    gate_act = jnp.einsum(
        "sjcd,jdf->sjcf", incoming, expert_gate, preferred_element_type=jnp.float32
    )
    up_act = jnp.einsum("sjcd,jdf->sjcf", incoming, expert_up, preferred_element_type=jnp.float32)
    hidden = (jax.nn.silu(gate_act) * up_act).astype(jnp.bfloat16)
    return (gate_act, up_act, hidden)


def per_device(
    tokens,
    attn_query,
    attn_key,
    attn_value,
    attn_output,
    norm_in,
    norm_query,
    norm_key,
    norm_mid,
    router,
    expert_gate,
    expert_up,
    expert_down,
    routes,
    pieces,
    cotangent,
):
    single = jnp.float32
    bfloat = jnp.bfloat16
    tok_rows = tokens.shape[0]
    model = tokens.shape[1]
    top_count = routes.shape[1]
    experts = router.shape[1]
    groups = lax.axis_size("expert")
    local_experts = expert_gate.shape[0]
    capacity = min(tok_rows, tok_rows * top_count // experts + tok_rows // 32)
    length = tok_rows * groups
    scale = HEAD ** (-0.5)
    (
        query_full,
        key_full,
        value_full,
        output_full,
        router_full,
        gain_in,
        gain_query,
        gain_key,
        gain_mid,
    ) = (
        lax.all_gather(attn_query, ("dp", "expert"), axis=0, tiled=True),
        lax.all_gather(attn_key, ("dp", "expert"), axis=0, tiled=True),
        lax.all_gather(attn_value, ("dp", "expert"), axis=0, tiled=True),
        lax.all_gather(attn_output, ("dp", "expert"), axis=0, tiled=True),
        lax.all_gather(router, ("dp", "expert"), axis=0, tiled=True),
        lax.all_gather(norm_in, ("dp", "expert"), axis=0, tiled=True),
        lax.all_gather(norm_query, ("dp", "expert"), axis=0, tiled=True),
        lax.all_gather(norm_key, ("dp", "expert"), axis=0, tiled=True),
        lax.all_gather(norm_mid, ("dp", "expert"), axis=0, tiled=True),
    )
    gain_in = gain_in.astype(single)
    gain_query = gain_query.astype(single)
    gain_key = gain_key.astype(single)
    gain_mid = gain_mid.astype(single)
    token_values = tokens.astype(single)
    normed, norm_in_back = jax.vjp(rms_scale, token_values, gain_in)
    normed_b = normed.astype(bfloat)
    query_raw = jnp.dot(normed_b, query_full, preferred_element_type=single)
    key_raw = jnp.dot(normed_b, key_full, preferred_element_type=single)
    value_raw = jnp.dot(normed_b, value_full, preferred_element_type=single)
    query_place = lax.axis_index("expert") * tok_rows + jnp.arange(tok_rows, dtype=jnp.int32)
    cosine, sine_table = angle_tables(query_place.astype(single), HEAD)

    def to_heads(raw_rows, gain_vector):
        return rotate(
            rms_scale(raw_rows, gain_vector).reshape(tok_rows, HEADS, HEAD), cosine, sine_table
        )

    query_rot, query_back = jax.vjp(to_heads, query_raw, gain_query)
    key_rot, key_back = jax.vjp(to_heads, key_raw, gain_key)
    query_b = query_rot.astype(bfloat)
    key_b = key_rot.astype(bfloat).reshape(tok_rows, model)
    value_b = value_raw.astype(bfloat)
    piece_b = pieces.astype(bfloat)
    key_all, value_all, piece_all = (
        lax.all_gather(key_b, "expert", axis=0, tiled=True),
        lax.all_gather(value_b, "expert", axis=0, tiled=True),
        lax.all_gather(piece_b, "expert", axis=0, tiled=True),
    )
    key_place = jnp.arange(length, dtype=jnp.int32)

    def masked_scores(key_rows, piece_rows):
        allowed = (key_place[None, :] <= query_place[:, None]) | (
            piece_b[:, None] == piece_rows[None, :]
        ) & (pieces[:, None] > 0)
        raw_scores = (
            jnp.einsum(
                "qhd,khd->hqk",
                query_b,
                key_rows.reshape(length, HEADS, HEAD),
                preferred_element_type=single,
            )
            * scale
        )
        return jnp.where(allowed[None], raw_scores, -1e30)

    scores = masked_scores(key_all, piece_all)
    highest = jnp.max(scores, axis=-1, keepdims=True)
    exponent = jnp.exp(scores - highest)
    total_mass = jnp.sum(exponent, axis=-1, keepdims=True)
    log_mass = highest + jnp.log(total_mass)
    weights_b = (exponent / total_mass).astype(bfloat)
    attended = (
        jnp.einsum(
            "hqk,khd->qhd",
            weights_b,
            value_all.reshape(length, HEADS, HEAD),
            preferred_element_type=single,
        )
        .reshape(tok_rows, model)
        .astype(bfloat)
    )
    residual = token_values + jnp.dot(attended, output_full, preferred_element_type=single)
    normed_mid, norm_mid_back = jax.vjp(rms_scale, residual, gain_mid)
    mid_b = normed_mid.astype(bfloat)
    logits = jnp.dot(mid_b, router_full, preferred_element_type=single)
    router_probs = softmax_rows(logits)
    expert_ids = jnp.arange(experts, dtype=jnp.int32)
    hits = routes[:, :, None] == expert_ids[None, None, :]
    route_gate = jnp.sum(jnp.where(hits, router_probs[:, None, :], 0.0), axis=-1)
    flat_routes = routes.reshape(-1)
    onehot = (flat_routes[:, None] == expert_ids[None, :]).astype(jnp.int32)
    rank_in = jnp.sum((jnp.cumsum(onehot, axis=0) - 1) * onehot, axis=1)
    slot_of = flat_routes * capacity + rank_in
    route_total = tok_rows * top_count
    owner = (
        jnp.full((experts * capacity,), route_total, jnp.int32)
        .at[slot_of]
        .set(jnp.arange(route_total, dtype=jnp.int32))
    )
    source_row = owner // top_count
    outgoing = jnp.concatenate([mid_b, jnp.zeros((1, model), bfloat)], axis=0)[source_row].reshape(
        experts, capacity, model
    )
    incoming = lax.all_to_all(outgoing, "expert", split_axis=0, concat_axis=0, tiled=True).reshape(
        groups, local_experts, capacity, model
    )
    gate_act, up_act, hidden = expert_forward(incoming, expert_gate, expert_up)
    returned = jnp.einsum(
        "sjcf,jfd->sjcd", hidden, expert_down, preferred_element_type=single
    ).astype(bfloat)
    arrived = lax.all_to_all(
        returned.reshape(experts, capacity, model),
        "expert",
        split_axis=0,
        concat_axis=0,
        tiled=True,
    ).reshape(experts * capacity, model)
    per_route = arrived[slot_of].reshape(tok_rows, top_count, model).astype(single)
    moe_out = jnp.sum(route_gate[:, :, None] * per_route, axis=1)
    output = (residual + moe_out).astype(bfloat)
    grad_out = cotangent.astype(single)
    gate_grad_route = jnp.sum(grad_out[:, None, :] * per_route, axis=-1)
    gate_slot = jnp.concatenate([route_gate.reshape(-1), jnp.zeros((1,), single)])[owner]
    grad_slot = jnp.concatenate([grad_out, jnp.zeros((1, model), single)], axis=0)[source_row]
    grad_rows = (gate_slot[:, None] * grad_slot).astype(bfloat).reshape(experts, capacity, model)
    grad_in_rows = lax.all_to_all(
        grad_rows, "expert", split_axis=0, concat_axis=0, tiled=True
    ).reshape(groups, local_experts, capacity, model)
    hidden_grad = jnp.einsum(
        "sjcd,jfd->sjcf", grad_in_rows, expert_down, preferred_element_type=single
    )
    sigmoid_gate = jax.nn.sigmoid(gate_act)
    gate_lin = (
        hidden_grad * up_act * sigmoid_gate * (1.0 + gate_act * (1.0 - sigmoid_gate))
    ).astype(bfloat)
    up_lin = (hidden_grad * gate_act * sigmoid_gate).astype(bfloat)
    grad_down = jnp.einsum("sjcf,sjcd->jfd", hidden, grad_in_rows, preferred_element_type=single)
    grad_gate = jnp.einsum("sjcd,sjcf->jdf", incoming, gate_lin, preferred_element_type=single)
    grad_up = jnp.einsum("sjcd,sjcf->jdf", incoming, up_lin, preferred_element_type=single)
    rows_grad = (
        jnp.einsum("sjcf,jdf->sjcd", gate_lin, expert_gate, preferred_element_type=single)
        + jnp.einsum("sjcf,jdf->sjcd", up_lin, expert_up, preferred_element_type=single)
    ).astype(bfloat)
    came_back = lax.all_to_all(
        rows_grad.reshape(experts, capacity, model),
        "expert",
        split_axis=0,
        concat_axis=0,
        tiled=True,
    ).reshape(experts * capacity, model)
    mid_grad = jnp.sum(
        came_back[slot_of].reshape(tok_rows, top_count, model).astype(single), axis=1
    )
    prob_grad = jnp.sum(jnp.where(hits, gate_grad_route[:, :, None], 0.0), axis=1)
    logit_grad = router_probs * (
        prob_grad - jnp.sum(router_probs * prob_grad, axis=-1, keepdims=True)
    )
    logit_b = logit_grad.astype(bfloat)
    grad_router = jnp.einsum("td,te->de", mid_b, logit_b, preferred_element_type=single)
    mid_grad = mid_grad + jnp.einsum(
        "te,de->td", logit_b, router_full, preferred_element_type=single
    )
    resid_norm_grad, grad_gain_mid = norm_mid_back(mid_grad)
    resid_grad = grad_out + resid_norm_grad
    resid_b = resid_grad.astype(bfloat)
    grad_output_w = jnp.einsum("tc,td->cd", attended, resid_b, preferred_element_type=single)
    attended_grad = (
        jnp.einsum("td,cd->tc", resid_b, output_full, preferred_element_type=single)
        .astype(bfloat)
        .reshape(tok_rows, HEADS, HEAD)
    )
    probs_again = jnp.exp(masked_scores(key_all, piece_all) - log_mass)
    probs_b = probs_again.astype(bfloat)
    value_heads = value_all.reshape(length, HEADS, HEAD)
    value_grad_all = jnp.einsum(
        "hqk,qhd->khd", probs_b, attended_grad, preferred_element_type=single
    )
    weight_grad = jnp.einsum(
        "qhd,khd->hqk", attended_grad, value_heads, preferred_element_type=single
    )
    inner = jnp.sum(probs_again * weight_grad, axis=-1, keepdims=True)
    score_b = (probs_again * (weight_grad - inner)).astype(bfloat)
    query_grad_rot = (
        jnp.einsum(
            "hqk,khd->qhd",
            score_b,
            key_all.reshape(length, HEADS, HEAD),
            preferred_element_type=single,
        )
        * scale
    )
    key_grad_all = (
        jnp.einsum("hqk,qhd->khd", score_b, query_b, preferred_element_type=single) * scale
    )
    key_grad_mine, value_grad_mine = (
        lax.psum_scatter(
            key_grad_all.reshape(length, model).astype(jnp.bfloat16),
            "expert",
            scatter_dimension=0,
            tiled=True,
        ).astype(jnp.float32),
        lax.psum_scatter(
            value_grad_all.reshape(length, model).astype(jnp.bfloat16),
            "expert",
            scatter_dimension=0,
            tiled=True,
        ).astype(jnp.float32),
    )
    query_raw_grad, grad_gain_query = query_back(query_grad_rot)
    key_raw_grad, grad_gain_key = key_back(key_grad_mine.reshape(tok_rows, HEADS, HEAD))
    query_rb = query_raw_grad.astype(bfloat)
    key_rb = key_raw_grad.astype(bfloat)
    value_rb = value_grad_mine.astype(bfloat)
    grad_query_w = jnp.einsum("tc,td->cd", normed_b, query_rb, preferred_element_type=single)
    grad_key_w = jnp.einsum("tc,td->cd", normed_b, key_rb, preferred_element_type=single)
    grad_value_w = jnp.einsum("tc,td->cd", normed_b, value_rb, preferred_element_type=single)
    normed_grad = (
        jnp.einsum("td,cd->tc", query_rb, query_full, preferred_element_type=single)
        + jnp.einsum("td,cd->tc", key_rb, key_full, preferred_element_type=single)
        + jnp.einsum("td,cd->tc", value_rb, value_full, preferred_element_type=single)
    )
    token_norm_grad, grad_gain_in = norm_in_back(normed_grad)
    input_grad = resid_grad + token_norm_grad
    gate_part, up_part, down_part = (
        lax.psum_scatter(
            grad_gate.astype(jnp.bfloat16), "dp", scatter_dimension=1, tiled=True
        ).astype(jnp.float32),
        lax.psum_scatter(
            grad_up.astype(jnp.bfloat16), "dp", scatter_dimension=1, tiled=True
        ).astype(jnp.float32),
        lax.psum_scatter(
            grad_down.astype(jnp.bfloat16), "dp", scatter_dimension=2, tiled=True
        ).astype(jnp.float32),
    )
    sum_query, sum_key, sum_value, sum_output, sum_router, sum_in, sum_qnorm, sum_knorm, sum_mid = (
        lax.psum_scatter(grad_query_w, ("dp", "expert"), scatter_dimension=0, tiled=True),
        lax.psum_scatter(grad_key_w, ("dp", "expert"), scatter_dimension=0, tiled=True),
        lax.psum_scatter(grad_value_w, ("dp", "expert"), scatter_dimension=0, tiled=True),
        lax.psum_scatter(grad_output_w, ("dp", "expert"), scatter_dimension=0, tiled=True),
        lax.psum_scatter(grad_router, ("dp", "expert"), scatter_dimension=0, tiled=True),
        lax.psum_scatter(grad_gain_in, ("dp", "expert"), scatter_dimension=0, tiled=True),
        lax.psum_scatter(grad_gain_query, ("dp", "expert"), scatter_dimension=0, tiled=True),
        lax.psum_scatter(grad_gain_key, ("dp", "expert"), scatter_dimension=0, tiled=True),
        lax.psum_scatter(grad_gain_mid, ("dp", "expert"), scatter_dimension=0, tiled=True),
    )
    return (
        output,
        input_grad,
        sum_query,
        sum_key,
        sum_value,
        sum_output,
        sum_in,
        sum_qnorm,
        sum_knorm,
        sum_mid,
        sum_router,
        gate_part,
        up_part,
        down_part,
    )


def solution(mesh):
    in_specs = (
        P(("dp", "expert"), None),
        P(("dp", "expert"), None),
        P(("dp", "expert"), None),
        P(("dp", "expert"), None),
        P(("dp", "expert"), None),
        P(("dp", "expert")),
        P(("dp", "expert")),
        P(("dp", "expert")),
        P(("dp", "expert")),
        P(("dp", "expert"), None),
        P("expert", None, None),
        P("expert", None, None),
        P("expert", None, None),
        P(("dp", "expert"), None),
        P(("dp", "expert")),
        P(("dp", "expert"), None),
    )
    out_specs = (
        P(("dp", "expert"), None),
        P(("dp", "expert"), None),
        P(("dp", "expert"), None),
        P(("dp", "expert"), None),
        P(("dp", "expert"), None),
        P(("dp", "expert"), None),
        P(("dp", "expert")),
        P(("dp", "expert")),
        P(("dp", "expert")),
        P(("dp", "expert")),
        P(("dp", "expert"), None),
        P("expert", "dp", None),
        P("expert", "dp", None),
        P("expert", None, "dp"),
    )
    return jax.shard_map(
        per_device, mesh=mesh, in_specs=in_specs, out_specs=out_specs, check_vma=False
    )
```

profile of v0, /device:TPU:0, one launch (start us, length us, event | category | flops | bytes accessed | tf_op | source)
XLA Modules:
  0.0 2231.1 jit_solution(7539776026103335941)
XLA Ops:
  12.9 42.6 %all-reduce.15 = (bf16[2048]{0:T(1024)(128)(2,1)S(1)}, bf16[2048]{0:T(1024)(128)(2,1)S(1)}, bf16[2048]{0:T(1024)(128)(2,1)S(1)}, bf16[2048]{0:T(1024)(128)(2,1)S(1)}) all-reduce(bf16[2048]{0:T(1024)(128)(2,1)S(1)} %dynamic-update-slice, bf16[2048]{0:T(1024)(128)(2,1)S(1)} %dynamic-update-slice.2, ...), channel_id=1, replica_groups=mesh['dp'=4,'expert'=8] {'dp','expert'}, use_global_device_ids=true, to_apply=%add.6 | all-reduce | flops 8192 | bytes 32768
  57.6 33.7 %all-gather.13.cloned.1.call-done = bf16[2048,2048]{1,0:T(8,128)(2,1)} async-done(((bf16[64,2048]{1,0:T(8,128)(2,1)}), bf16[2048,2048]{1,0:T(8,128)(2,1)}) %all-gather.13.cloned.1.call-update) | async-done | bytes 8388624 | tf_op jit(solution)/shard_map/all_gather | solution.py:98
  97.7 72.6 %all-gather.15.cloned.1.call-done = bf16[2048,2048]{1,0:T(8,128)(2,1)} async-done(((bf16[64,2048]{1,0:T(8,128)(2,1)}), bf16[2048,2048]{1,0:T(8,128)(2,1)}) %all-gather.15.cloned.1.call-update) | async-done | bytes 8388624 | tf_op jit(solution)/shard_map/all_gather | solution.py:99
  180.0 69.3 %all-gather.9.cloned.1.call-done = bf16[2048,2048]{1,0:T(8,128)(2,1)} async-done(((bf16[64,2048]{1,0:T(8,128)(2,1)}), bf16[2048,2048]{1,0:T(8,128)(2,1)}) %all-gather.9.cloned.1.call-update) | async-done | bytes 8388624 | tf_op jit(solution)/shard_map/all_gather | solution.py:100
  274.4 13.2 all-gather.17.cloned.1.call-done
  297.3 29.4 %all-gather.11.cloned.1.call-done = bf16[1024,2048]{1,0:T(8,128)(2,1)} async-done(((bf16[128,2048]{1,0:T(8,128)(2,1)}), bf16[1024,2048]{1,0:T(8,128)(2,1)}) %all-gather.11.cloned.1.call-update) | async-done | bytes 4194320 | tf_op jit(solution)/shard_map/all_gather | solution.py:134
  333.9 73.0 %all-gather.19.cloned.1.call-done = bf16[2048,2048]{1,0:T(8,128)(2,1)} async-done(((bf16[64,2048]{1,0:T(8,128)(2,1)}), bf16[2048,2048]{1,0:T(8,128)(2,1)}) %all-gather.19.cloned.1.call-update) | async-done | bytes 8388624 | tf_op jit(solution)/shard_map/all_gather | solution.py:101
  430.4 85.5 %all-gather.1 = bf16[32,64,16]{1,2,0:T(8,128)(2,1)S(1)} all-gather(bf16[1,64,16]{1,2,0:T(8,128)(2,1)S(1)} %bitcast.236), channel_id=1, replica_groups=mesh['dp'=4,'expert'=8] {'dp','expert'}, dimensions={0}, use_global_device_ids=true | all-gather | bytes 67584 | tf_op jit(solution)/shard_map/all_gather | solution.py:102
  572.2 33.2 %all-to-all-done.2 = bf16[16,68,2048]{2,1,0:T(8,128)(2,1)} async-done(((bf16[16,68,2048]{2,1,0:T(8,128)(2,1)}), bf16[16,68,2048]{2,1,0:T(8,128)(2,1)}, u32[]{:S(2)}, u32[]{:S(2)}) %all-to-all-start.2) | async-done | bytes 4456480 | tf_op jit(solution)/shard_map/all_to_all | solution.py:214
  605.4 13.8 fusion.19
  659.6 31.3 %all-to-all-done.1 = bf16[16,68,2048]{2,1,0:T(8,128)(2,1)} async-done(((bf16[16,68,2048]{2,1,0:T(8,128)(2,1)}), bf16[16,68,2048]{2,1,0:T(8,128)(2,1)}, u32[]{:S(2)}, u32[]{:S(2)}) %all-to-all-start.1) | async-done | bytes 4456480 | tf_op jit(solution)/shard_map/all_to_all | solution.py:199
  719.5 30.8 %all-to-all-done.3 = bf16[16,68,2048]{2,1,0:T(8,128)(2,1)} async-done(((bf16[16,68,2048]{2,1,0:T(8,128)(2,1)}), bf16[16,68,2048]{2,1,0:T(8,128)(2,1)}, u32[]{:S(2)}, u32[]{:S(2)}) %all-to-all-start.3) | async-done | bytes 4456480 | tf_op jit(solution)/shard_map/all_to_all | solution.py:232
  757.4 11.8 gather_fusion.4
  820.9 11.8 bitcast_convert_fusion
  881.9 17.6 reduce-scatter.31.cloned.1.call-done
  931.1 105.5 %reduce-scatter.35.cloned.1.call-done = f32[64,16]{1,0:T(8,128)} async-done(((f32[2048,16]{1,0:T(8,128)}), f32[64,16]{1,0:T(8,128)}) %reduce-scatter.35.cloned.1.call-update) | async-done | bytes 4112
  1054.8 42.9 %all-reduce.14 = (f32[2048]{0:T(1024)S(1)}, f32[2048]{0:T(1024)S(1)}, f32[2048]{0:T(1024)S(1)}, f32[2048]{0:T(1024)S(1)}) all-reduce(f32[2048]{0:T(1024)S(1)} %get-tuple-element.22, f32[2048]{0:T(1024)S(1)} %get-tuple-element.20, f32[2048]{0:T(1024)S(1)} %get-tuple-element.18, ...), channel_id=8, replica_groups=mesh['dp'=4,'expert'=8] {'dp','expert'}, use_global_device_ids=true, to_apply=%region_30.31.clone | all-reduce | flops 8192 | bytes 65536
  1101.3 79.1 %reduce-scatter.29.cloned.1.call-done = bf16[2,1024,512]{2,1,0:T(8,128)(2,1)} async-done(((bf16[2,1024,2048]{2,1,0:T(8,128)(2,1)}), bf16[2,1024,512]{2,1,0:T(8,128)(2,1)}) %reduce-scatter.29.cloned.1.call-update) | async-done | bytes 2097168 | tf_op jit(solution)/shard_map/reduce_scatter | solution.py:319
  1184.6 143.5 %reduce-scatter.25.cloned.1.call-done = bf16[2,512,1024]{2,1,0:T(8,128)(2,1)} async-done(((bf16[2,2048,1024]{2,1,0:T(8,128)(2,1)}), bf16[2,512,1024]{2,1,0:T(8,128)(2,1)}) %reduce-scatter.25.cloned.1.call-update) | async-done | bytes 2097168 | tf_op jit(solution)/shard_map/reduce_scatter | solution.py:313
  1332.2 143.5 %reduce-scatter.27.cloned.1.call-done = bf16[2,512,1024]{2,1,0:T(8,128)(2,1)} async-done(((bf16[2,2048,1024]{2,1,0:T(8,128)(2,1)}), bf16[2,512,1024]{2,1,0:T(8,128)(2,1)}) %reduce-scatter.27.cloned.1.call-update) | async-done | bytes 2097168 | tf_op jit(solution)/shard_map/reduce_scatter | solution.py:316
  1479.8 182.6 %reduce-scatter.23.cloned.1.call-done = f32[64,2048]{1,0:T(8,128)} async-done(((f32[2048,2048]{1,0:T(8,128)}), f32[64,2048]{1,0:T(8,128)}) %reduce-scatter.23.cloned.1.call-update) | async-done | bytes 524304 | tf_op jit(solution)/shard_map/reduce_scatter | solution.py:327
  1662.3 187.1 %reduce-scatter.21.cloned.1.call-done = f32[64,2048]{1,0:T(8,128)} async-done(((f32[2048,2048]{1,0:T(8,128)}), f32[64,2048]{1,0:T(8,128)}) %reduce-scatter.21.cloned.1.call-update) | async-done | bytes 524304 | tf_op jit(solution)/shard_map/reduce_scatter | solution.py:326
  1849.5 187.3 %reduce-scatter.19.cloned.1.call-done = f32[64,2048]{1,0:T(8,128)} async-done(((f32[2048,2048]{1,0:T(8,128)}), f32[64,2048]{1,0:T(8,128)}) %reduce-scatter.19.cloned.1.call-update) | async-done | bytes 524304 | tf_op jit(solution)/shard_map/reduce_scatter | solution.py:325
  2036.8 187.4 %reduce-scatter.17.cloned.1.call-done = f32[64,2048]{1,0:T(8,128)} async-done(((f32[2048,2048]{1,0:T(8,128)}), f32[64,2048]{1,0:T(8,128)}) %reduce-scatter.17.cloned.1.call-update) | async-done | bytes 524304 | tf_op jit(solution)/shard_map/reduce_scatter | solution.py:324
  (299 shorter events, 387.1 us)
Async XLA Ops:
  7.2 84.2 %all-gather.13.cloned.1.call-start = ((), (), s32[]{:S(2)}) async-start(), calls=%async_computation.16 | async-start | bytes 8650752 | tf_op jit(solution)/shard_map/all_gather | solution.py:98
  7.9 162.4 %all-gather.15.cloned.1.call-start = ((), (), s32[]{:S(2)}) async-start(), calls=%async_computation.17 | async-start | bytes 8650752 | tf_op jit(solution)/shard_map/all_gather | solution.py:99
  8.7 240.6 %all-gather.9.cloned.1.call-start = ((), (), s32[]{:S(2)}) async-start(), calls=%async_computation.14 | async-start | bytes 8650752 | tf_op jit(solution)/shard_map/all_gather | solution.py:100
  9.4 278.2 %all-gather.17.cloned.1.call-start = ((), (), s32[]{:S(2)}) async-start(), calls=%async_computation.18 | async-start | bytes 4718592 | tf_op jit(solution)/shard_map/all_gather | solution.py:133
  55.5 193.7 %copy-start.22 = (f32[2048]{0:T(1024)}, f32[2048]{0:T(1024)S(1)}, u32[]{:S(2)}) copy-start(f32[2048]{0:T(1024)S(1)} %convert_element_type.165) | copy-start | bytes 24580
  55.5 119.6 %copy-start.31 = (f32[2048]{0:T(1024)}, f32[2048]{0:T(1024)S(1)}, u32[]{:S(2)}) copy-start(f32[2048]{0:T(1024)S(1)} %convert_element_type.171) | copy-start | bytes 24580
  57.3 191.9 %copy-start.35 = (f32[128]{0:T(128)}, f32[128]{0:T(128)S(1)}, u32[]{:S(2)}) copy-start(f32[128]{0:T(128)S(1)} %fusion.78) | copy-start | bytes 1540
  179.9 146.8 %all-gather.11.cloned.1.call-start = ((), (), s32[]{:S(2)}) async-start(), calls=%async_computation.15 | async-start | bytes 4718592 | tf_op jit(solution)/shard_map/all_gather | solution.py:134
  254.7 152.1 %all-gather.19.cloned.1.call-start = ((), (), s32[]{:S(2)}) async-start(), calls=%async_computation.19 | async-start | bytes 8650752 | tf_op jit(solution)/shard_map/all_gather | solution.py:101
  255.6 156.1 %copy-start.33 = (f32[2048]{0:T(1024)}, f32[2048]{0:T(1024)S(1)}, u32[]{:S(2)}) copy-start(f32[2048]{0:T(1024)S(1)} %convert_element_type.177) | copy-start | bytes 24580
  425.7 119.9 %all-to-all-start = ((bf16[16,68,2048]{2,1,0:T(8,128)(2,1)}), bf16[16,68,2048]{2,1,0:T(8,128)(2,1)}, u32[]{:S(2)}, u32[]{:S(2)}) async-start(bf16[16,68,2048]{2,1,0:T(8,128)(2,1)} %reshape.387), calls=%async_computation | async-start | bytes 9437184 | tf_op jit(solution)/shard_map/all_to_all | solution.py:192
  545.6 59.8 %all-to-all-start.2 = ((bf16[16,68,2048]{2,1,0:T(8,128)(2,1)}), bf16[16,68,2048]{2,1,0:T(8,128)(2,1)}, u32[]{:S(2)}, u32[]{:S(2)}) async-start(bf16[16,68,2048]{2,1,0:T(8,128)(2,1)} %multiply_convert_fusion), calls=%async_computation.2 | async-start | bytes 9437184 | tf_op jit(solution)/shard_map/all_to_all | solution.py:214
  631.3 59.5 %all-to-all-start.1 = ((bf16[16,68,2048]{2,1,0:T(8,128)(2,1)}), bf16[16,68,2048]{2,1,0:T(8,128)(2,1)}, u32[]{:S(2)}, u32[]{:S(2)}) async-start(bf16[16,68,2048]{2,1,0:T(8,128)(2,1)} %bitcast.217), calls=%async_computation.1 | async-start | bytes 9437184 | tf_op jit(solution)/shard_map/all_to_all | solution.py:199
  690.8 59.5 %all-to-all-start.3 = ((bf16[16,68,2048]{2,1,0:T(8,128)(2,1)}), bf16[16,68,2048]{2,1,0:T(8,128)(2,1)}, u32[]{:S(2)}, u32[]{:S(2)}) async-start(bf16[16,68,2048]{2,1,0:T(8,128)(2,1)} %bitcast.216), calls=%async_computation.3 | async-start | bytes 9437184 | tf_op jit(solution)/shard_map/all_to_all | solution.py:232
  695.6 170.2 %reduce-scatter.33.cloned.1.call-start = ((), (), s32[]{:S(2)}) async-start(), calls=%async_computation.28 | async-start | bytes 4718592
  796.1 103.5 %reduce-scatter.31.cloned.1.call-start = ((), (), s32[]{:S(2)}) async-start(), calls=%async_computation.27 | async-start | bytes 4718592
  819.5 217.2 %reduce-scatter.35.cloned.1.call-start = ((), (), s32[]{:S(2)}) async-start(), calls=%async_computation.29 | async-start | bytes 1081344
  820.9 359.5 %reduce-scatter.29.cloned.1.call-start = ((), (), s32[]{:S(2)}) async-start(), calls=%async_computation.26 | async-start | bytes 10485760 | tf_op jit(solution)/shard_map/reduce_scatter | solution.py:319
  832.7 495.4 %reduce-scatter.25.cloned.1.call-start = ((), (), s32[]{:S(2)}) async-start(), calls=%async_computation.24 | async-start | bytes 10485760 | tf_op jit(solution)/shard_map/reduce_scatter | solution.py:313
  844.5 631.2 %reduce-scatter.27.cloned.1.call-start = ((), (), s32[]{:S(2)}) async-start(), calls=%async_computation.25 | async-start | bytes 10485760 | tf_op jit(solution)/shard_map/reduce_scatter | solution.py:316
  856.3 806.0 %reduce-scatter.23.cloned.1.call-start = ((), (), s32[]{:S(2)}) async-start(), calls=%async_computation.23 | async-start | bytes 17301504 | tf_op jit(solution)/shard_map/reduce_scatter | solution.py:327
  865.8 983.7 %reduce-scatter.21.cloned.1.call-start = ((), (), s32[]{:S(2)}) async-start(), calls=%async_computation.22 | async-start | bytes 17301504 | tf_op jit(solution)/shard_map/reduce_scatter | solution.py:326
  876.1 1160.7 %reduce-scatter.19.cloned.1.call-start = ((), (), s32[]{:S(2)}) async-start(), calls=%async_computation.21 | async-start | bytes 17301504 | tf_op jit(solution)/shard_map/reduce_scatter | solution.py:325
  917.7 1306.5 %reduce-scatter.17.cloned.1.call-start = ((), (), s32[]{:S(2)}) async-start(), calls=%async_computation.20 | async-start | bytes 17301504 | tf_op jit(solution)/shard_map/reduce_scatter | solution.py:324
  (55 other events, 1450.0 us)
Sparse Core Ops, SparseCore 0:
  10.9 80.4 all-gather.12
  94.2 76.0 all-gather.14
  173.1 76.0 all-gather.8
  251.5 36.0 all-gather.16
  289.9 36.7 all-gather.10
  329.4 77.4 all-gather.18
  796.2 47.6 reduce-scatter.32
  848.3 51.2 reduce-scatter.30
  901.8 134.7 reduce-scatter.34
  1039.0 141.3 reduce-scatter.28
  1182.9 145.2 reduce-scatter.24
  1330.5 145.1 reduce-scatter.26
  1478.7 183.6 reduce-scatter.22
  1665.2 184.2 reduce-scatter.20
  1852.3 184.4 reduce-scatter.18
  2039.6 184.5 reduce-scatter.16
where the time goes:
time: 2240 us; the launch traced here: 2230 us
  waiting for transfers between devices  1620 us (72%)
  matrix products  216 us (10%)
  blocking collectives  180 us (8%)
  local copies, waits for them, and re-layouts  121 us (5%)
  other arithmetic  56 us (2%)
    reduce_scatter x1, waiting for transfers between devices, per_device(): lax.psum_scatter(grad_query_w, ('dp', 'expert'), scatter_dimension=0, til...  187 us
    reduce_scatter x1, waiting for transfers between devices, per_device(): lax.psum_scatter(grad_key_w, ('dp', 'expert'), scatter_dimension=0, tiled...  187 us
    reduce_scatter x1, waiting for transfers between devices, per_device(): lax.psum_scatter(grad_value_w, ('dp', 'expert'), scatter_dimension=0, til...  187 us
    reduce_scatter x1, waiting for transfers between devices, per_device(): lax.psum_scatter(grad_output_w, ('dp', 'expert'), scatter_dimension=0, ti...  183 us
    reduce_scatter x1, waiting for transfers between devices, per_device(): lax.psum_scatter(grad_gate.astype(jnp.bfloat16), 'dp', scatter_dimension=...  144 us
    reduce_scatter x1, waiting for transfers between devices, per_device(): lax.psum_scatter(grad_up.astype(jnp.bfloat16), 'dp', scatter_dimension=1,...  143 us
    unnamed x19, waiting for transfers between devices  126 us
    all_gather x1, blocking collectives, per_device(): lax.all_gather(router, ('dp', 'expert'), axis=0, tiled=True)  85.5 us
  transfers between devices with their start and end apart: 20, of which 18 were waited for; matrix products, arithmetic and copies ran while one was open for 13% of the time, Pallas kernels for 0%

commit v1 on v0

v1 whole, which is shorter than its diff:
```python
import math

import jax
import jax.numpy as jnp
from jax import lax
from jax.sharding import PartitionSpec as P

HEAD = 128
eps_norm = 1e-05
rope_base = 10000.0
single = jnp.float32
bfloat = jnp.bfloat16


def dot32(left, right, dims):
    return lax.dot_general(left, right, (dims, ((), ())), preferred_element_type=single)


def swap(values, axis, mask):
    count = lax.axis_size(axis)
    return lax.ppermute(values, axis, [(i, i ^ mask) for i in range(count)])


def gather_each(values, axis):
    count = lax.axis_size(axis)
    return [values] + [swap(values, axis, mask) for mask in range(1, count)]


def gather_pairs(values):
    count = lax.axis_size("expert")
    blocks = [None] * count
    for mask in range(0, count, 2):
        blocks[mask] = values if mask == 0 else swap(values, "expert", mask)
        blocks[mask + 1] = swap(blocks[mask], "expert", 1)
    return blocks


def gather_steps(values, axis, count):
    held = values[None]
    order = [0]
    mask = count - 1
    while mask > 0:
        other = swap(held, axis, mask)
        held = jnp.concatenate([held, other], axis=0)
        order = order + [place ^ mask for place in order]
        mask >>= 1
    return held, order


def scatter_sum_pairs(parts):
    count = len(parts)
    odd = jnp.stack([parts[mask + 1] for mask in range(0, count, 2)])
    arrived = swap(odd, "expert", 1)
    sums = [
        (parts[mask].astype(single) + arrived[mask // 2].astype(single)).astype(bfloat)
        for mask in range(0, count, 2)
    ]
    total = sums[0].astype(single)
    for place in range(1, count // 2):
        total = total + swap(sums[place], "expert", 2 * place).astype(single)
    return total


def sum_rows_over_expert(values):
    count = lax.axis_size("expert")

    def reorder(array, mask):
        return jnp.concatenate(
            [array[..., j ^ mask : (j ^ mask) + 1, :] for j in range(count)], axis=-2
        )

    total = values + reorder(swap(values, "expert", 1), 1)
    out = total
    for mask in range(2, count, 2):
        out = out + reorder(swap(total, "expert", mask), mask)
    return out


def permute_blocks(array, mask, count):
    rows = array.shape[0] // count
    if mask == 0:
        return array
    return jnp.concatenate(
        [array[(j ^ mask) * rows : ((j ^ mask) + 1) * rows] for j in range(count)], axis=0
    )


def per_device(
    tokens,
    attn_query,
    attn_key,
    attn_value,
    attn_output,
    norm_in,
    norm_query,
    norm_key,
    norm_mid,
    router,
    expert_gate,
    expert_up,
    expert_down,
    routes,
    pieces,
    cotangent,
):
    n = lax.axis_size("expert")
    m = lax.axis_size("dp")
    rows, model = tokens.shape
    shard = attn_query.shape[0]
    experts = router.shape[1]
    local = expert_gate.shape[0]
    hidden_units = expert_gate.shape[2]
    length = rows * n
    near = min(m, 4)
    width = model // n
    heads = width // HEAD
    mine = lax.axis_index("expert")
    plane = lax.axis_index("dp")
    scale = HEAD ** (-0.5)
    slots = jnp.arange(n, dtype=jnp.int32) ^ mine

    small = jnp.concatenate(
        [norm_in[None], norm_query[None], norm_key[None], norm_mid[None], router.T], axis=0
    )
    kinds = small.shape[0]
    small = jnp.stack(gather_each(small, "dp"))
    small = jnp.stack(gather_each(small, "expert"))
    small = jnp.take(small, slots, axis=0)
    small = jnp.take(small, jnp.arange(m, dtype=jnp.int32) ^ plane, axis=1)
    small = small.transpose(2, 1, 0, 3).reshape(kinds, model)
    gain_in, gain_query, gain_key, gain_mid = [small[i].astype(single) for i in range(4)]
    router_t = small[4:]

    info = jnp.concatenate([routes.T, pieces[None]], axis=0)
    info = jnp.stack(gather_each(info, "expert"), axis=1)
    info = jnp.stack(gather_each(info, "dp"))
    piece_row = info[0, -1].reshape(length)

    x_b = jnp.concatenate(gather_pairs(tokens), axis=0)
    packed = jnp.stack([attn_query, attn_key, attn_value]).reshape(3, shard, n, width)
    packed = packed.transpose(2, 0, 1, 3)
    packed = lax.all_to_all(packed, "expert", split_axis=0, concat_axis=0, tiled=True)
    packed = packed.transpose(1, 0, 2, 3).reshape(3, n * shard, width)
    w_qk = lax.all_gather(packed[:2], "dp", axis=1, tiled=True)
    w_v = lax.all_gather(packed[2], "dp", axis=0, tiled=True)
    w_q, w_k = w_qk[0], w_qk[1]
    wo_full = lax.all_gather(attn_output, ("dp", "expert"), axis=0, tiled=True)
    wo = jnp.take(wo_full.reshape(n, width, model), slots, axis=0).reshape(model, model)
    wo_own = lax.dynamic_slice_in_dim(wo_full, mine * width, width, 0)

    x = x_b.astype(single)
    rs_in = lax.rsqrt(jnp.mean(x * x, axis=-1, keepdims=True) + eps_norm)
    normed_b = (x * rs_in * gain_in).astype(bfloat)
    query_raw = dot32(normed_b, w_q, ((1,), (0,)))
    key_raw = dot32(normed_b, w_k, ((1,), (0,)))
    squares = jnp.stack([jnp.sum(query_raw**2, axis=-1), jnp.sum(key_raw**2, axis=-1)])
    squares = sum_rows_over_expert(squares.reshape(2, n, rows)).reshape(2, length)
    rs_q = lax.rsqrt(squares[0] / model + eps_norm)[:, None]
    rs_k = lax.rsqrt(squares[1] / model + eps_norm)[:, None]
    value_b = dot32(normed_b, w_v, ((1,), (0,))).astype(bfloat)

    place = (slots[:, None] * rows + jnp.arange(rows, dtype=jnp.int32)[None, :]).reshape(length)
    half = HEAD // 2
    inverse = jnp.exp(jnp.arange(half, dtype=single) * (-2.0 * math.log(rope_base) / HEAD))
    angles = place.astype(single)[:, None] * inverse[None, :]
    cosine = jnp.cos(angles)
    sine = jnp.sin(angles)

    def rotate(values, back):
        out = []
        sn = -sine if back else sine
        for h in range(heads):
            u = values[:, h * HEAD : h * HEAD + half]
            w = values[:, h * HEAD + half : (h + 1) * HEAD]
            out += [u * cosine - w * sn, w * cosine + u * sn]
        return jnp.concatenate(out, axis=-1)

    own_gain_q = lax.dynamic_slice_in_dim(gain_query, mine * width, width)
    own_gain_k = lax.dynamic_slice_in_dim(gain_key, mine * width, width)
    query_b = rotate(query_raw * rs_q * own_gain_q, False).astype(bfloat)
    key_b = rotate(key_raw * rs_k * own_gain_k, False).astype(bfloat)

    def per_head(array):
        return [array[:, h * HEAD : (h + 1) * HEAD] for h in range(heads)]

    allowed = (place[None, :] <= place[:, None]) | (
        (piece_row[:, None] == piece_row[None, :]) & (piece_row[:, None] > 0)
    )
    probs = []
    mixed = []
    for q_h, k_h, v_h in zip(per_head(query_b), per_head(key_b), per_head(value_b)):
        scores = jnp.where(allowed, dot32(q_h, k_h, ((1,), (1,))) * scale, -1e30)
        exponent = jnp.exp(scores - jnp.max(scores, axis=-1, keepdims=True))
        prob = exponent / jnp.sum(exponent, axis=-1, keepdims=True)
        probs.append(prob)
        mixed.append(dot32(prob.astype(bfloat), v_h, ((1,), (0,))))
    attended = jnp.concatenate(mixed, axis=-1).astype(bfloat)
    att = gather_pairs(attended)
    att = jnp.concatenate([permute_blocks(att[k], k, n) for k in range(n)], axis=1)

    residual = x + dot32(att, wo, ((1,), (0,)))
    rs_mid = lax.rsqrt(jnp.mean(residual * residual, axis=-1, keepdims=True) + eps_norm)
    mid = (residual * rs_mid * gain_mid).astype(bfloat)

    def other_planes(own_block):
        held, order = gather_steps(own_block, "dp", near)
        blocks = gather_pairs(held[1:])
        return jnp.stack(blocks, axis=1)

    cot_plane = jnp.concatenate(gather_pairs(cotangent), axis=0)
    cot_others = other_planes(cotangent)
    mid_others = other_planes(mid[:rows])
    order = gather_steps(jnp.zeros((), jnp.int32), "dp", near)[1]

    def router_probs_of(mid_rows):
        logits = dot32(mid_rows, router_t, ((1,), (1,)))
        exponent = jnp.exp(logits - jnp.max(logits, axis=-1, keepdims=True))
        return exponent / jnp.sum(exponent, axis=-1, keepdims=True)

    block = 2 * rows
    cap = 2 * min(rows, rows * routes.shape[1] // experts + rows // 32)
    upper = (
        jnp.arange(block, dtype=jnp.int32)[:, None] <= jnp.arange(block, dtype=jnp.int32)[None, :]
    ).astype(bfloat)

    def picks(route_rows):
        ids = mine * local + jnp.arange(local, dtype=jnp.int32)
        hit = jnp.any(route_rows[:, None] == ids[None, :, None, None], axis=2)
        rank = lax.dot_general(
            hit.astype(bfloat), upper, (((2,), (0,)), ((), ())), preferred_element_type=single
        )
        wanted = jnp.arange(1, cap + 1, dtype=jnp.int32).astype(single)
        return hit[:, :, None, :] & (rank[:, :, None, :] == wanted[None, None, :, None])

    def expert_rows(mid_rows, cot_rows, route_rows):
        groups = route_rows.shape[0]
        router_probs = router_probs_of(mid_rows)
        local_probs = lax.dynamic_slice_in_dim(router_probs, mine * local, local, 1)
        local_probs = local_probs.reshape(groups, block, local).transpose(0, 2, 1)
        pick = picks(route_rows)
        pick_b = pick.astype(bfloat)
        gate_row = jnp.sum(jnp.where(pick, local_probs[:, :, None, :], 0.0), axis=-1)
        entered = jnp.einsum("gjct,gtd->jgcd", pick_b, mid_rows.reshape(groups, block, model))
        cot_row = jnp.einsum("gjct,gtd->jgcd", pick_b, cot_rows.reshape(groups, block, model))
        dreturned = (gate_row.transpose(1, 0, 2)[..., None] * cot_row.astype(single)).astype(bfloat)
        gate_act = jnp.einsum("jgcd,jdf->jgcf", entered, expert_gate, preferred_element_type=single)
        up_act = jnp.einsum("jgcd,jdf->jgcf", entered, expert_up, preferred_element_type=single)
        sig = jax.nn.sigmoid(gate_act)
        silu = gate_act * sig
        hidden = (silu * up_act).astype(bfloat)
        dhidden = jnp.einsum(
            "jgcd,jfd->jgcf", dreturned, expert_down, preferred_element_type=single
        )
        gate_lin = (dhidden * up_act * sig * (1.0 + gate_act * (1.0 - sig))).astype(bfloat)
        up_lin = (dhidden * silu).astype(bfloat)
        return router_probs, local_probs, pick, pick_b, entered, cot_row, dreturned, hidden, gate_lin, up_lin

    def groups_of(info_planes):
        planes = info_planes.shape[0]
        r = info_planes[:, :-1].reshape(planes, -1, n // 2, block)
        return r.transpose(0, 2, 1, 3).reshape(planes * n // 2, -1, block)

    own_groups = groups_of(info[:1])
    (router_probs, local_probs, pick, pick_b, entered, cot_row, dreturned, hidden, gate_lin, up_lin) = (
        expert_rows(mid, cot_plane, own_groups)
    )
    returned = jnp.einsum(
        "jgcf,jfd->jgcd", hidden, expert_down, preferred_element_type=single
    ).astype(bfloat)
    dgate_row = jnp.sum(cot_row.astype(single) * returned.astype(single), axis=-1)
    dmid_rows = (
        jnp.einsum("jgcf,jdf->jgcd", gate_lin, expert_gate, preferred_element_type=single)
        + jnp.einsum("jgcf,jdf->jgcd", up_lin, expert_up, preferred_element_type=single)
    ).astype(bfloat)
    dmid = jnp.einsum(
        "gjct,jgcd->gtd", pick_b, dmid_rows, preferred_element_type=single
    ).reshape(length, model)
    dprobs = jnp.sum(
        jnp.where(pick, dgate_row.transpose(1, 0, 2)[..., None], 0.0), axis=2
    )
    dprobs = dprobs.transpose(0, 2, 1).reshape(length, local)
    dprobs = lax.dynamic_update_slice(
        jnp.zeros((length, experts), single), dprobs, (jnp.zeros((), jnp.int32), mine * local)
    )
    dlogits = router_probs * (dprobs - jnp.sum(router_probs * dprobs, axis=-1, keepdims=True))
    dlogits_b = dlogits.astype(bfloat)
    router_grad = dot32(dlogits_b, mid, ((0,), (0,)))
    dmid = dmid + dot32(dlogits_b, router_t, ((1,), (0,)))
    mid_grad = jnp.sum(dmid * (residual * rs_mid), axis=0)
    scaled = dmid * gain_mid
    inner = jnp.mean(scaled * residual, axis=-1, keepdims=True)
    dres_part = (rs_mid * (scaled - residual * (rs_mid * rs_mid * inner))).astype(bfloat)

    datt_all = dot32(dres_part, wo, ((1,), (1,))).astype(bfloat)
    datt = scatter_sum_pairs(
        [permute_blocks(datt_all[:, k * width : (k + 1) * width], k, n) for k in range(n)]
    )
    datt = datt + dot32(cot_plane, wo_own, ((1,), (1,)))
    datt_b = datt.astype(bfloat)
    dq_rot, dk_rot, dv = [], [], []
    for prob, da, q_h, k_h, v_h in zip(
        probs, per_head(datt_b), per_head(query_b), per_head(key_b), per_head(value_b)
    ):
        dprob = dot32(da, v_h, ((1,), (1,)))
        dsum = jnp.sum(prob * dprob, axis=-1, keepdims=True)
        dscores = (prob * (dprob - dsum)).astype(bfloat)
        dv.append(dot32(prob.astype(bfloat), da, ((0,), (0,))))
        dq_rot.append(dot32(dscores, k_h, ((1,), (0,))) * scale)
        dk_rot.append(dot32(dscores, q_h, ((0,), (0,))) * scale)
    dq_un = rotate(jnp.concatenate(dq_rot, axis=-1), True)
    dk_un = rotate(jnp.concatenate(dk_rot, axis=-1), True)
    inners = jnp.stack(
        [
            jnp.sum(dq_un * own_gain_q * query_raw, axis=-1),
            jnp.sum(dk_un * own_gain_k * key_raw, axis=-1),
        ]
    )
    inners = sum_rows_over_expert(inners.reshape(2, n, rows)).reshape(2, length)
    query_gain_grad = jnp.sum(dq_un * query_raw * rs_q, axis=0)
    key_gain_grad = jnp.sum(dk_un * key_raw * rs_k, axis=0)
    dq_b = (
        rs_q * dq_un * own_gain_q - query_raw * (rs_q**3 / model * inners[0][:, None])
    ).astype(bfloat)
    dk_b = (
        rs_k * dk_un * own_gain_k - key_raw * (rs_k**3 / model * inners[1][:, None])
    ).astype(bfloat)
    dv_b = jnp.concatenate(dv, axis=-1).astype(bfloat)
    dnormed_part = (
        dot32(dq_b, w_q, ((1,), (1,)))
        + dot32(dk_b, w_k, ((1,), (1,)))
        + dot32(dv_b, w_v, ((1,), (1,)))
    ).astype(bfloat)

    def own_rows(array, k):
        return array[k * rows : (k + 1) * rows]

    dnormed = scatter_sum_pairs([own_rows(dnormed_part, k) for k in range(n)])

    def weight_sum(partial):
        summed = lax.psum_scatter(
            partial.astype(bfloat), "dp", scatter_dimension=0, tiled=True
        )
        moved = lax.all_to_all(
            summed.reshape(n, shard, width), "expert", split_axis=0, concat_axis=0, tiled=True
        )
        return moved.transpose(1, 0, 2).reshape(shard, model).astype(single)

    value_grad = weight_sum(dot32(normed_b, dv_b, ((0,), (0,))))
    query_grad = weight_sum(dot32(normed_b, dq_b, ((0,), (0,))))
    key_grad = weight_sum(dot32(normed_b, dk_b, ((0,), (0,))))

    moe_part = jnp.einsum(
        "gjct,jgcd->gtd",
        jnp.where(pick, local_probs[:, :, None, :], 0.0).astype(bfloat),
        returned,
        preferred_element_type=single,
    ).astype(bfloat).reshape(length, model)
    moe = scatter_sum_pairs([own_rows(moe_part, k) for k in range(n)])
    output = (residual[:rows] + moe).astype(bfloat)
    dres = scatter_sum_pairs([own_rows(dres_part, k) for k in range(n)])
    dres = dres + cotangent.astype(single)
    dres_b = dres.astype(bfloat)
    cols = dres_b.reshape(rows, n, width).transpose(1, 0, 2)
    cols = jnp.take(cols, slots, axis=0)
    cols = jnp.concatenate(
        [cols[0]] + [swap(cols[k], "expert", k) for k in range(1, n)], axis=0
    )
    output_part = dot32(att, cols, ((0,), (0,)))
    output_part = jnp.take(output_part.reshape(n, width, width), slots, axis=0)
    output_grad = weight_sum(output_part.reshape(model, width))

    other_info = jnp.stack([info[k] for k in order[1:]])
    other = expert_rows(
        mid_others.reshape(-1, model), cot_others.reshape(-1, model), groups_of(other_info)
    )

    def rows_of(own_part, other_part):
        return jnp.concatenate(
            [
                own_part.reshape(local, -1, own_part.shape[-1]),
                other_part.reshape(local, -1, other_part.shape[-1]),
            ],
            axis=1,
        )

    span = model // m
    far = m // near

    def cut(array):
        parts = array.reshape(array.shape[:2] + (far, near, span))
        parts = lax.dynamic_index_in_dim(parts, plane % near, 3, keepdims=False)
        return parts.reshape(array.shape[:2] + (far * span,))

    def sum_over_far(parts):
        if far == 1:
            return parts[0]
        parts = jnp.take(parts, jnp.arange(far, dtype=jnp.int32) ^ (plane // near), axis=0)
        total = parts[0]
        for k in range(1, far):
            total = total + swap(parts[k].astype(bfloat), "dp", k * near).astype(single)
        return total

    hidden_all = rows_of(hidden, other[7])
    gate_all = rows_of(gate_lin, other[8])
    up_all = rows_of(up_lin, other[9])
    entered_cut = cut(rows_of(entered, other[4]))
    dret_cut = cut(rows_of(dreturned, other[6]))
    gate_grad = jnp.einsum("jrd,jrf->jdf", entered_cut, gate_all, preferred_element_type=single)
    up_grad = jnp.einsum("jrd,jrf->jdf", entered_cut, up_all, preferred_element_type=single)
    down_grad = jnp.einsum("jrf,jrd->jfd", hidden_all, dret_cut, preferred_element_type=single)
    gate_grad, up_grad = [
        sum_over_far(
            grad.reshape(local, far, span, hidden_units).transpose(1, 0, 2, 3)
        )
        for grad in (gate_grad, up_grad)
    ]
    down_grad = sum_over_far(
        down_grad.reshape(local, hidden_units, far, span).transpose(2, 0, 1, 3)
    )

    x_own = tokens.astype(single)
    rs_own = rs_in[:rows]
    scaled_in = dnormed * gain_in
    inner_in = jnp.mean(scaled_in * x_own, axis=-1, keepdims=True)
    input_grad = dres + rs_own * (scaled_in - x_own * (rs_own * rs_own * inner_in))
    in_grad = jnp.sum(dnormed * x_own * rs_own, axis=0)

    def placed(part):
        return lax.dynamic_update_slice(jnp.zeros((model,), single), part, (mine * width,))

    small_grad = jnp.concatenate(
        [
            in_grad[None],
            placed(query_gain_grad)[None],
            placed(key_gain_grad)[None],
            mid_grad[None],
            router_grad,
        ],
        axis=0,
    ).reshape(kinds, m, n, shard)
    small_grad = jnp.take(small_grad, slots, axis=2)
    small_sum = small_grad[:, :, 0]
    for k in range(1, n):
        small_sum = small_sum + swap(small_grad[:, :, k], "expert", k)
    small_sum = jnp.take(small_sum, jnp.arange(m, dtype=jnp.int32) ^ plane, axis=1)
    total = small_sum[:, 0]
    for k in range(1, m):
        total = total + swap(small_sum[:, k], "dp", k)

    return (
        output,
        input_grad,
        query_grad,
        key_grad,
        value_grad,
        output_grad,
        total[0],
        total[1],
        total[2],
        total[3],
        total[4:].T,
        gate_grad,
        up_grad,
        down_grad,
    )


def solution(mesh):
    both = ("dp", "expert")
    in_specs = (
        [P(both, None)] * 5
        + [P(both)] * 4
        + [P(both, None)]
        + [P("expert", None, None)] * 3
        + [P(both, None), P(both), P(both, None)]
    )
    out_specs = (
        [P(both, None)] * 6
        + [P(both)] * 4
        + [P(both, None)]
        + [P("expert", "dp", None)] * 2
        + [P("expert", None, "dp")]
    )
    return jax.shard_map(
        per_device,
        mesh=mesh,
        in_specs=tuple(in_specs),
        out_specs=tuple(out_specs),
        check_vma=False,
    )
```

time: 2240 us -> 1180 us (0.53)
  waiting for transfers between devices: 1620 us -> 303 us
  blocking collectives: 180 us -> 17.7 us
  local copies, waits for them, and re-layouts: 121 us -> 275 us
  other arithmetic: 56 us -> 151 us
  starting transfers between devices: 20.1 us -> 113 us
  matrix products: 216 us -> 295 us
    reduce_scatter x7 -> x4, waiting for transfers between devices: 1110 us -> 0.03 us  [weight_sum(): lax.psum_scatter(partial.astype(bfloat), 'dp', scatter_dimension=0, tiled...]
    ppermute x0 -> x100, waiting for transfers between devices: none -> 295 us  [swap(): return lax.ppermute(values, axis, [(i, i ^ mask) for i in range(count)])]
    all_gather x6 -> x3, waiting for transfers between devices: 291 us -> 0.01 us  [the longest x1 0.01 us: per_device(): w_qk = lax.all_gather(packed[:2], 'dp', axis=1, tiled=True)]
    unnamed x19 -> x7, waiting for transfers between devices: 126 us -> 0.11 us
    ppermute x0 -> x100, starting transfers between devices: none -> 98.1 us  [swap(): return lax.ppermute(values, axis, [(i, i ^ mask) for i in range(count)])]
    all_gather x2 -> x0, blocking collectives: 94.2 us -> none  [the longest x1 85.5 us: per_device(): lax.all_gather(router, ('dp', 'expert'), axis=0, tiled=True)]
    all_to_all x4, waiting for transfers between devices: 95.2 us -> 7.42 us  [weight_sum(): lax.all_to_all(summed.reshape(n, shard, width), 'expert', split_axis=0, c...]
    unnamed x2 -> x0, blocking collectives: 85.5 us -> none
  transfers between devices with their start and end apart: 20 -> 111, of which waited for: 18 -> 34; matrix products, arithmetic and copies ran while one was open for 13% -> 47% of each run, Pallas kernels for 0% -> 0%
where the time goes in v1:
time: 1180 us; the launch traced here: 1170 us
  waiting for transfers between devices  303 us (26%)
  matrix products  295 us (25%)
  local copies, waits for them, and re-layouts  275 us (23%)
  other arithmetic  151 us (13%)
  starting transfers between devices  113 us (10%)
  blocking collectives  17.7 us (2%)
  between operations  16.9 us (1%)
    ppermute x100, waiting for transfers between devices, swap(): return lax.ppermute(values, axis, [(i, i ^ mask) for i in range(count)])  295 us
    ppermute x100, starting transfers between devices, swap(): return lax.ppermute(values, axis, [(i, i ^ mask) for i in range(count)])  98.1 us
    dot_general x29, matrix products, dot32(): lax.dot_general(left, right, (dims, ((), ())), preferred_element_type=sin...  96.6 us
    unnamed x354, local copies, waits for them, and re-layouts  91.8 us
    concatenate x2, other arithmetic, rows_of(): jnp.concatenate([own_part.reshape(local, -1, own_part.shape[-1]), other_p...  79.7 us
    concatenate x4, local copies, waits for them, and re-layouts, rows_of(): jnp.concatenate([own_part.reshape(local, -1, own_part.shape[-1]), other_p...  76.6 us
    dot_general x2, matrix products, expert_rows(): jnp.einsum('jgcd,jdf->jgcf', entered, expert_up, preferred_element_type=s...  42.3 us
    dot_general x2, matrix products, expert_rows(): jnp.einsum('jgcd,jfd->jgcf', dreturned, expert_down, preferred_element_ty...  36 us
  transfers between devices with their start and end apart: 111, of which 34 were waited for; matrix products, arithmetic and copies ran while one was open for 47% of the time, Pallas kernels for 0%

profile of v1, /device:TPU:0, one launch (start us, length us, event | category | flops | bytes accessed | tf_op | source)
XLA Modules:
  0.0 1172.1 jit_solution(734486713820551705)
XLA Ops:
  10.6 17.7 %all_to_all.25 = bf16[8,3,64,256]{3,2,1,0:T(8,128)(2,1)S(1)} all-to-all(bf16[8,3,64,256]{3,2,1,0:T(8,128)(2,1)S(1)} %copy.176), channel_id=1, replica_groups=mesh['dp'=4,'expert'=8] {'expert'}, dimensions={0} | all-to-all | bytes 1572864 | tf_op jit(solution)/shard_map/all_to_all | solution.py:142
  61.7 38.2 %collective-permute-done.90 = s32[9,8,128]{2,0,1:T(8,128)S(1)} collective-permute-done((s32[9,8,128]{2,0,1:T(8,128)S(1)}, s32[9,8,128]{2,0,1:T(8,128)S(1)}, u32[]{:S(2)}, u32[]{:S(2)}) %collective-permute-start.90) | collective-permute-done | bytes 36896 | tf_op jit(solution)/shard_map/ppermute | solution.py:21
  164.6 14.0 %collective-permute-done.92 = bf16[2,128,2048]{2,1,0:T(8,128)(2,1)S(1)} collective-permute-done((bf16[2,128,2048]{2,1,0:T(8,128)(2,1)S(1)}, bf16[2,128,2048]{2,1,0:T(8,128)(2,1)S(1)}, u32[]{:S(2)}, u32[]{:S(2)}) %collective-permute-start.92) | collective-permute-done | bytes 1048608 | tf_op jit(solution)/shard_map/ppermute | solution.py:21
  196.2 36.4 %collective-permute-done.94 = bf16[3,128,2048]{2,1,0:T(8,128)(2,1)} collective-permute-done((bf16[3,128,2048]{2,1,0:T(8,128)(2,1)}, bf16[3,128,2048]{2,1,0:T(8,128)(2,1)}, u32[]{:S(2)}, u32[]{:S(2)}) %collective-permute-start.94) | collective-permute-done | bytes 1572896 | tf_op jit(solution)/shard_map/ppermute | solution.py:21
  237.5 26.2 %collective-permute-done.25 = f32[2,8,128]{2,1,0:T(8,128)S(1)} collective-permute-done((f32[2,8,128]{2,1,0:T(8,128)S(1)}, f32[2,8,128]{2,1,0:T(8,128)S(1)}, u32[]{:S(2)}, u32[]{:S(2)}) %collective-permute-start.25) | collective-permute-done | bytes 8224 | tf_op jit(solution)/shard_map/ppermute | solution.py:21
  354.3 24.4 %multiply_reduce_fusion.2 = (f32[1024]{0:T(1024)S(1)}, f32[1024,2048]{1,0:T(8,128)S(1)}) fusion(bf16[1024,2048]{0,1:T(8,128)(2,1)} %slice_dynamic-update-slice_fusion, bf16[2048,2048]{1,0:T(8,128)(2,1)} %bitcast_select_fusion, bf16[1024,2048]{1,0:T(8,128)(2,1)S(1)} %copy-done.7), kind=kOutput, calls=%fused_computation.70 | convolution fusion | flops 8598322176 | bytes 25169920 | tf_op jit(solution)/shard_map/dot_general | solution.py:16
  392.6 12.0 %multiply_convert_fusion.7 = (bf16[2,4,136,1024]{3,2,1,0:T(8,128)(2,1)S(1)}, f32[2,4,136,1024]{3,2,1,0:T(8,128)}) fusion(f32[2,4,136,1024]{3,2,1,0:T(8,128)S(1)} %fusion.23, bf16[2,2048,1024]{2,1,0:T(8,128)(2,1)} %param.27, bf16[2,4,136,2048]{3,2,0,1:T(8,128)(2,1)S(1)} %convolution_bitcast_fusion.1), kind=kOutput, calls=%fused_computation.80 | convolution fusion | flops 4570087424 | bytes 23986176 | tf_op jit(solution)/shard_map/jgcd,jdf->jgcf/dot_general | solution.py:247
  426.6 14.5 %multiply_convert_fusion.6 = (bf16[2,4,136,1024]{3,2,1,0:T(8,128)(2,1)S(1)}, bf16[2,4,136,1024]{3,2,1,0:T(8,128)(2,1)}) fusion(f32[2,4,136,1024]{3,2,1,0:T(8,128)} %copy-done.116, f32[2,4,136,1024]{3,2,1,0:T(8,128)} %get-tuple-element.218, bf16[2,4,136,2048]{3,2,1,0:T(8,128)(2,1)} %fusion.16, bf16[2,1024,2048]{2,1,0:T(8,128)(2,1)} %param.28), kind=kOutput, calls=%fused_computation.79 | convolution fusion | flops 4577886208 | bytes 26214400 | tf_op jit(solution)/shard_map/jgcd,jfd->jgcf/dot_general | solution.py:251
  441.1 13.5 %fusion.35 = f32[2,4,136,2048]{3,2,0,1:T(8,128)} fusion(bf16[2,2048,1024]{2,1,0:T(8,128)(2,1)} %param.27, bf16[2,4,136,1024]{3,2,1,0:T(8,128)(2,1)} %get-tuple-element.35), kind=kOutput, calls=%fused_computation.60 | convolution fusion | flops 4563402752 | bytes 19529728 | tf_op jit(solution)/shard_map/jgcf,jdf->jgcd/dot_general | solution.py:273
  454.6 12.8 %fusion.39 = f32[4,256,2048,1]{2,1,3,0:T(8,128)} fusion(f32[2,4,136,2048]{3,2,0,1:T(8,128)} %fusion.35, bf16[2,2048,1024]{2,1,0:T(8,128)(2,1)} %param.26, bf16[2,4,136,1024]{3,2,1,0:T(8,128)(2,1)S(1)} %get-tuple-element.34, f32[4,2,256]{2,1,0:T(2,128)S(1)} %fusion.162, f32[136]{0:T(256)S(1)} %add_convert_fusion.3, ...), kind=kOutput, calls=%fused_computation.71 | convolution fusion | flops 5709266944 | bytes 27929120 | tf_op jit(solution)/shard_map/gjct,jgcd->gtd/dot_general | solution.py:275
  479.5 12.8 %convolution_convert_fusion = bf16[1024,2048]{1,0:T(8,128)(2,1)S(1)} fusion(bf16[1024,2048]{1,0:T(8,128)(2,1)S(1)} %multiply_convert_fusion.3, bf16[2048,2048]{1,0:T(8,128)(2,1)} %bitcast_select_fusion), kind=kOutput, calls=%fused_computation.93 | convolution fusion | flops 8592031744 | bytes 16777216 | tf_op jit(solution)/shard_map/dot_general | solution.py:16
  614.9 17.8 %collective-permute-done.38 = bf16[128,2048]{1,0:T(8,128)(2,1)} collective-permute-done((bf16[128,2048]{1,0:T(8,128)(2,1)}, bf16[128,2048]{1,0:T(8,128)(2,1)}, u32[]{:S(2)}, u32[]{:S(2)}) %collective-permute-start.38) | collective-permute-done | bytes 524320 | tf_op jit(solution)/shard_map/ppermute | solution.py:21
  651.3 25.5 %collective-permute-done.55 = f32[2,8,128]{2,1,0:T(8,128)S(1)} collective-permute-done((f32[2,8,128]{2,1,0:T(8,128)S(1)}, f32[2,8,128]{2,1,0:T(8,128)S(1)}, u32[]{:S(2)}, u32[]{:S(2)}) %collective-permute-start.55) | collective-permute-done | bytes 8224 | tf_op jit(solution)/shard_map/ppermute | solution.py:21
  678.0 24.5 %collective-permute-done.56 = f32[2,8,128]{2,1,0:T(8,128)S(1)} collective-permute-done((f32[2,8,128]{2,1,0:T(8,128)S(1)}, f32[2,8,128]{2,1,0:T(8,128)S(1)}, u32[]{:S(2)}, u32[]{:S(2)}) %collective-permute-start.56) | collective-permute-done | bytes 8224 | tf_op jit(solution)/shard_map/ppermute | solution.py:21
  772.2 21.3 %fusion.21 = f32[2,12,136,1024]{3,2,1,0:T(8,128)} fusion(bf16[2,2048,1024]{2,1,0:T(8,128)(2,1)} %param.26, bf16[2,12,136,2048]{3,2,0,1:T(8,128)(2,1)} %convolution_bitcast_fusion), kind=kOutput, calls=%fused_computation.45 | convolution fusion | flops 13690208256 | bytes 35127296 | tf_op jit(solution)/shard_map/jgcd,jdf->jgcf/dot_general | solution.py:246
  816.7 21.5 %fusion.29 = f32[2,12,136,1024]{3,2,1,0:T(8,128)} fusion(bf16[2,1024,2048]{2,1,0:T(8,128)(2,1)} %param.28, bf16[2,12,136,2048]{3,2,0,1:T(8,128)(2,1)} %fusion), kind=kOutput, calls=%fused_computation.53 | convolution fusion | flops 13690208256 | bytes 35127296 | tf_op jit(solution)/shard_map/jgcd,jfd->jgcf/dot_general | solution.py:251
  838.1 11.1 copy.212
  849.3 27.9 %concatenate.230 = bf16[2,1632,1,4,512]{4,3,1,0,2:T(4,128)(2,1)} reshape(bf16[2,12,136,2048]{3,2,1,0:T(8,128)(2,1)} %copy.208) | data formatting | bytes 26738688 | tf_op jit(solution)/shard_map/concatenate | solution.py:378
  877.2 39.8 %fusion.3 = bf16[2,2176,1,1,512]{4,3,1,0,2:T(2,128)(2,1)} fusion(s32[]{:T(128)S(6)} %select_n.141, bf16[2,544,1,4,512]{4,3,1,0,2:T(4,128)(2,1)} %concatenate.227, bf16[2,1632,1,4,512]{4,3,1,0,2:T(4,128)(2,1)} %concatenate.230), kind=kLoop, calls=%fused_computation.23 | loop fusion | flops 8912896 | bytes 22282244 | tf_op jit(solution)/shard_map/concatenate | solution.py:378
  916.9 20.8 %copy.209 = bf16[2,2176,1,1,512]{1,4,0,3,2:T(8,128)(2,1)} copy(bf16[2,2176,1,1,512]{4,3,1,0,2:T(2,128)(2,1)} %fusion.3) | data formatting | bytes 8912896 | tf_op jit(solution)/shard_map/jit(dynamic_index_in_dim)/dynamic_slice | solution.py:391
  937.8 30.3 %multiply_convert_fusion = (bf16[2,12,136,1024]{3,2,1,0:T(8,128)(2,1)}, bf16[2,12,136,1024]{3,2,1,0:T(8,128)(2,1)}, bf16[2,12,136,1024]{3,2,1,0:T(8,128)(2,1)}) fusion(f32[2,12,136,1024]{3,2,1,0:T(8,128)} %fusion.21, f32[2,12,136,1024]{3,2,1,0:T(8,128)} %fusion.29, bf16[2,2048,1024]{2,1,0:T(8,128)(2,1)} %param.27, ...), kind=kOutput, calls=%fused_computation.13 | convolution fusion | flops 13740343296 | bytes 68550656 | tf_op jit(solution)/shard_map/jgcd,jdf->jgcf/dot_general | solution.py:247
  977.7 28.0 %concatenate.238 = bf16[2,1632,1,4,512]{4,3,1,0,2:T(4,128)(2,1)} reshape(bf16[2,12,136,2048]{3,2,1,0:T(8,128)(2,1)} %copy.212) | data formatting | bytes 26738688 | tf_op jit(solution)/shard_map/concatenate | solution.py:378
  1005.7 40.0 %fusion.2 = bf16[2,2176,1,1,512]{4,3,1,0,2:T(2,128)(2,1)} fusion(s32[]{:T(128)S(6)} %select_n.141, bf16[2,544,1,4,512]{4,3,1,0,2:T(4,128)(2,1)} %concatenate.237, bf16[2,1632,1,4,512]{4,3,1,0,2:T(4,128)(2,1)} %concatenate.238), kind=kLoop, calls=%fused_computation.22 | loop fusion | flops 8912896 | bytes 22282244 | tf_op jit(solution)/shard_map/concatenate | solution.py:378
  1067.6 13.3 %fusion.12 = f32[2,1024,512]{2,1,0:T(8,128)} fusion(bf16[2,1632,1024]{1,2,0:T(8,128)(2,1)} %copy.216, bf16[2,544,1024]{1,2,0:T(8,128)(2,1)} %copy.215, bf16[2,2176,1,1,512]{4,3,1,0,2:T(2,128)(2,1)} %fusion.2), kind=kOutput, calls=%fused_computation.32 | convolution fusion | flops 4581228544 | bytes 17563648 | tf_op jit(solution)/shard_map/jrf,jrd->jfd/dot_general | solution.py:410
  (807 shorter events, 610.7 us)
Async XLA Ops:
  7.2 179.1 %all-gather.4.cloned.1.call-start = ((), (), s32[]{:S(2)}) async-start(), calls=%async_computation.9 | async-start | bytes 2621440 | tf_op jit(solution)/shard_map/all_gather | solution.py:144
  29.2 163.0 %all-gather.6.cloned.1.call-start = ((), (), s32[]{:S(2)}) async-start(), calls=%async_computation.10 | async-start | bytes 1310720 | tf_op jit(solution)/shard_map/all_gather | solution.py:145
  30.0 308.6 %all-gather.8.cloned.1.call-start = ((), (), s32[]{:S(2)}) async-start(), calls=%async_computation.11 | async-start | bytes 8650752 | tf_op jit(solution)/shard_map/all_gather | solution.py:147
  34.7 70.6 %collective-permute-start = (bf16[128,2048]{1,0:T(8,128)(2,1)S(1)}, bf16[128,2048]{1,0:T(8,128)(2,1)S(1)}, u32[]{:S(2)}, u32[]{:S(2)}) collective-permute-start(bf16[128,2048]{1,0:T(8,128)(2,1)S(1)} %copy-done.19), channel_id=1, source_target_pairs={{0,1},{1,0},{2,3},{3,2},{4,5},{5,4},{6,7},{7,6},{8,9},{9,8},{10,11... | collective-permute-start | bytes 1572872 | tf_op jit(solution)/shard_map/ppermute | solution.py:21
  35.3 700.7 %reduce-scatter.9.cloned.1.call-start = ((), (), s32[]{:S(2)}) async-start(), calls=%async_computation.14 | async-start | bytes 1310720 | tf_op jit(solution)/shard_map/reduce_scatter | solution.py:340
  43.4 61.1 %collective-permute-start.91 = (bf16[1,128,2048]{2,1,0:T(8,128)(2,1)S(1)}, bf16[1,128,2048]{2,1,0:T(8,128)(2,1)S(1)}, u32[]{:S(2)}, u32[]{:S(2)}) collective-permute-start(bf16[1,128,2048]{2,1,0:T(8,128)(2,1)S(1)} %bitcast.548), channel_id=1, source_target_pairs={{0,24},{8,16},{16,8},{24,0},{1,25},{9,17},{17,9},{25,1},{2,26},{10... | collective-permute-start | bytes 1572872 | tf_op jit(solution)/shard_map/ppermute | solution.py:21
  184.8 105.8 %collective-permute-start.96 = (bf16[3,128,2048]{2,1,0:T(8,128)(2,1)}, bf16[3,128,2048]{2,1,0:T(8,128)(2,1)}, u32[]{:S(2)}, u32[]{:S(2)}) collective-permute-start(bf16[3,128,2048]{2,1,0:T(8,128)(2,1)} %constant_dynamic-update-slice_fusion.84), channel_id=1, source_target_pairs={{0,4},{1,5},{2,6},{3,7},{4,0},{5,1},{6,2},{7,3},{8,12},{9,13},{10,... | collective-permute-start | bytes 4718600 | tf_op jit(solution)/shard_map/ppermute | solution.py:21
  184.8 107.9 %collective-permute-start.98 = (bf16[3,128,2048]{2,1,0:T(8,128)(2,1)}, bf16[3,128,2048]{2,1,0:T(8,128)(2,1)}, u32[]{:S(2)}, u32[]{:S(2)}) collective-permute-start(bf16[3,128,2048]{2,1,0:T(8,128)(2,1)} %constant_dynamic-update-slice_fusion.84), channel_id=1, source_target_pairs={{0,6},{1,7},{2,4},{3,5},{4,2},{5,3},{6,0},{7,1},{8,14},{9,15},{10,... | collective-permute-start | bytes 4718600 | tf_op jit(solution)/shard_map/ppermute | solution.py:21
  232.5 78.3 %collective-permute-start.95 = (bf16[3,128,2048]{2,1,0:T(8,128)(2,1)}, bf16[3,128,2048]{2,1,0:T(8,128)(2,1)}, u32[]{:S(2)}, u32[]{:S(2)}) collective-permute-start(bf16[3,128,2048]{2,1,0:T(8,128)(2,1)} %collective-permute-done.94), channel_id=1, source_target_pairs={{0,1},{1,0},{2,3},{3,2},{4,5},{5,4},{6,7},{7,6},{8,9},{9,8},{10,11... | collective-permute-start | bytes 4718600 | tf_op jit(solution)/shard_map/ppermute | solution.py:21
  494.7 69.3 %collective-permute-start.35 = (bf16[4,128,2048]{2,1,0:T(8,128)(2,1)}, bf16[4,128,2048]{2,1,0:T(8,128)(2,1)}, u32[]{:S(2)}, u32[]{:S(2)}) collective-permute-start(bf16[4,128,2048]{2,1,0:T(8,128)(2,1)} %pad_maximum_fusion), channel_id=1, source_target_pairs={{0,1},{1,0},{2,3},{3,2},{4,5},{5,4},{6,7},{7,6},{8,9},{9,8},{10,11... | collective-permute-start | bytes 6291464 | tf_op jit(solution)/shard_map/ppermute | solution.py:21
  496.8 70.8 %collective-permute-start.46 = (bf16[4,128,2048]{2,1,0:T(8,128)(2,1)}, bf16[4,128,2048]{2,1,0:T(8,128)(2,1)}, u32[]{:S(2)}, u32[]{:S(2)}) collective-permute-start(bf16[4,128,2048]{2,1,0:T(8,128)(2,1)} %pad_maximum_fusion.1), channel_id=1, source_target_pairs={{0,1},{1,0},{2,3},{3,2},{4,5},{5,4},{6,7},{7,6},{8,9},{9,8},{10,11... | collective-permute-start | bytes 6291464 | tf_op jit(solution)/shard_map/ppermute | solution.py:21
  556.2 172.7 %collective-permute-start.81 = (bf16[3,128,2048]{2,1,0:T(8,128)(2,1)}, bf16[3,128,2048]{2,1,0:T(8,128)(2,1)}, u32[]{:S(2)}, u32[]{:S(2)}) collective-permute-start(bf16[3,128,2048]{2,1,0:T(8,128)(2,1)} %constant_dynamic-update-slice_fusion.82), channel_id=1, source_target_pairs={{0,1},{1,0},{2,3},{3,2},{4,5},{5,4},{6,7},{7,6},{8,9},{9,8},{10,11... | collective-permute-start | bytes 4718600 | tf_op jit(solution)/shard_map/ppermute | solution.py:21
  567.6 155.9 %collective-permute-start.82 = (bf16[3,128,2048]{2,1,0:T(8,128)(2,1)}, bf16[3,128,2048]{2,1,0:T(8,128)(2,1)}, u32[]{:S(2)}, u32[]{:S(2)}) collective-permute-start(bf16[3,128,2048]{2,1,0:T(8,128)(2,1)} %constant_dynamic-update-slice_fusion.82), channel_id=1, source_target_pairs={{0,2},{1,3},{2,0},{3,1},{4,6},{5,7},{6,4},{7,5},{8,10},{9,11},{10,... | collective-permute-start | bytes 4718600 | tf_op jit(solution)/shard_map/ppermute | solution.py:21
  576.5 56.3 %collective-permute-start.38 = (bf16[128,2048]{1,0:T(8,128)(2,1)}, bf16[128,2048]{1,0:T(8,128)(2,1)}, u32[]{:S(2)}, u32[]{:S(2)}) collective-permute-start(bf16[128,2048]{1,0:T(8,128)(2,1)} %get-tuple-element.45), channel_id=1, source_target_pairs={{0,6},{1,7},{2,4},{3,5},{4,2},{5,3},{6,0},{7,1},{8,14},{9,15},{10,... | collective-permute-start | bytes 1572872 | tf_op jit(solution)/shard_map/ppermute | solution.py:21
  588.2 55.2 %collective-permute-start.36 = (bf16[128,2048]{1,0:T(8,128)(2,1)}, bf16[128,2048]{1,0:T(8,128)(2,1)}, u32[]{:S(2)}, u32[]{:S(2)}) collective-permute-start(bf16[128,2048]{1,0:T(8,128)(2,1)} %get-tuple-element.44), channel_id=1, source_target_pairs={{0,2},{1,3},{2,0},{3,1},{4,6},{5,7},{6,4},{7,5},{8,10},{9,11},{10,... | collective-permute-start | bytes 1572872 | tf_op jit(solution)/shard_map/ppermute | solution.py:21
  611.4 514.8 %reduce-scatter.5.cloned.1.call-start = ((), (), s32[]{:S(2)}) async-start(), calls=%async_computation.12 | async-start | bytes 1310720 | tf_op jit(solution)/shard_map/reduce_scatter | solution.py:340
  632.7 97.7 %collective-permute-start.84 = (bf16[3,128,2048]{2,1,0:T(8,128)(2,1)}, bf16[3,128,2048]{2,1,0:T(8,128)(2,1)}, u32[]{:S(2)}, u32[]{:S(2)}) collective-permute-start(bf16[3,128,2048]{2,1,0:T(8,128)(2,1)} %constant_dynamic-update-slice_fusion.82), channel_id=1, source_target_pairs={{0,4},{1,5},{2,6},{3,7},{4,0},{5,1},{6,2},{7,3},{8,12},{9,13},{10,... | collective-permute-start | bytes 4718600 | tf_op jit(solution)/shard_map/ppermute | solution.py:21
  633.6 106.7 %collective-permute-start.86 = (bf16[3,128,2048]{2,1,0:T(8,128)(2,1)}, bf16[3,128,2048]{2,1,0:T(8,128)(2,1)}, u32[]{:S(2)}, u32[]{:S(2)}) collective-permute-start(bf16[3,128,2048]{2,1,0:T(8,128)(2,1)} %constant_dynamic-update-slice_fusion.82), channel_id=1, source_target_pairs={{0,6},{1,7},{2,4},{3,5},{4,2},{5,3},{6,0},{7,1},{8,14},{9,15},{10,... | collective-permute-start | bytes 4718600 | tf_op jit(solution)/shard_map/ppermute | solution.py:21
  707.0 387.2 %collective-permute-start.49 = (bf16[128,2048]{1,0:T(8,128)(2,1)}, bf16[128,2048]{1,0:T(8,128)(2,1)}, u32[]{:S(2)}, u32[]{:S(2)}) collective-permute-start(bf16[128,2048]{1,0:T(8,128)(2,1)} %get-tuple-element.39), channel_id=1, source_target_pairs={{0,6},{1,7},{2,4},{3,5},{4,2},{5,3},{6,0},{7,1},{8,14},{9,15},{10,... | collective-permute-start | bytes 1572872 | tf_op jit(solution)/shard_map/ppermute | solution.py:21
  713.8 421.0 %reduce-scatter.7.cloned.1.call-start = ((), (), s32[]{:S(2)}) async-start(), calls=%async_computation.13 | async-start | bytes 1310720 | tf_op jit(solution)/shard_map/reduce_scatter | solution.py:340
  728.9 365.3 %collective-permute-start.48 = (bf16[128,2048]{1,0:T(8,128)(2,1)}, bf16[128,2048]{1,0:T(8,128)(2,1)}, u32[]{:S(2)}, u32[]{:S(2)}) collective-permute-start(bf16[128,2048]{1,0:T(8,128)(2,1)} %get-tuple-element.40), channel_id=1, source_target_pairs={{0,4},{1,5},{2,6},{3,7},{4,0},{5,1},{6,2},{7,3},{8,12},{9,13},{10,... | collective-permute-start | bytes 1572872 | tf_op jit(solution)/shard_map/ppermute | solution.py:21
  736.0 390.2 %all-to-all-start.3 = ((bf16[8,64,256]{2,1,0:T(8,128)(2,1)}), bf16[8,64,256]{2,1,0:T(8,128)(2,1)}, u32[]{:S(2)}, u32[]{:S(2)}) async-start(bf16[8,64,256]{2,1,0:T(8,128)(2,1)} %bitcast.582), calls=%async_computation.6 | async-start | bytes 524288 | tf_op jit(solution)/shard_map/all_to_all | solution.py:343
  740.1 413.8 %reduce-scatter.11.cloned.1.call-start = ((), (), s32[]{:S(2)}) async-start(), calls=%async_computation.15 | async-start | bytes 1310720 | tf_op jit(solution)/shard_map/reduce_scatter | solution.py:340
  740.3 320.9 %collective-permute-start.58 = (bf16[4,128,2048]{2,1,0:T(8,128)(2,1)}, bf16[4,128,2048]{2,1,0:T(8,128)(2,1)}, u32[]{:S(2)}, u32[]{:S(2)}) collective-permute-start(bf16[4,128,2048]{2,1,0:T(8,128)(2,1)} %pad_maximum_fusion.3), channel_id=1, source_target_pairs={{0,1},{1,0},{2,3},{3,2},{4,5},{5,4},{6,7},{7,6},{8,9},{9,8},{10,11... | collective-permute-start | bytes 6291464 | tf_op jit(solution)/shard_map/ppermute | solution.py:21
  (217 other events, 5186.6 us)
Sparse Core Ops, SparseCore 0:
  29.3 72.8 all-gather.3
  104.3 27.0 all-gather.5
  134.3 95.6 all-gather.7
  611.5 25.2 reduce-scatter.8
  713.9 25.0 reduce-scatter.4
  741.2 25.7 reduce-scatter.6
  1123.4 25.0 reduce-scatter.10

commit v2 on v1

v2 whole, which is shorter than its diff:
```python
import functools
import math

import jax
import jax.numpy as jnp
from jax import lax
from jax.experimental import pallas as pl
from jax.experimental.pallas import tpu as pltpu
from jax.sharding import PartitionSpec as P

HEAD = 128
eps_norm = 1e-05
rope_base = 10000.0
single = jnp.float32
bfloat = jnp.bfloat16


def dot32(left, right, dims):
    return lax.dot_general(left, right, (dims, ((), ())), preferred_element_type=single)


def after(values, *earlier):
    for result in earlier:
        zero = jnp.minimum(jnp.abs(result[(-1,) * result.ndim]), 0)
        values = values + zero.astype(values.dtype)
    return values


def swap(values, axis, mask):
    count = lax.axis_size(axis)
    return lax.ppermute(values, axis, [(i, i ^ mask) for i in range(count)])


def slot_order():
    count = lax.axis_size("expert")
    return list(range(0, count, 2)) + list(range(1, count, 2))


def gather_chips(values):
    count = lax.axis_size("expert")
    return [values if mask == 0 else swap(values, "expert", mask) for mask in range(0, count, 2)]


def gather_halves(values, *earlier):
    even = after(jnp.stack(gather_chips(values)), *earlier)
    return even, swap(even, "expert", 1)


def gather_steps(values, axis, count, first=None):
    held = values[None]
    order = [0]
    mask = count - 1
    while mask > 0:
        other = first if first is not None and mask == count - 1 else swap(held, axis, mask)
        held = jnp.concatenate([held, other], axis=0)
        order = order + [place ^ mask for place in order]
        mask >>= 1
    return held, order


def scatter_sum(even, odd, with_first=False):
    half = lax.axis_size("expert") // 2
    rows = even.shape[0] // half
    arrived = swap(odd, "expert", 1)
    total = None
    for place in reversed(range(half)):
        part = slice(place * rows, (place + 1) * rows)
        pair = even[part].astype(single) + arrived[part].astype(single)
        if place > 0:
            pair = swap(pair.astype(bfloat), "expert", 2 * place).astype(single)
        if place == half - 1:
            first = arrived
        total = pair if total is None else total + pair
    return (total, first) if with_first else total


def sum_rows_over_expert(values):
    order = slot_order()

    def reorder(array, mask):
        return jnp.concatenate(
            [array[:, order.index(s ^ mask)][:, None] for s in order], axis=1
        )

    total = values + reorder(swap(values, "expert", 1), 1)
    out = total
    for mask in range(2, len(order), 2):
        out = out + reorder(swap(total, "expert", mask), mask)
    return out


def rows_of_group(pieces, g, groups, ids_ref):
    if len(pieces) == 2:
        return jnp.concatenate([pieces[0][0, g], pieces[1][0, g]], axis=0)
    if len(pieces) > 2:
        return jnp.concatenate([pieces[g][0], pieces[groups + g][0]], axis=0)
    at = 2 + ids_ref[1]
    return jnp.concatenate(
        [pieces[0][0, ids_ref[at + 2 * g]], pieces[0][0, ids_ref[at + 2 * g + 1]]], axis=0
    )


def enter_rows(ids_ref, rank_ref, prob_ref, mid_refs, cot_refs, groups, block, cap, put):
    spots = lax.broadcasted_iota(jnp.int32, (cap, block), 0).astype(single) + 1.0
    for g in range(groups):
        pick = rank_ref[0, 0, g : g + 1, :] == spots
        pick_b = pick.astype(single).astype(bfloat)
        gate_col = jnp.sum(
            jnp.where(pick, prob_ref[0, 0, g : g + 1, :], 0.0), axis=1, keepdims=True
        )
        entered = dot32(pick_b, rows_of_group(mid_refs, g, groups, ids_ref), ((1,), (0,)))
        cot_row = dot32(pick_b, rows_of_group(cot_refs, g, groups, ids_ref), ((1,), (0,)))
        put(g, entered.astype(bfloat), (cot_row * gate_col).astype(bfloat))


def hidden_and_gradients(x, d, gate, up, down):
    gate_act = dot32(x, gate, ((1,), (0,)))
    up_act = dot32(x, up, ((1,), (0,)))
    sig = 1.0 / (1.0 + jnp.exp(-gate_act))
    silu = gate_act * sig
    hidden = (silu * up_act).astype(bfloat)
    dhidden = dot32(d, down, ((1,), (1,)))
    gate_lin = (dhidden * up_act * sig * (1.0 + gate_act * (1.0 - sig))).astype(bfloat)
    up_lin = (dhidden * silu).astype(bfloat)
    return hidden, gate_lin, up_lin


def cut_of(array, ids_ref, near, far, span):
    parts = [
        array[:, pl.ds(pl.multiple_of((u * near + ids_ref[0]) * span, span), span)]
        for u in range(far)
    ]
    return parts[0] if far == 1 else jnp.concatenate(parts, axis=1)


def own_kernel(
    groups, block, cap, near, far, span, ids_ref, rank_ref, prob_ref, mid_even, mid_odd, cot_even,
    cot_odd, gate_ref, up_ref, down_ref, all_prob_ref, router_ref, hidden_out, gate_out, up_out,
    x_cut, d_cut, moe_even, moe_odd, dmid_even, dmid_odd, dlog_ref, rows_x, rows_d, sum_r, sum_x,
):
    e = pl.program_id(0)
    f = pl.program_id(1)

    @pl.when(f == 0)
    def _():
        def put(g, entered, dreturned):
            rows_x[g * cap : (g + 1) * cap, :] = entered
            rows_d[g * cap : (g + 1) * cap, :] = dreturned

        enter_rows(
            ids_ref, rank_ref, prob_ref, (mid_even, mid_odd), (cot_even, cot_odd), groups, block, cap, put
        )
        x_cut[0] = cut_of(rows_x, ids_ref, near, far, span)
        d_cut[0] = cut_of(rows_d, ids_ref, near, far, span)

    hidden, gate_lin, up_lin = hidden_and_gradients(
        rows_x[...], rows_d[...], gate_ref[0], up_ref[0], down_ref[0]
    )
    hidden_out[0] = hidden
    gate_out[0] = gate_lin
    up_out[0] = up_lin

    def parts():
        r_part = dot32(hidden, down_ref[0], ((1,), (0,)))
        x_part = dot32(gate_lin, gate_ref[0], ((1,), (1,))) + dot32(
            up_lin, up_ref[0], ((1,), (1,))
        )
        return r_part, x_part

    @pl.when(f == 0)
    def _():
        sum_r[...], sum_x[...] = parts()

    @pl.when(f > 0)
    def _():
        r_part, x_part = parts()
        sum_r[...] += r_part
        sum_x[...] += x_part

    @pl.when(f == pl.num_programs(1) - 1)
    def _():
        half = block // 2
        experts = all_prob_ref.shape[1]
        expert_row = lax.broadcasted_iota(jnp.int32, (experts, block), 0)
        spots = lax.broadcasted_iota(jnp.int32, (cap, block), 0).astype(single) + 1.0
        for g in range(groups):
            pick = rank_ref[0, 0, g : g + 1, :] == spots
            pick_f = pick.astype(single)
            pick_b = pick_f.astype(bfloat)
            weighted = (pick_f * prob_ref[0, 0, g : g + 1, :]).astype(bfloat)
            returned = sum_r[g * cap : (g + 1) * cap, :].astype(bfloat)
            cot_row = dot32(
                pick_b, rows_of_group((cot_even, cot_odd), g, groups, ids_ref), ((1,), (0,))
            )
            dgate = jnp.sum(cot_row * returned.astype(single), axis=1, keepdims=True)
            dgate = jnp.sum(jnp.where(pick, dgate, 0.0), axis=0, keepdims=True)
            probs = all_prob_ref[g]
            mine = jnp.where(expert_row == ids_ref[1] + e, dgate, 0.0)
            inner = jnp.sum(probs * mine, axis=0, keepdims=True)
            dlog = probs * (mine - inner)
            moe = dot32(weighted, returned, ((0,), (0,)))
            dmid = dot32(
                pick_b, sum_x[g * cap : (g + 1) * cap, :].astype(bfloat), ((0,), (0,))
            ) + dot32(dlog.astype(bfloat), router_ref[...], ((0,), (0,)))
            rows = slice(g * half, (g + 1) * half)

            @pl.when(e == 0)
            def _():
                dlog_ref[g] = dlog
                moe_even[rows, :] = moe[:half].astype(bfloat)
                moe_odd[rows, :] = moe[half:].astype(bfloat)
                dmid_even[rows, :] = dmid[:half].astype(bfloat)
                dmid_odd[rows, :] = dmid[half:].astype(bfloat)

            @pl.when(e > 0)
            def _():
                dlog_ref[g] += dlog
                for ref, add in (
                    (moe_even, moe[:half]),
                    (moe_odd, moe[half:]),
                    (dmid_even, dmid[:half]),
                    (dmid_odd, dmid[half:]),
                ):
                    ref[rows, :] = (ref[rows, :].astype(single) + add).astype(bfloat)


def others_kernel(
    mids, cots, groups, block, cap, near, far, span, more, ids_ref, rank_ref, prob_ref, *refs
):
    mid_refs, cot_refs, refs = refs[:mids], refs[mids : mids + cots], refs[mids + cots :]
    gate_ref, up_ref, down_ref = refs[:3]
    refs = refs[3:]
    if more:
        own_refs, in_refs, refs = refs[:5], refs[5:8], refs[8:]
    gate_out, up_out, down_out, rows_x, rows_d, hidden_all, gate_all, up_all = refs
    f = pl.program_id(1)
    p = pl.program_id(2)
    height = groups * cap

    @pl.when(f == 0)
    def _():
        def put(g, entered, dreturned):
            rows_x[pl.ds(p * height + g * cap, cap), :] = entered
            rows_d[pl.ds(p * height + g * cap, cap), :] = dreturned

        enter_rows(ids_ref, rank_ref, prob_ref, mid_refs, cot_refs, groups, block, cap, put)

    here = pl.ds(pl.multiple_of(p * height, 16), height)
    hidden, gate_lin, up_lin = hidden_and_gradients(
        rows_x[here, :], rows_d[here, :], gate_ref[0], up_ref[0], down_ref[0]
    )
    hidden_all[here, :] = hidden
    gate_all[here, :] = gate_lin
    up_all[here, :] = up_lin

    @pl.when(p == pl.num_programs(2) - 1)
    def _():
        x_cut = cut_of(rows_x, ids_ref, near, far, span)
        d_cut = cut_of(rows_d, ids_ref, near, far, span)
        gate_part = dot32(x_cut, gate_all[...], ((0,), (0,)))
        up_part = dot32(x_cut, up_all[...], ((0,), (0,)))
        down_part = dot32(hidden_all[...], d_cut, ((0,), (0,)))
        if more:
            x_own, d_own, hidden_own, gate_own, up_own = [ref[0] for ref in own_refs]
            gate_part += in_refs[0][0] + dot32(x_own, gate_own, ((0,), (0,)))
            up_part += in_refs[1][0] + dot32(x_own, up_own, ((0,), (0,)))
            down_part += in_refs[2][0] + dot32(hidden_own, d_own, ((0,), (0,)))
        gate_out[0] = gate_part
        up_out[0] = up_part
        down_out[0] = down_part


vmem = 60 * 1024 * 1024
chunk_units = 512


def routed_own(ids, cap, near, far, rank, prob, mid, cot, gate, up, down, probs, router_t):
    local, _, groups, block = rank.shape
    model = mid[0].shape[-1]
    tokens = groups * block
    units = gate.shape[2]
    chunk = min(chunk_units, units)
    span = model // (near * far)
    own_cols = far * span
    height = groups * cap

    def fixed(shape):
        return pl.BlockSpec(shape, lambda e, f, s: (0,) * len(shape), pipeline_mode=pl.Buffered(1))

    table = pl.BlockSpec((1, 1, groups, block), lambda e, f, s: (e, 0, 0, 0))
    wide = pl.BlockSpec((1, model, chunk), lambda e, f, s: (e, 0, f))
    tall = pl.BlockSpec((1, chunk, model), lambda e, f, s: (e, f, 0))
    lin = pl.BlockSpec((1, height, chunk), lambda e, f, s: (e, 0, f))
    cut = pl.BlockSpec((1, height, own_cols), lambda e, f, s: (e, 0, 0))
    args = [rank, prob, *mid, *cot, gate, up, down, probs, router_t]
    return pl.pallas_call(
        functools.partial(own_kernel, groups, block, cap, near, far, span),
        grid_spec=pltpu.PrefetchScalarGridSpec(
            num_scalar_prefetch=1,
            grid=(local, units // chunk),
            in_specs=[table, table]
            + [fixed(piece.shape) for piece in (*mid, *cot)]
            + [wide, wide, tall, fixed(probs.shape), fixed(router_t.shape)],
            out_specs=[lin] * 3 + [cut] * 2 + [fixed((tokens // 2, model))] * 4 + [fixed(probs.shape)],
            scratch_shapes=[pltpu.VMEM((height, model), bfloat)] * 2
            + [pltpu.VMEM((height, model), single)] * 2,
        ),
        out_shape=[jax.ShapeDtypeStruct((local, height, units), bfloat)] * 3
        + [jax.ShapeDtypeStruct((local, height, own_cols), bfloat)] * 2
        + [jax.ShapeDtypeStruct((tokens // 2, model), bfloat)] * 4
        + [jax.ShapeDtypeStruct(probs.shape, single)],
        compiler_params=pltpu.CompilerParams(
            dimension_semantics=("arbitrary",) * 2, vmem_limit_bytes=vmem
        ),
        cost_estimate=pl.CostEstimate(
            flops=12 * local * height * model * units,
            bytes_accessed=48 << 20,
            transcendentals=height * units,
        ),
        name="routed_own",
    )(ids, *args)


def routed_others(ids, cap, near, far, rank, prob, mid, cot, gate, up, down, more=None):
    local, planes, groups, block = rank.shape
    model = mid.shape[-1]
    units = gate.shape[2]
    chunk = min(chunk_units, units)
    span = model // (near * far)
    own_cols = far * span
    height = groups * cap
    mode = pl.Buffered(1) if planes == 1 else None

    def at_plane(ndim):
        def place(e, f, p, s):
            return (s[2 + jnp.where(f == 0, p, planes - 1)],) + (0,) * (ndim - 1)

        return place

    def rows_spec(piece):
        return pl.BlockSpec((1,) + piece.shape[1:], at_plane(piece.ndim), pipeline_mode=mode)

    table = pl.BlockSpec((1, 1, groups, block), lambda e, f, p, s: (e, p, 0, 0))
    wide = pl.BlockSpec((1, model, chunk), lambda e, f, p, s: (e, 0, f))
    tall = pl.BlockSpec((1, chunk, model), lambda e, f, p, s: (e, f, 0))
    wide_grad = pl.BlockSpec((1, own_cols, chunk), lambda e, f, p, s: (e, 0, f))
    tall_grad = pl.BlockSpec((1, chunk, own_cols), lambda e, f, p, s: (e, f, 0))
    lin = pl.BlockSpec((1, height, chunk), lambda e, f, p, s: (e, 0, f))
    cut = pl.BlockSpec((1, height, own_cols), lambda e, f, p, s: (e, 0, 0))
    in_specs = [table, table] + [rows_spec(piece) for piece in (mid, *cot)] + [wide, wide, tall]
    args = [rank, prob, mid, *cot, gate, up, down]
    aliases = {}
    if more is not None:
        in_specs += [cut, cut, lin, lin, lin, wide_grad, wide_grad, tall_grad]
        args += list(more)
        aliases = {len(args) - 2: 0, len(args) - 1: 1, len(args): 2}
    return pl.pallas_call(
        functools.partial(
            others_kernel, 1, len(cot), groups, block, cap, near, far, span, more is not None
        ),
        grid_spec=pltpu.PrefetchScalarGridSpec(
            num_scalar_prefetch=1,
            grid=(local, units // chunk, planes),
            in_specs=in_specs,
            out_specs=[wide_grad, wide_grad, tall_grad],
            scratch_shapes=[pltpu.VMEM((planes * height, model), bfloat)] * 2
            + [pltpu.VMEM((planes * height, chunk), bfloat)] * 3,
        ),
        out_shape=[
            jax.ShapeDtypeStruct((local, own_cols, units), single),
            jax.ShapeDtypeStruct((local, own_cols, units), single),
            jax.ShapeDtypeStruct((local, units, own_cols), single),
        ],
        input_output_aliases=aliases,
        compiler_params=pltpu.CompilerParams(
            dimension_semantics=("arbitrary",) * 3, vmem_limit_bytes=vmem
        ),
        cost_estimate=pl.CostEstimate(
            flops=8 * local * planes * height * model * units,
            bytes_accessed=64 << 20,
            transcendentals=planes * height * units,
        ),
        name="routed_others",
    )(ids, *args)


def per_device(
    tokens,
    attn_query,
    attn_key,
    attn_value,
    attn_output,
    norm_in,
    norm_query,
    norm_key,
    norm_mid,
    router,
    expert_gate,
    expert_up,
    expert_down,
    routes,
    pieces,
    cotangent,
):
    n = lax.axis_size("expert")
    m = lax.axis_size("dp")
    rows, model = tokens.shape
    shard = attn_query.shape[0]
    experts = router.shape[1]
    top = routes.shape[1]
    local = expert_gate.shape[0]
    length = rows * n
    near = min(m, 4)
    far = m // near
    groups = [[g * near * n + i for i in range(near * n)] for g in range(far)] if far > 1 else None

    def gather_near(values):
        full = lax.all_gather(values, ("dp", "expert"), axis=0, axis_index_groups=groups)
        return full.reshape((near, n) + values.shape)

    half = n // 2
    width = model // n
    heads = width // HEAD
    block = 2 * rows
    mine = lax.axis_index("expert")
    plane = lax.axis_index("dp")
    scale = HEAD ** (-0.5)
    order = slot_order()
    slots = jnp.asarray(order, jnp.int32) ^ mine
    cap = -(-2 * min(rows, rows * top // experts + rows // 32) // 16) * 16

    parts = jnp.stack([attn_query, attn_key, attn_value]).reshape(3, shard, n, width)
    parts_out = parts.transpose(2, 0, 1, 3)
    parts = lax.all_to_all(parts_out, "expert", split_axis=0, concat_axis=0, tiled=True)
    parts = parts.transpose(1, 0, 2, 3).reshape(3, n * shard, width)

    def all_rows(part, first=None):
        held, places = gather_steps(part, "dp", m, first)
        out = []
        for kind in range(part.shape[0]):
            full = jnp.zeros((m, n * shard, width), bfloat)
            for at, kd in enumerate(places):
                full = lax.dynamic_update_slice(
                    full, held[at, kind][None], (plane ^ kd, jnp.int32(0), jnp.int32(0))
                )
            out.append(full.reshape(model, width))
        return out

    first_rows = swap(parts[None, :2], "dp", m - 1)
    x_even, x_odd = gather_halves(after(tokens, parts), first_rows)
    w_q, w_k = all_rows(parts[:2], first_rows)
    cot_even, cot_odd = gather_halves(after(cotangent, x_odd))
    packed = jnp.concatenate(
        [norm_in[None], norm_query[None], norm_key[None], norm_mid[None], router.T], axis=0
    )
    kinds = packed.shape[0]
    packed = jnp.concatenate(
        [
            jnp.pad(packed.reshape(-1), (0, -kinds * shard % HEAD)).reshape(-1, HEAD),
            routes.T.astype(bfloat).reshape(top * rows // HEAD, HEAD),
            pieces.astype(bfloat).reshape(rows // HEAD, HEAD),
        ],
        axis=0,
    )
    packed = after(packed, parts_out)
    small = jnp.stack([packed] + [swap(packed, "dp", mask) for mask in range(1, m)])
    small = jnp.concatenate(gather_halves(small), axis=0)
    cut = -(-kinds * shard // HEAD)
    gains = jnp.take(small[:, :, :cut], jnp.asarray([order.index(j) for j in range(n)]), axis=0)
    gains = jnp.take(gains, jnp.arange(n, dtype=jnp.int32) ^ mine, axis=0)
    gains = jnp.take(gains, jnp.arange(m, dtype=jnp.int32) ^ plane, axis=1)
    gains = gains.reshape(n, m, -1)[:, :, : kinds * shard].reshape(n, m, kinds, shard).transpose(2, 1, 0, 3).reshape(kinds, model)
    gain_in, gain_query, gain_key, gain_mid = [gains[i].astype(single) for i in range(4)]
    router_t = gains[4:]
    piece_row = small[:, 0, cut + top * rows // HEAD :].reshape(length)
    route_rows = small[:, :, cut : cut + top * rows // HEAD].reshape(n, m, top, rows)

    x = jnp.concatenate([x_even, x_odd], axis=0).reshape(length, model).astype(single)
    rs_in = lax.rsqrt(jnp.mean(x * x, axis=-1, keepdims=True) + eps_norm)
    normed_b = (x * rs_in * gain_in).astype(bfloat)
    normed_b = after(normed_b, cot_odd)
    query_raw = dot32(normed_b, w_q, ((1,), (0,)))
    key_raw = dot32(normed_b, w_k, ((1,), (0,)))
    (w_v,) = all_rows(after(parts[2:], w_k, cot_odd))
    near_groups = [[g * near + i for i in range(near)] for g in range(far)] if far > 1 else None
    cot_chunks = [
        lax.all_gather(after(cot_even[place], w_k), "dp", axis=0, axis_index_groups=near_groups)
        for place in range(half)
    ]
    own_shards = []
    send = after(attn_output, w_v)
    for turn in range(m):
        pairs = [(s, ((s % m + turn) % m) * n + s // m) for s in range(m * n)]
        own_shards.append(lax.ppermute(send, ("dp", "expert"), pairs))
    wo = jnp.zeros((m, shard, model), bfloat)
    for turn in range(m):
        wo = lax.dynamic_update_slice(
            wo, own_shards[turn][None], ((plane - turn) % m, jnp.int32(0), jnp.int32(0))
        )
    wo = wo.reshape(width, model)

    squares = jnp.stack([jnp.sum(query_raw**2, axis=-1), jnp.sum(key_raw**2, axis=-1)])
    squares = sum_rows_over_expert(squares.reshape(2, n, rows)).reshape(2, length)
    rs_q = lax.rsqrt(squares[0] / model + eps_norm)[:, None]
    rs_k = lax.rsqrt(squares[1] / model + eps_norm)[:, None]
    value_b = dot32(normed_b, w_v, ((1,), (0,))).astype(bfloat)

    place = (slots[:, None] * rows + jnp.arange(rows, dtype=jnp.int32)[None, :]).reshape(length)
    turn_half = HEAD // 2
    inverse = jnp.exp(jnp.arange(turn_half, dtype=single) * (-2.0 * math.log(rope_base) / HEAD))
    angles = place.astype(single)[:, None] * inverse[None, :]
    cosine = jnp.cos(angles)
    sine = jnp.sin(angles)

    def rotate(values, back):
        out = []
        sn = -sine if back else sine
        for h in range(heads):
            u = values[:, h * HEAD : h * HEAD + turn_half]
            w = values[:, h * HEAD + turn_half : (h + 1) * HEAD]
            out += [u * cosine - w * sn, w * cosine + u * sn]
        return jnp.concatenate(out, axis=-1)

    own_gain_q = lax.dynamic_slice_in_dim(gain_query, mine * width, width)
    own_gain_k = lax.dynamic_slice_in_dim(gain_key, mine * width, width)
    query_b = rotate(query_raw * rs_q * own_gain_q, False).astype(bfloat)
    key_b = rotate(key_raw * rs_k * own_gain_k, False).astype(bfloat)

    def per_head(array):
        return [array[:, h * HEAD : (h + 1) * HEAD] for h in range(heads)]

    allowed = (place[None, :] <= place[:, None]) | (
        (piece_row[:, None] == piece_row[None, :]) & (piece_row[:, None] > 0)
    )
    probs = []
    mixed = []
    for q_h, k_h, v_h in zip(per_head(query_b), per_head(key_b), per_head(value_b)):
        scores = jnp.where(allowed, dot32(q_h, k_h, ((1,), (1,))) * scale, -1e30)
        exponent = jnp.exp(scores - jnp.max(scores, axis=-1, keepdims=True))
        prob = exponent / jnp.sum(exponent, axis=-1, keepdims=True)
        probs.append(prob)
        mixed.append(dot32(prob.astype(bfloat), v_h, ((1,), (0,))))
    attended = jnp.concatenate(mixed, axis=-1).astype(bfloat)

    def halves(array):
        return array[: length // 2], array[length // 2 :]

    projected = [dot32(part, wo, ((1,), (0,))).astype(bfloat) for part in halves(attended)]
    x_own = tokens.astype(single)
    residual = x_own + scatter_sum(*projected)
    rs_mid = lax.rsqrt(jnp.mean(residual * residual, axis=-1, keepdims=True) + eps_norm)
    mid = (residual * rs_mid * gain_mid).astype(bfloat)
    mid_even, mid_odd = gather_halves(mid)
    mid_planes = gather_near(after(mid, mid_odd))

    def router_probs_of(mid_rows):
        logits = dot32(router_t, mid_rows.reshape(-1, model), ((1,), (1,)))
        exponent = jnp.exp(logits - jnp.max(logits, axis=0, keepdims=True))
        return exponent / jnp.sum(exponent, axis=0, keepdims=True)

    upper = (
        jnp.arange(block, dtype=jnp.int32)[:, None] <= jnp.arange(block, dtype=jnp.int32)[None, :]
    ).astype(bfloat)
    ids = (mine * local + jnp.arange(local, dtype=jnp.int32)).astype(bfloat)

    def ranks(kd):
        named = route_rows[:, kd]
        hit = jnp.any(named[None] == ids[:, None, None, None], axis=2)
        hit = jnp.concatenate([hit[:, :half], hit[:, half:]], axis=-1)
        rank = lax.dot_general(
            hit.astype(bfloat), upper, (((2,), (0,)), ((), ())), preferred_element_type=single
        )
        return jnp.where(hit, rank, 0.0)

    def local_probs(array):
        return lax.dynamic_slice_in_dim(array, mine * local, local, 0)

    def grouped(even, odd):
        return jnp.concatenate(
            [even.reshape(-1, half, rows), odd.reshape(-1, half, rows)], axis=-1
        )

    router_probs = grouped(router_probs_of(mid_even), router_probs_of(mid_odd))
    fixed_ids = jnp.stack([plane % near, mine * local])

    def by_group(blocks):
        return jnp.stack([blocks[:half], blocks[half:]], axis=1).reshape(n)

    own_out = routed_own(
        fixed_ids,
        cap,
        near,
        far,
        after(ranks(0)[:, None], cot_chunks[0]),
        local_probs(router_probs)[:, None],
        [mid_even[None], mid_odd[None]],
        [cot_even[None], cot_odd[None]],
        expert_gate,
        expert_up,
        expert_down,
        router_probs.transpose(1, 0, 2),
        router_t,
    )
    hidden_own, gate_lin_own, up_lin_own, x_own_cut, d_own_cut = own_out[:5]
    moe_even, moe_odd, dmid_even, dmid_odd, dlogits = own_out[5:]
    dmid = scatter_sum(dmid_even, after(dmid_odd, cot_chunks[1]))
    scaled = after(dmid, cot_chunks[2]) * gain_mid
    cot_chunks += [swap(after(chunk, dmid), "expert", 1) for chunk in cot_chunks]
    dlogits = dlogits.transpose(1, 0, 2).astype(bfloat)
    router_grad = dot32(
        dlogits[:, :, :rows].reshape(experts, -1), mid_even.reshape(-1, model), ((1,), (0,))
    ) + dot32(dlogits[:, :, rows:].reshape(experts, -1), mid_odd.reshape(-1, model), ((1,), (0,)))

    all_probs = router_probs_of(mid_planes).reshape(experts, near, n, rows)
    all_probs = jnp.take(local_probs(all_probs), by_group(slots), axis=2)

    def add_sequences(masks, more, *earlier):
        planes = [plane % near ^ kd for kd in masks]
        tables = [
            lax.dynamic_index_in_dim(all_probs, there, 1, keepdims=False).reshape(local, half, block)
            for there in planes
        ]
        return routed_others(
            jnp.concatenate([plane[None] % near, jnp.full((1,), len(masks), jnp.int32), jnp.stack(planes), by_group(slots)]),
            cap,
            near,
            far,
            after(jnp.stack([ranks(kd) for kd in masks], axis=1), *earlier),
            jnp.stack(tables, axis=1),
            mid_planes,
            cot_chunks,
            expert_gate,
            expert_up,
            expert_down,
            more,
        )

    mid_grad = jnp.sum(dmid * (residual * rs_mid), axis=0)
    inner = jnp.mean(scaled * residual, axis=-1, keepdims=True)
    dres = cotangent.astype(single) + rs_mid * (scaled - residual * (rs_mid * rs_mid * inner))
    dres_chips = gather_chips(dres.astype(bfloat))
    dres_even = jnp.stack(dres_chips)
    dres_odd = swap(dres_even, "expert", 1).reshape(-1, model)
    dres_even = dres_even.reshape(-1, model)
    datt_b = jnp.concatenate(
        [dot32(part, wo, ((1,), (1,))) for part in (dres_even, dres_odd)], axis=0
    )
    datt_b = after(datt_b, *cot_chunks[3:half]).astype(bfloat)

    moe = scatter_sum(after(moe_even, dres_odd), after(moe_odd, dres_odd))
    output = (residual + moe).astype(bfloat)

    dq_rot, dk_rot, dv = [], [], []
    for prob, da, q_h, k_h, v_h in zip(
        probs, per_head(datt_b), per_head(query_b), per_head(key_b), per_head(value_b)
    ):
        dprob = dot32(da, v_h, ((1,), (1,)))
        dsum = jnp.sum(prob * dprob, axis=-1, keepdims=True)
        dscores = (prob * (dprob - dsum)).astype(bfloat)
        dv.append(dot32(prob.astype(bfloat), da, ((0,), (0,))))
        dq_rot.append(dot32(dscores, k_h, ((1,), (0,))) * scale)
        dk_rot.append(dot32(dscores, q_h, ((0,), (0,))) * scale)
    dq_un = rotate(jnp.concatenate(dq_rot, axis=-1), True)
    dk_un = rotate(jnp.concatenate(dk_rot, axis=-1), True)
    inners = jnp.stack(
        [
            jnp.sum(dq_un * own_gain_q * query_raw, axis=-1),
            jnp.sum(dk_un * own_gain_k * key_raw, axis=-1),
        ]
    )
    inners = after(inners, moe, mid_planes)
    inners = sum_rows_over_expert(inners.reshape(2, n, rows)).reshape(2, length)
    query_gain_grad = jnp.sum(dq_un * query_raw * rs_q, axis=0)
    key_gain_grad = jnp.sum(dk_un * key_raw * rs_k, axis=0)
    dq_b = (
        rs_q * dq_un * own_gain_q - query_raw * (rs_q**3 / model * inners[0][:, None])
    ).astype(bfloat)
    dk_b = (
        rs_k * dk_un * own_gain_k - key_raw * (rs_k**3 / model * inners[1][:, None])
    ).astype(bfloat)
    dv_b = jnp.concatenate(dv, axis=-1).astype(bfloat)
    dnormed_part = [
            (
                dot32(dq_part, w_q, ((1,), (1,)))
                + dot32(dk_part, w_k, ((1,), (1,)))
                + dot32(dv_part, w_v, ((1,), (1,)))
            ).astype(bfloat)
            for dq_part, dk_part, dv_part in zip(halves(dq_b), halves(dk_b), halves(dv_b))
    ]
    dnormed = scatter_sum(*dnormed_part)
    dnormed_part = dnormed_part[0]

    def planes_sum(partials):
        return lax.psum_scatter(
            jnp.stack(partials).astype(bfloat), "dp", scatter_dimension=1, tiled=True
        )

    output_part = dot32(dres_even, attended[: length // 2], ((0,), (0,))) + dot32(
        dres_odd, attended[length // 2 :], ((0,), (0,))
    )
    early = planes_sum([dot32(normed_b, dv_b, ((0,), (0,))), after(output_part, mid_planes)])
    late = planes_sum([dot32(normed_b, part, ((0,), (0,))) for part in (dq_b, dk_b)])
    summed = jnp.concatenate([early[:1], late], axis=0)
    moved = lax.all_to_all(
        summed.reshape(3, n, shard, width).transpose(1, 0, 2, 3),
        "expert",
        split_axis=0,
        concat_axis=0,
        tiled=True,
    )
    moved = moved.transpose(1, 2, 0, 3).reshape(3, shard, model).astype(single)
    value_grad, query_grad, key_grad = moved[0], moved[1], moved[2]
    output_sum = early[1].reshape(model // m, m, shard).transpose(1, 2, 0)
    pieces_here = []
    for turn in range(m):
        pairs = [(((s % m + turn) % m) * n + s // m, s) for s in range(m * n)]
        sent = lax.dynamic_index_in_dim(output_sum, (plane - turn) % m, 0, keepdims=False)
        pieces_here.append(lax.ppermute(sent, ("dp", "expert"), pairs))
    shard_at = (plane * n + mine) % m
    output_grad = jnp.take(
        jnp.stack(pieces_here), (jnp.arange(m, dtype=jnp.int32) - shard_at) % m, axis=0
    )
    output_grad = output_grad.transpose(1, 0, 2).reshape(shard, model).astype(single)

    rs_own = rs_in[:rows]
    scaled_in = dnormed * gain_in
    inner_in = jnp.mean(scaled_in * x_own, axis=-1, keepdims=True)
    input_grad = dres + rs_own * (scaled_in - x_own * (rs_own * rs_own * inner_in))
    in_grad = jnp.sum(dnormed * x_own * rs_own, axis=0)

    def placed(part):
        return lax.dynamic_update_slice(jnp.zeros((model,), single), part, (mine * width,))

    small_grad = jnp.concatenate(
        [
            in_grad[None],
            placed(query_gain_grad)[None],
            placed(key_gain_grad)[None],
            mid_grad[None],
            router_grad,
        ],
        axis=0,
    ).reshape(kinds, m, n, shard)
    small_grad = jnp.take(small_grad, jnp.arange(n, dtype=jnp.int32) ^ mine, axis=2)
    small_pair = small_grad[:, :, 0::2] + swap(small_grad[:, :, 1::2], "expert", 1)
    small_sum = small_pair[:, :, 0]
    for k in range(2, n, 2):
        small_sum = small_sum + swap(small_pair[:, :, k // 2], "expert", k)
    small_sum = jnp.take(small_sum, jnp.arange(m, dtype=jnp.int32) ^ plane, axis=1)
    total = small_sum[:, 0]
    for k in range(1, m):
        total = total + swap(small_sum[:, k], "dp", k)

    weight_sums = add_sequences(list(range(1, near - 1)), None, dnormed_part)
    own_rows = [x_own_cut, d_own_cut, hidden_own, gate_lin_own, up_lin_own]
    weight_sums = add_sequences([near - 1], own_rows + list(weight_sums), dnormed, summed, moved, total)
    gate_grad, up_grad, down_grad = weight_sums
    span = model // m

    def sum_over_far(parts):
        if far == 1:
            return parts[0]
        parts = jnp.take(parts, jnp.arange(far, dtype=jnp.int32) ^ (plane // near), axis=0)
        total = parts[0]
        for k in range(1, far):
            total = total + swap(parts[k].astype(bfloat), "dp", k * near).astype(single)
        return total

    units = expert_gate.shape[2]
    gate_grad, up_grad = [
        sum_over_far(grad.reshape(local, far, span, units).transpose(1, 0, 2, 3))
        for grad in (gate_grad, up_grad)
    ]
    down_grad = sum_over_far(down_grad.reshape(local, units, far, span).transpose(2, 0, 1, 3))

    return (
        output,
        input_grad,
        query_grad,
        key_grad,
        value_grad,
        output_grad,
        total[0],
        total[1],
        total[2],
        total[3],
        total[4:].T,
        gate_grad,
        up_grad,
        down_grad,
    )


def solution(mesh):
    both = ("dp", "expert")
    in_specs = (
        [P(both, None)] * 5
        + [P(both)] * 4
        + [P(both, None)]
        + [P("expert", None, None)] * 3
        + [P(both, None), P(both), P(both, None)]
    )
    out_specs = (
        [P(both, None)] * 6
        + [P(both)] * 4
        + [P(both, None)]
        + [P("expert", "dp", None)] * 2
        + [P("expert", None, "dp")]
    )
    return jax.shard_map(
        per_device,
        mesh=mesh,
        in_specs=tuple(in_specs),
        out_specs=tuple(out_specs),
        check_vma=False,
    )
```

time: 1180 us -> 793 us (0.67)
  matrix products: 295 us -> 62.2 us
  local copies, waits for them, and re-layouts: 275 us -> 73.7 us
  Pallas kernels: 0 us -> 152 us
  waiting for transfers between devices: 303 us -> 230 us
  other arithmetic: 151 us -> 101 us
  starting transfers between devices: 113 us -> 134 us
  blocking collectives: 17.7 us -> 0 us
  between operations: 16.9 us -> 31.6 us
    dot_general x19 -> x4, matrix products: 199 us -> 3.01 us  [ranks(): lax.dot_general(hit.astype(bfloat), upper, (((2,), (0,)), ((), ())), pref...]
    pallas_call x0 -> x3, Pallas kernels: none -> 152 us  [the longest x2 94.3 us: routed_others(): pl.pallas_call(functools.partial(others_kernel, 1, len(cot), groups, bloc...]
    ppermute x100 -> x62, waiting for transfers between devices: 295 us -> 212 us  [swap(): return lax.ppermute(values, axis, [(i, i ^ mask) for i in range(count)])]
    concatenate x13 -> x8, local copies, waits for them, and re-layouts: 83.3 us -> 2.37 us  [the longest x4 1.57 us: reorder(): jnp.concatenate([array[:, order.index(s ^ mask)][:, None] for s in order]...]
    concatenate x4 -> x5, other arithmetic: 79.8 us -> 1.75 us  [the longest x1 1.11 us: per_device(): summed = jnp.concatenate([early[:1], late], axis=0)]
    unnamed x354 -> x357, local copies, waits for them, and re-layouts: 91.8 us -> 18.7 us
    dot_general x29 -> x35, matrix products: 96.6 us -> 59.2 us  [dot32(): lax.dot_general(left, right, (dims, ((), ())), preferred_element_type=sin...]
    add x2 -> x24, other arithmetic: 0.05 us -> 28.6 us  [the longest x21 25.7 us: after(): values = values + zero.astype(values.dtype)]
  transfers between devices with their start and end apart: 111 -> 79, of which waited for: 34 -> 28; matrix products, arithmetic and copies ran while one was open for 47% -> 27% of each run, Pallas kernels for 0% -> 14%
where the time goes in v2:
time: 793 us; the launch traced here: 785 us
  waiting for transfers between devices  230 us (29%)
  Pallas kernels  152 us (19%)
  starting transfers between devices  134 us (17%)
  other arithmetic  101 us (13%)
  local copies, waits for them, and re-layouts  73.7 us (9%)
  matrix products  62.2 us (8%)
  between operations  31.6 us (4%)
    ppermute x62, waiting for transfers between devices, swap(): return lax.ppermute(values, axis, [(i, i ^ mask) for i in range(count)])  212 us
    ppermute x62, starting transfers between devices, swap(): return lax.ppermute(values, axis, [(i, i ^ mask) for i in range(count)])  102 us
    pallas_call x2, Pallas kernels, routed_others(): pl.pallas_call(functools.partial(others_kernel, 1, len(cot), groups, bloc...  94.3 us
    dot_general x35, matrix products, dot32(): lax.dot_general(left, right, (dims, ((), ())), preferred_element_type=sin...  59.2 us
    pallas_call x1, Pallas kernels, routed_own(): pl.pallas_call(functools.partial(own_kernel, groups, block, cap, near, fa...  57.6 us
    add x21, other arithmetic, after(): values = values + zero.astype(values.dtype)  25.7 us
    slice x21, local copies, waits for them, and re-layouts, after(): zero = jnp.minimum(jnp.abs(result[(-1,) * result.ndim]), 0)  20.6 us
    unnamed x357, local copies, waits for them, and re-layouts  18.7 us
  transfers between devices with their start and end apart: 79, of which 28 were waited for; matrix products, arithmetic and copies ran while one was open for 27% of the time, Pallas kernels for 14%

profile of v2, /device:TPU:0, one launch (start us, length us, event | category | flops | bytes accessed | tf_op | source)
XLA Modules:
  0.0 785.2 jit_solution(5001454205054181917)
XLA Ops:
  38.1 10.0 %collective-permute-done.10 = bf16[1,2,512,256]{3,2,1,0:T(8,128)(2,1)S(1)} collective-permute-done((bf16[1,2,512,256]{3,2,1,0:T(8,128)(2,1)S(1)}, bf16[1,2,512,256]{3,2,1,0:T(8,128)(2,1)S(1)}, u32[]{:S(2)}, u32[]{:S(2)}) %collective-permute-start.10) | collective-permute-done | bytes 524320 | tf_op jit(solution)/shard_map/ppermute | solution.py:31
  48.1 11.9 %collective-permute-start.1 = (bf16[19,128]{1,0:T(8,128)(2,1)S(1)}, bf16[19,128]{1,0:T(8,128)(2,1)S(1)}, u32[]{:S(2)}, u32[]{:S(2)}) collective-permute-start(bf16[19,128]{1,0:T(8,128)(2,1)S(1)} %maximum_add_fusion.9), channel_id=1, source_target_pairs={{0,16},{8,24},{16,0},{24,8},{1,17},{9,25},{17,1},{25,9},{2,18},{10... | collective-permute-start | bytes 14600 | tf_op jit(solution)/shard_map/ppermute | solution.py:31
  74.2 17.6 %collective-permute-done.16 = bf16[2,2,512,256]{3,2,1,0:T(8,128)(2,1)} collective-permute-done((bf16[2,2,512,256]{3,2,1,0:T(8,128)(2,1)}, bf16[2,2,512,256]{3,2,1,0:T(8,128)(2,1)}, u32[]{:S(2)}, u32[]{:S(2)}) %collective-permute-start.16) | collective-permute-done | bytes 1048608 | tf_op jit(solution)/shard_map/ppermute | solution.py:31
  104.3 11.0 %collective-permute-done.14 = bf16[128,2048]{1,0:T(8,128)(2,1)} collective-permute-done((bf16[128,2048]{1,0:T(8,128)(2,1)}, bf16[128,2048]{1,0:T(8,128)(2,1)}, u32[]{:S(2)}, u32[]{:S(2)}) %collective-permute-start.14) | collective-permute-done | bytes 524320 | tf_op jit(solution)/shard_map/ppermute | solution.py:31
  115.4 10.0 %collective-permute-done.13 = bf16[128,2048]{1,0:T(8,128)(2,1)} collective-permute-done((bf16[128,2048]{1,0:T(8,128)(2,1)}, bf16[128,2048]{1,0:T(8,128)(2,1)}, u32[]{:S(2)}, u32[]{:S(2)}) %collective-permute-start.13) | collective-permute-done | bytes 524320 | tf_op jit(solution)/shard_map/ppermute | solution.py:31
  174.7 16.4 %collective-permute-start.22 = (bf16[2,1,512,256]{3,2,1,0:T(8,128)(2,1)S(1)}, bf16[2,1,512,256]{3,2,1,0:T(8,128)(2,1)S(1)}, u32[]{:S(2)}, u32[]{:S(2)}) collective-permute-start(bf16[2,1,512,256]{3,2,1,0:T(8,128)(2,1)S(1)} %pad_maximum_fusion.11), channel_id=1, source_target_pairs={{0,8},{8,0},{16,24},{24,16},{1,9},{9,1},{17,25},{25,17},{2,10},{10... | collective-permute-start | bytes 1572872 | tf_op jit(solution)/shard_map/ppermute | solution.py:31
  191.8 18.3 %collective-permute-done.22 = bf16[2,1,512,256]{3,2,1,0:T(8,128)(2,1)S(1)} collective-permute-done((bf16[2,1,512,256]{3,2,1,0:T(8,128)(2,1)S(1)}, bf16[2,1,512,256]{3,2,1,0:T(8,128)(2,1)S(1)}, u32[]{:S(2)}, u32[]{:S(2)}) %collective-permute-start.22) | collective-permute-done | bytes 524320 | tf_op jit(solution)/shard_map/ppermute | solution.py:31
  241.0 7.0 collective-permute-start.28
  248.0 8.5 %collective-permute-start.30 = (bf16[128,2048]{1,0:T(8,128)(2,1)S(1)}, bf16[128,2048]{1,0:T(8,128)(2,1)S(1)}, u32[]{:S(2)}, u32[]{:S(2)}) collective-permute-start(bf16[128,2048]{1,0:T(8,128)(2,1)S(1)} %get-tuple-element.80), channel_id=1, source_target_pairs={{0,2},{1,3},{2,0},{3,1},{4,6},{5,7},{6,4},{7,5},{8,10},{9,11},{10,... | collective-permute-start | bytes 1572872 | tf_op jit(solution)/shard_map/ppermute | solution.py:31
  260.7 19.0 %collective-permute-done.30 = bf16[128,2048]{1,0:T(8,128)(2,1)S(1)} collective-permute-done((bf16[128,2048]{1,0:T(8,128)(2,1)S(1)}, bf16[128,2048]{1,0:T(8,128)(2,1)S(1)}, u32[]{:S(2)}, u32[]{:S(2)}) %collective-permute-start.30) | collective-permute-done | bytes 524320 | tf_op jit(solution)/shard_map/ppermute | solution.py:31
  287.4 8.2 %collective-permute-done.32 = bf16[128,2048]{1,0:T(8,128)(2,1)S(1)} collective-permute-done((bf16[128,2048]{1,0:T(8,128)(2,1)S(1)}, bf16[128,2048]{1,0:T(8,128)(2,1)S(1)}, u32[]{:S(2)}, u32[]{:S(2)}) %collective-permute-start.32) | collective-permute-done | bytes 524320 | tf_op jit(solution)/shard_map/ppermute | solution.py:31
  298.2 9.8 %collective-permute-done.33 = bf16[128,2048]{1,0:T(8,128)(2,1)S(1)} collective-permute-done((bf16[128,2048]{1,0:T(8,128)(2,1)S(1)}, bf16[128,2048]{1,0:T(8,128)(2,1)S(1)}, u32[]{:S(2)}, u32[]{:S(2)}) %collective-permute-start.33) | collective-permute-done | bytes 524320 | tf_op jit(solution)/shard_map/ppermute | solution.py:31
  333.4 57.6 %routed_own.1 = (bf16[2,576,1024]{2,1,0:T(8,128)(2,1)}, bf16[2,576,1024]{2,1,0:T(8,128)(2,1)}, bf16[2,576,1024]{2,1,0:T(8,128)(2,1)}, bf16[2,576,512]{2,1,0:T(8,...) custom-call(s32[2]{0:T(128)} %pad_add_fusion.1.ids_ref, ...), custom_call_target="tpu_custom_call" | custom-call | flops 28991029248 | bytes 50331648 | tf_op jit(solution)/shard_map/routed_own/pallas_call | solution.py:296
  407.4 6.5 fusion.3
  417.8 13.3 %collective-permute-done.36 = bf16[128,2048]{1,0:T(8,128)(2,1)} collective-permute-done((bf16[128,2048]{1,0:T(8,128)(2,1)}, bf16[128,2048]{1,0:T(8,128)(2,1)}, u32[]{:S(2)}, u32[]{:S(2)}) %collective-permute-start.36) | collective-permute-done | bytes 524320 | tf_op jit(solution)/shard_map/ppermute | solution.py:31
  431.1 22.3 %collective-permute-done.38 = bf16[128,2048]{1,0:T(8,128)(2,1)} collective-permute-done((bf16[128,2048]{1,0:T(8,128)(2,1)}, bf16[128,2048]{1,0:T(8,128)(2,1)}, u32[]{:S(2)}, u32[]{:S(2)}) %collective-permute-start.38) | collective-permute-done | bytes 524320 | tf_op jit(solution)/shard_map/ppermute | solution.py:31
  465.5 9.0 %collective-permute-done.41 = bf16[128,2048]{1,0:T(8,128)(2,1)} collective-permute-done((bf16[128,2048]{1,0:T(8,128)(2,1)}, bf16[128,2048]{1,0:T(8,128)(2,1)}, u32[]{:S(2)}, u32[]{:S(2)}) %collective-permute-start.41) | collective-permute-done | bytes 524320 | tf_op jit(solution)/shard_map/ppermute | solution.py:31
  474.5 9.1 %collective-permute-done.40 = bf16[128,2048]{1,0:T(8,128)(2,1)} collective-permute-done((bf16[128,2048]{1,0:T(8,128)(2,1)}, bf16[128,2048]{1,0:T(8,128)(2,1)}, u32[]{:S(2)}, u32[]{:S(2)}) %collective-permute-start.40) | collective-permute-done | bytes 524320 | tf_op jit(solution)/shard_map/ppermute | solution.py:31
  539.2 10.1 %collective-permute-done.46 = bf16[128,2048]{1,0:T(8,128)(2,1)} collective-permute-done((bf16[128,2048]{1,0:T(8,128)(2,1)}, bf16[128,2048]{1,0:T(8,128)(2,1)}, u32[]{:S(2)}, u32[]{:S(2)}) %collective-permute-start.46) | collective-permute-done | bytes 524320 | tf_op jit(solution)/shard_map/ppermute | solution.py:31
  561.1 10.6 %fusion.220 = (f32[4096]{0:T(1024)S(1)}, f32[16,4096]{1,0:T(8,128)S(1)}) fusion(bf16[16,2048]{1,0:T(8,128)(2,1)S(1)} %copy-done.77, bf16[4096,2048]{1,0:T(8,128)(2,1)} %all-gather.19.cloned.1.call-done), kind=kOutput, calls=%fused_computation.475 | convolution fusion | flops 268496896 | bytes 17121280 | tf_op jit(solution)/shard_map/dot_general | solution.py:19
  603.3 7.9 %collective-permute-done.52 = bf16[128,2048]{1,0:T(8,128)(2,1)} collective-permute-done((bf16[128,2048]{1,0:T(8,128)(2,1)}, bf16[128,2048]{1,0:T(8,128)(2,1)}, u32[]{:S(2)}, u32[]{:S(2)}) %collective-permute-start.52) | collective-permute-done | bytes 524320 | tf_op jit(solution)/shard_map/ppermute | solution.py:31
  611.3 10.5 %collective-permute-done.54 = bf16[128,2048]{1,0:T(8,128)(2,1)} collective-permute-done((bf16[128,2048]{1,0:T(8,128)(2,1)}, bf16[128,2048]{1,0:T(8,128)(2,1)}, u32[]{:S(2)}, u32[]{:S(2)}) %collective-permute-start.54) | collective-permute-done | bytes 524320 | tf_op jit(solution)/shard_map/ppermute | solution.py:31
  630.0 55.9 %routed_others.2 = (f32[2,512,1024]{2,1,0:T(8,128)}, f32[2,512,1024]{2,1,0:T(8,128)}, f32[2,1024,512]{2,1,0:T(8,128)}) custom-call(s32[12]{0:T(128)} %concatenate.174.ids_ref, f32[2,2,4,256]{3,2,1,0:T(4,128)} %copy.437.rank_ref, f32[2,2,4,256]{3,2,1,0:T(4,128)} %pad_maximum_fusion.30.prob_ref, bf16[4,8,128,2048]{3,2,1,0:T(8,128)(2,1)} %bitcast.438, ...), custom_call_target="tpu_custom_call" | custom-call | flops 38654705664 | bytes 67108864 | tf_op jit(solution)/shard_map/routed_others/pallas_call | solution.py:357
  739.7 38.4 %routed_others.3 = (f32[2,512,1024]{2,1,0:T(8,128)}, f32[2,512,1024]{2,1,0:T(8,128)}, f32[2,1024,512]{2,1,0:T(8,128)}) custom-call(s32[11]{0:T(128)} %pad_add_fusion.2.ids_ref, f32[2,1,4,256]{3,2,1,0:T(4,128)} %fusion.21.rank_ref, f32[2,1,4,256]{3,2,1,0:T(4,128)} %stack_reshape.9.prob_ref, ...), custom_call_target="tpu_custom_call", output_to_operand_aliasing={{0}: (20, {}), {1}: (21, {}), {2}: (22, {})} | custom-call | flops 19327352832 | bytes 67108864 | tf_op jit(solution)/shard_map/routed_others/pallas_call | solution.py:357
  (786 shorter events, 354.6 us)
Async XLA Ops:
  15.9 308.4 %all-gather.11.cloned.1.call-start = ((), (), s32[]{:S(2)}) async-start(), calls=%async_computation.6 | async-start | bytes 2621440 | tf_op jit(solution)/shard_map/all_gather | solution.py:487
  18.2 50.5 %collective-permute-start.2 = (bf16[19,128]{1,0:T(8,128)(2,1)S(1)}, bf16[19,128]{1,0:T(8,128)(2,1)S(1)}, u32[]{:S(2)}, u32[]{:S(2)}) collective-permute-start(bf16[19,128]{1,0:T(8,128)(2,1)S(1)} %maximum_add_fusion.9), channel_id=1, source_target_pairs={{0,24},{8,16},{16,8},{24,0},{1,25},{9,17},{17,9},{25,1},{2,26},{10... | collective-permute-start | bytes 14600 | tf_op jit(solution)/shard_map/ppermute | solution.py:31
  30.7 30.5 %collective-permute-start.8 = (bf16[128,2048]{1,0:T(8,128)(2,1)}, bf16[128,2048]{1,0:T(8,128)(2,1)S(1)}, u32[]{:S(2)}, u32[]{:S(2)}) collective-permute-start(bf16[128,2048]{1,0:T(8,128)(2,1)} %broadcast_add_fusion.13), channel_id=1, source_target_pairs={{0,4},{1,5},{2,6},{3,7},{4,0},{5,1},{6,2},{7,3},{8,12},{9,13},{10,... | collective-permute-start | bytes 1572872 | tf_op jit(solution)/shard_map/ppermute | solution.py:31
  31.2 30.1 %collective-permute-start.7 = (bf16[128,2048]{1,0:T(8,128)(2,1)}, bf16[128,2048]{1,0:T(8,128)(2,1)S(1)}, u32[]{:S(2)}, u32[]{:S(2)}) collective-permute-start(bf16[128,2048]{1,0:T(8,128)(2,1)} %broadcast_add_fusion.13), channel_id=1, source_target_pairs={{0,2},{1,3},{2,0},{3,1},{4,6},{5,7},{6,4},{7,5},{8,10},{9,11},{10,... | collective-permute-start | bytes 1572872 | tf_op jit(solution)/shard_map/ppermute | solution.py:31
  31.8 29.5 %collective-permute-start.9 = (bf16[128,2048]{1,0:T(8,128)(2,1)}, bf16[128,2048]{1,0:T(8,128)(2,1)}, u32[]{:S(2)}, u32[]{:S(2)}) collective-permute-start(bf16[128,2048]{1,0:T(8,128)(2,1)} %broadcast_add_fusion.13), channel_id=1, source_target_pairs={{0,6},{1,7},{2,4},{3,5},{4,2},{5,3},{6,0},{7,1},{8,14},{9,15},{10,... | collective-permute-start | bytes 1572872 | tf_op jit(solution)/shard_map/ppermute | solution.py:31
  63.9 32.4 %collective-permute-start.11 = (bf16[4,128,2048]{2,1,0:T(8,128)(2,1)S(1)}, bf16[4,128,2048]{2,1,0:T(8,128)(2,1)}, u32[]{:S(2)}, u32[]{:S(2)}) collective-permute-start(bf16[4,128,2048]{2,1,0:T(8,128)(2,1)S(1)} %maximum_add_fusion), channel_id=1, source_target_pairs={{0,1},{1,0},{2,3},{3,2},{4,5},{5,4},{6,7},{7,6},{8,9},{9,8},{10,11... | collective-permute-start | bytes 6291464 | tf_op jit(solution)/shard_map/ppermute | solution.py:31
  69.4 33.1 %collective-permute-start.5 = (bf16[4,19,128]{2,0,1:T(4,128)(2,1)S(1)}, bf16[4,19,128]{2,0,1:T(4,128)(2,1)S(1)}, u32[]{:S(2)}, u32[]{:S(2)}) collective-permute-start(bf16[4,19,128]{2,0,1:T(4,128)(2,1)S(1)} %get-tuple-element.67), channel_id=1, source_target_pairs={{0,6},{1,7},{2,4},{3,5},{4,2},{5,3},{6,0},{7,1},{8,14},{9,15},{10,... | collective-permute-start | bytes 58376 | tf_op jit(solution)/shard_map/ppermute | solution.py:31
  71.0 32.0 %collective-permute-start.4 = (bf16[4,19,128]{2,0,1:T(4,128)(2,1)S(1)}, bf16[4,19,128]{2,0,1:T(4,128)(2,1)S(1)}, u32[]{:S(2)}, u32[]{:S(2)}) collective-permute-start(bf16[4,19,128]{2,0,1:T(4,128)(2,1)S(1)} %get-tuple-element.67), channel_id=1, source_target_pairs={{0,4},{1,5},{2,6},{3,7},{4,0},{5,1},{6,2},{7,3},{8,12},{9,13},{10,... | collective-permute-start | bytes 58376 | tf_op jit(solution)/shard_map/ppermute | solution.py:31
  72.7 30.3 %collective-permute-start.3 = (bf16[4,19,128]{2,0,1:T(4,128)(2,1)S(1)}, bf16[4,19,128]{2,0,1:T(4,128)(2,1)S(1)}, u32[]{:S(2)}, u32[]{:S(2)}) collective-permute-start(bf16[4,19,128]{2,0,1:T(4,128)(2,1)S(1)} %get-tuple-element.67), channel_id=1, source_target_pairs={{0,2},{1,3},{2,0},{3,1},{4,6},{5,7},{6,4},{7,5},{8,10},{9,11},{10,... | collective-permute-start | bytes 58376 | tf_op jit(solution)/shard_map/ppermute | solution.py:31
  102.5 224.3 %all-gather.13.cloned.1.call-start = ((), (), s32[]{:S(2)}) async-start(), calls=%async_computation.7 | async-start | bytes 2621440 | tf_op jit(solution)/shard_map/all_gather | solution.py:487
  144.1 269.9 %all-gather.17.cloned.1.call-start = ((), (), s32[]{:S(2)}) async-start(), calls=%async_computation.9 | async-start | bytes 2621440 | tf_op jit(solution)/shard_map/all_gather | solution.py:487
  174.7 35.4 %collective-permute-start.22 = (bf16[2,1,512,256]{3,2,1,0:T(8,128)(2,1)S(1)}, bf16[2,1,512,256]{3,2,1,0:T(8,128)(2,1)S(1)}, u32[]{:S(2)}, u32[]{:S(2)}) collective-permute-start(bf16[2,1,512,256]{3,2,1,0:T(8,128)(2,1)S(1)} %pad_maximum_fusion.11), channel_id=1, source_target_pairs={{0,8},{8,0},{16,24},{24,16},{1,9},{9,1},{17,25},{25,17},{2,10},{10... | collective-permute-start | bytes 1572872 | tf_op jit(solution)/shard_map/ppermute | solution.py:31
  236.8 179.0 %all-gather.15.cloned.1.call-start = ((), (), s32[]{:S(2)}) async-start(), calls=%async_computation.8 | async-start | bytes 2621440 | tf_op jit(solution)/shard_map/all_gather | solution.py:487
  248.0 31.7 %collective-permute-start.30 = (bf16[128,2048]{1,0:T(8,128)(2,1)S(1)}, bf16[128,2048]{1,0:T(8,128)(2,1)S(1)}, u32[]{:S(2)}, u32[]{:S(2)}) collective-permute-start(bf16[128,2048]{1,0:T(8,128)(2,1)S(1)} %get-tuple-element.80), channel_id=1, source_target_pairs={{0,2},{1,3},{2,0},{3,1},{4,6},{5,7},{6,4},{7,5},{8,10},{9,11},{10,... | collective-permute-start | bytes 1572872 | tf_op jit(solution)/shard_map/ppermute | solution.py:31
  287.2 266.3 %all-gather.19.cloned.1.call-start = ((), (), s32[]{:S(2)}) async-start(), calls=%async_computation.10 | async-start | bytes 17301504 | tf_op jit(solution)/shard_map/all_gather | solution.py:418
  318.3 384.3 %reduce-scatter.3.cloned.1.call-start = ((), (), s32[]{:S(2)}) async-start(), calls=%async_computation.4 | async-start | bytes 2621440 | tf_op jit(solution)/shard_map/reduce_scatter | solution.py:694
  403.9 27.2 %collective-permute-start.36 = (bf16[128,2048]{1,0:T(8,128)(2,1)}, bf16[128,2048]{1,0:T(8,128)(2,1)}, u32[]{:S(2)}, u32[]{:S(2)}) collective-permute-start(bf16[128,2048]{1,0:T(8,128)(2,1)} %get-tuple-element.76), channel_id=1, source_target_pairs={{0,6},{1,7},{2,4},{3,5},{4,2},{5,3},{6,0},{7,1},{8,14},{9,15},{10,... | collective-permute-start | bytes 1572872 | tf_op jit(solution)/shard_map/ppermute | solution.py:31
  404.9 48.6 %collective-permute-start.38 = (bf16[128,2048]{1,0:T(8,128)(2,1)}, bf16[128,2048]{1,0:T(8,128)(2,1)}, u32[]{:S(2)}, u32[]{:S(2)}) collective-permute-start(bf16[128,2048]{1,0:T(8,128)(2,1)} %get-tuple-element.77), channel_id=1, source_target_pairs={{0,2},{1,3},{2,0},{3,1},{4,6},{5,7},{6,4},{7,5},{8,10},{9,11},{10,... | collective-permute-start | bytes 1572872 | tf_op jit(solution)/shard_map/ppermute | solution.py:31
  406.9 46.6 %collective-permute-start.37 = (bf16[128,2048]{1,0:T(8,128)(2,1)}, bf16[128,2048]{1,0:T(8,128)(2,1)}, u32[]{:S(2)}, u32[]{:S(2)}) collective-permute-start(bf16[128,2048]{1,0:T(8,128)(2,1)} %get-tuple-element.78), channel_id=1, source_target_pairs={{0,4},{1,5},{2,6},{3,7},{4,0},{5,1},{6,2},{7,3},{8,12},{9,13},{10,... | collective-permute-start | bytes 1572872 | tf_op jit(solution)/shard_map/ppermute | solution.py:31
  488.6 141.4 %collective-permute-start.66 = (bf16[4,128,2048]{2,1,0:T(8,128)(2,1)}, bf16[4,128,2048]{2,1,0:T(8,128)(2,1)}, u32[]{:S(2)}, u32[]{:S(2)}) collective-permute-start(bf16[4,128,2048]{2,1,0:T(8,128)(2,1)} %broadcast_add_fusion.3), channel_id=1, source_target_pairs={{0,1},{1,0},{2,3},{3,2},{4,5},{5,4},{6,7},{7,6},{8,9},{9,8},{10,11... | collective-permute-start | bytes 6291464 | tf_op jit(solution)/shard_map/ppermute | solution.py:31
  490.8 139.2 %collective-permute-start.69 = (bf16[4,128,2048]{2,1,0:T(8,128)(2,1)}, bf16[4,128,2048]{2,1,0:T(8,128)(2,1)}, u32[]{:S(2)}, u32[]{:S(2)}) collective-permute-start(bf16[4,128,2048]{2,1,0:T(8,128)(2,1)} %broadcast_add_fusion), channel_id=1, source_target_pairs={{0,1},{1,0},{2,3},{3,2},{4,5},{5,4},{6,7},{7,6},{8,9},{9,8},{10,11... | collective-permute-start | bytes 6291464 | tf_op jit(solution)/shard_map/ppermute | solution.py:31
  559.6 144.3 %reduce-scatter.5.cloned.1.call-start = ((), (), s32[]{:S(2)}) async-start(), calls=%async_computation.5 | async-start | bytes 2621440 | tf_op jit(solution)/shard_map/reduce_scatter | solution.py:694
  629.5 56.5 %collective-permute-start.59 = (f32[20,4,4,64]{3,1,0,2:T(4,128)S(1)}, f32[20,4,4,64]{3,1,0,2:T(4,128)S(1)}, u32[]{:S(2)}, u32[]{:S(2)}) collective-permute-start(f32[20,4,4,64]{3,1,0,2:T(4,128)S(1)} %slice.795), channel_id=1, source_target_pairs={{0,1},{1,0},{2,3},{3,2},{4,5},{5,4},{6,7},{7,6},{8,9},{9,8},{10,11... | collective-permute-start | bytes 245768 | tf_op jit(solution)/shard_map/ppermute | solution.py:31
  706.0 28.5 %all-to-all-start.1 = ((bf16[8,3,64,256]{3,2,1,0:T(8,128)(2,1)}), bf16[8,3,64,256]{3,2,1,0:T(8,128)(2,1)S(1)}, u32[]{:S(2)}, u32[]{:S(2)}) async-start(bf16[8,3,64,256]{3,2,1,0:T(8,128)(2,1)} %bitcast.436), calls=%async_computation.3 | async-start | bytes 1572864 | tf_op jit(solution)/shard_map/all_to_all | solution.py:704
  (225 other events, 2904.8 us)
Sparse Core Ops, SparseCore 0:
  102.7 43.4 all-gather.10
  147.7 60.0 all-gather.12
  237.0 55.4 all-gather.16
  293.9 44.6 all-gather.14
  341.3 136.4 all-gather.18
  559.7 41.0 reduce-scatter.2
  624.1 41.5 reduce-scatter.4

commit v3 on v2

--- a/solution.py
+++ b/solution.py
@@ -29,6 +29,13 @@
 def swap(values, axis, mask):
     count = lax.axis_size(axis)
     return lax.ppermute(values, axis, [(i, i ^ mask) for i in range(count)])
+
+
+def stage(ready, compute):
+    shapes = jax.eval_shape(compute)
+    return lax.cond(
+        ready, compute, lambda: jax.tree.map(lambda a: jnp.zeros(a.shape, a.dtype), shapes)
+    )
 
 
 def slot_order():
@@ -56,6 +63,21 @@
         order = order + [place ^ mask for place in order]
         mask >>= 1
     return held, order
+
+
+def pair_sums(even, odd):
+    half = lax.axis_size("expert") // 2
+    rows = even.shape[0] // half
+    arrived = swap(odd, "expert", 1)
+    parts = [slice(place * rows, (place + 1) * rows) for place in range(half)]
+    return [(even[part].astype(single) + arrived[part].astype(single)).astype(bfloat) for part in parts]
+
+
+def sum_chips(pairs):
+    total = pairs[0].astype(single)
+    for place in range(1, len(pairs)):
+        total = total + swap(pairs[place], "expert", 2 * place).astype(single)
+    return total
 
 
 def scatter_sum(even, odd, with_first=False):
@@ -89,15 +111,11 @@
     return out
 
 
-def rows_of_group(pieces, g, groups, ids_ref):
-    if len(pieces) == 2:
-        return jnp.concatenate([pieces[0][0, g], pieces[1][0, g]], axis=0)
-    if len(pieces) > 2:
-        return jnp.concatenate([pieces[g][0], pieces[groups + g][0]], axis=0)
-    at = 2 + ids_ref[1]
-    return jnp.concatenate(
-        [pieces[0][0, ids_ref[at + 2 * g]], pieces[0][0, ids_ref[at + 2 * g + 1]]], axis=0
-    )
+def rows_of_group(pieces, g, groups):
+    first = len(pieces) // 2
+    share = groups // first
+    at, part = g // share, g % share
+    return jnp.concatenate([pieces[at][0, part], pieces[first + at][0, part]], axis=0)
 
 
 def enter_rows(ids_ref, rank_ref, prob_ref, mid_refs, cot_refs, groups, block, cap, put):
@@ -108,8 +126,8 @@
         gate_col = jnp.sum(
             jnp.where(pick, prob_ref[0, 0, g : g + 1, :], 0.0), axis=1, keepdims=True
         )
-        entered = dot32(pick_b, rows_of_group(mid_refs, g, groups, ids_ref), ((1,), (0,)))
-        cot_row = dot32(pick_b, rows_of_group(cot_refs, g, groups, ids_ref), ((1,), (0,)))
+        entered = dot32(pick_b, rows_of_group(mid_refs, g, groups), ((1,), (0,)))
+        cot_row = dot32(pick_b, rows_of_group(cot_refs, g, groups), ((1,), (0,)))
         put(g, entered.astype(bfloat), (cot_row * gate_col).astype(bfloat))
 
 
@@ -190,7 +208,7 @@
             weighted = (pick_f * prob_ref[0, 0, g : g + 1, :]).astype(bfloat)
             returned = sum_r[g * cap : (g + 1) * cap, :].astype(bfloat)
             cot_row = dot32(
-                pick_b, rows_of_group((cot_even, cot_odd), g, groups, ids_ref), ((1,), (0,))
+                pick_b, rows_of_group((cot_even, cot_odd), g, groups), ((1,), (0,))
             )
             dgate = jnp.sum(cot_row * returned.astype(single), axis=1, keepdims=True)
             dgate = jnp.sum(jnp.where(pick, dgate, 0.0), axis=0, keepdims=True)
@@ -323,7 +341,7 @@
 
 def routed_others(ids, cap, near, far, rank, prob, mid, cot, gate, up, down, more=None):
     local, planes, groups, block = rank.shape
-    model = mid.shape[-1]
+    model = mid[0].shape[-1]
     units = gate.shape[2]
     chunk = min(chunk_units, units)
     span = model // (near * far)
@@ -347,8 +365,8 @@
     tall_grad = pl.BlockSpec((1, chunk, own_cols), lambda e, f, p, s: (e, f, 0))
     lin = pl.BlockSpec((1, height, chunk), lambda e, f, p, s: (e, 0, f))
     cut = pl.BlockSpec((1, height, own_cols), lambda e, f, p, s: (e, 0, 0))
-    in_specs = [table, table] + [rows_spec(piece) for piece in (mid, *cot)] + [wide, wide, tall]
-    args = [rank, prob, mid, *cot, gate, up, down]
+    in_specs = [table, table] + [rows_spec(piece) for piece in (*mid, *cot)] + [wide, wide, tall]
+    args = [rank, prob, *mid, *cot, gate, up, down]
     aliases = {}
     if more is not None:
         in_specs += [cut, cut, lin, lin, lin, wide_grad, wide_grad, tall_grad]
@@ -356,7 +374,7 @@
         aliases = {len(args) - 2: 0, len(args) - 1: 1, len(args): 2}
     return pl.pallas_call(
         functools.partial(
-            others_kernel, 1, len(cot), groups, block, cap, near, far, span, more is not None
+            others_kernel, len(mid), len(cot), groups, block, cap, near, far, span, more is not None
         ),
         grid_spec=pltpu.PrefetchScalarGridSpec(
             num_scalar_prefetch=1,
@@ -412,18 +430,13 @@
     length = rows * n
     near = min(m, 4)
     far = m // near
-    groups = [[g * near * n + i for i in range(near * n)] for g in range(far)] if far > 1 else None
-
-    def gather_near(values):
-        full = lax.all_gather(values, ("dp", "expert"), axis=0, axis_index_groups=groups)
-        return full.reshape((near, n) + values.shape)
-
     half = n // 2
     width = model // n
     heads = width // HEAD
     block = 2 * rows
     mine = lax.axis_index("expert")
     plane = lax.axis_index("dp")
+    ready = routes[0, 0] >= 0
     scale = HEAD ** (-0.5)
     order = slot_order()
     slots = jnp.asarray(order, jnp.int32) ^ mine
@@ -446,10 +459,6 @@
             out.append(full.reshape(model, width))
         return out
 
-    first_rows = swap(parts[None, :2], "dp", m - 1)
-    x_even, x_odd = gather_halves(after(tokens, parts), first_rows)
-    w_q, w_k = all_rows(parts[:2], first_rows)
-    cot_even, cot_odd = gather_halves(after(cotangent, x_odd))
     packed = jnp.concatenate(
         [norm_in[None], norm_query[None], norm_key[None], norm_mid[None], router.T], axis=0
     )
@@ -463,8 +472,16 @@
         axis=0,
     )
     packed = after(packed, parts_out)
-    small = jnp.stack([packed] + [swap(packed, "dp", mask) for mask in range(1, m)])
+    small, places = gather_steps(packed, "dp", m)
+    first_rows = swap(after(parts[None], small), "dp", m - 1)
+    small = jnp.stack([small[places.index(kd)] for kd in range(m)])
     small = jnp.concatenate(gather_halves(small), axis=0)
+    chips = gather_chips(after(jnp.stack([tokens, cotangent]), parts))
+    x_even = after(jnp.stack([piece[0] for piece in chips]), first_rows)
+    x_odd = swap(x_even, "expert", 1)
+    cot_even = jnp.stack([piece[1] for piece in chips])
+    cot_odd = swap(cot_even, "expert", 1)
+    w_q, w_k, w_v = all_rows(parts, first_rows)
     cut = -(-kinds * shard // HEAD)
     gains = jnp.take(small[:, :, :cut], jnp.asarray([order.index(j) for j in range(n)]), axis=0)
     gains = jnp.take(gains, jnp.arange(n, dtype=jnp.int32) ^ mine, axis=0)
@@ -478,32 +495,9 @@
     x = jnp.concatenate([x_even, x_odd], axis=0).reshape(length, model).astype(single)
     rs_in = lax.rsqrt(jnp.mean(x * x, axis=-1, keepdims=True) + eps_norm)
     normed_b = (x * rs_in * gain_in).astype(bfloat)
-    normed_b = after(normed_b, cot_odd)
-    query_raw = dot32(normed_b, w_q, ((1,), (0,)))
-    key_raw = dot32(normed_b, w_k, ((1,), (0,)))
-    (w_v,) = all_rows(after(parts[2:], w_k, cot_odd))
+
     near_groups = [[g * near + i for i in range(near)] for g in range(far)] if far > 1 else None
-    cot_chunks = [
-        lax.all_gather(after(cot_even[place], w_k), "dp", axis=0, axis_index_groups=near_groups)
-        for place in range(half)
-    ]
-    own_shards = []
-    send = after(attn_output, w_v)
-    for turn in range(m):
-        pairs = [(s, ((s % m + turn) % m) * n + s // m) for s in range(m * n)]
-        own_shards.append(lax.ppermute(send, ("dp", "expert"), pairs))
-    wo = jnp.zeros((m, shard, model), bfloat)
-    for turn in range(m):
-        wo = lax.dynamic_update_slice(
-            wo, own_shards[turn][None], ((plane - turn) % m, jnp.int32(0), jnp.int32(0))
-        )
-    wo = wo.reshape(width, model)
-
-    squares = jnp.stack([jnp.sum(query_raw**2, axis=-1), jnp.sum(key_raw**2, axis=-1)])
-    squares = sum_rows_over_expert(squares.reshape(2, n, rows)).reshape(2, length)
-    rs_q = lax.rsqrt(squares[0] / model + eps_norm)[:, None]
-    rs_k = lax.rsqrt(squares[1] / model + eps_norm)[:, None]
-    value_b = dot32(normed_b, w_v, ((1,), (0,))).astype(bfloat)
+    cot_planes = lax.all_gather(after(cot_even, w_v), "dp", axis=0, axis_index_groups=near_groups)
 
     place = (slots[:, None] * rows + jnp.arange(rows, dtype=jnp.int32)[None, :]).reshape(length)
     turn_half = HEAD // 2
@@ -523,40 +517,11 @@
 
     own_gain_q = lax.dynamic_slice_in_dim(gain_query, mine * width, width)
     own_gain_k = lax.dynamic_slice_in_dim(gain_key, mine * width, width)
-    query_b = rotate(query_raw * rs_q * own_gain_q, False).astype(bfloat)
-    key_b = rotate(key_raw * rs_k * own_gain_k, False).astype(bfloat)
-
     def per_head(array):
         return [array[:, h * HEAD : (h + 1) * HEAD] for h in range(heads)]
 
-    allowed = (place[None, :] <= place[:, None]) | (
-        (piece_row[:, None] == piece_row[None, :]) & (piece_row[:, None] > 0)
-    )
-    probs = []
-    mixed = []
-    for q_h, k_h, v_h in zip(per_head(query_b), per_head(key_b), per_head(value_b)):
-        scores = jnp.where(allowed, dot32(q_h, k_h, ((1,), (1,))) * scale, -1e30)
-        exponent = jnp.exp(scores - jnp.max(scores, axis=-1, keepdims=True))
-        prob = exponent / jnp.sum(exponent, axis=-1, keepdims=True)
-        probs.append(prob)
-        mixed.append(dot32(prob.astype(bfloat), v_h, ((1,), (0,))))
-    attended = jnp.concatenate(mixed, axis=-1).astype(bfloat)
-
     def halves(array):
         return array[: length // 2], array[length // 2 :]
-
-    projected = [dot32(part, wo, ((1,), (0,))).astype(bfloat) for part in halves(attended)]
-    x_own = tokens.astype(single)
-    residual = x_own + scatter_sum(*projected)
-    rs_mid = lax.rsqrt(jnp.mean(residual * residual, axis=-1, keepdims=True) + eps_norm)
-    mid = (residual * rs_mid * gain_mid).astype(bfloat)
-    mid_even, mid_odd = gather_halves(mid)
-    mid_planes = gather_near(after(mid, mid_odd))
-
-    def router_probs_of(mid_rows):
-        logits = dot32(router_t, mid_rows.reshape(-1, model), ((1,), (1,)))
-        exponent = jnp.exp(logits - jnp.max(logits, axis=0, keepdims=True))
-        return exponent / jnp.sum(exponent, axis=0, keepdims=True)
 
     upper = (
         jnp.arange(block, dtype=jnp.int32)[:, None] <= jnp.arange(block, dtype=jnp.int32)[None, :]
@@ -572,6 +537,64 @@
         )
         return jnp.where(hit, rank, 0.0)
 
+    own_ranks = after(ranks(0)[:, None], cot_odd)
+
+    x_own = tokens.astype(single)
+
+    def forward():
+        query_raw = dot32(normed_b, w_q, ((1,), (0,)))
+        key_raw = dot32(normed_b, w_k, ((1,), (0,)))
+        own_shards = []
+        send = attn_output
+        for turn in range(m):
+            pairs = [(s, ((s % m + turn) % m) * n + s // m) for s in range(m * n)]
+            own_shards.append(lax.ppermute(send, ("dp", "expert"), pairs))
+        wo = jnp.zeros((m, shard, model), bfloat)
+        for turn in range(m):
+            wo = lax.dynamic_update_slice(
+                wo, own_shards[turn][None], ((plane - turn) % m, jnp.int32(0), jnp.int32(0))
+            )
+        wo = wo.reshape(width, model)
+
+        squares = jnp.stack([jnp.sum(query_raw**2, axis=-1), jnp.sum(key_raw**2, axis=-1)])
+        squares = sum_rows_over_expert(squares.reshape(2, n, rows)).reshape(2, length)
+        rs_q = lax.rsqrt(squares[0] / model + eps_norm)[:, None]
+        rs_k = lax.rsqrt(squares[1] / model + eps_norm)[:, None]
+        value_b = dot32(normed_b, w_v, ((1,), (0,))).astype(bfloat)
+
+        query_b = rotate(query_raw * rs_q * own_gain_q, False).astype(bfloat)
+        key_b = rotate(key_raw * rs_k * own_gain_k, False).astype(bfloat)
+
+        allowed = (place[None, :] <= place[:, None]) | (
+            (piece_row[:, None] == piece_row[None, :]) & (piece_row[:, None] > 0)
+        )
+        probs = []
+        mixed = []
+        for q_h, k_h, v_h in zip(per_head(query_b), per_head(key_b), per_head(value_b)):
+            scores = jnp.where(allowed, dot32(q_h, k_h, ((1,), (1,))) * scale, -1e30)
+            exponent = jnp.exp(scores - jnp.max(scores, axis=-1, keepdims=True))
+            prob = exponent / jnp.sum(exponent, axis=-1, keepdims=True)
+            probs.append(prob)
+            mixed.append(dot32(prob.astype(bfloat), v_h, ((1,), (0,))))
+        attended = jnp.concatenate(mixed, axis=-1).astype(bfloat)
+
+        projected = [dot32(part, wo, ((1,), (0,))).astype(bfloat) for part in halves(attended)]
+        residual = x_own + scatter_sum(*projected)
+        rs_mid = lax.rsqrt(jnp.mean(residual * residual, axis=-1, keepdims=True) + eps_norm)
+        mid = after(residual * rs_mid * gain_mid, own_ranks).astype(bfloat)
+        mid_even, mid_odd = gather_halves(mid)
+        kept = (query_raw, key_raw, rs_q, rs_k, query_b, key_b, value_b, wo)
+        return kept, probs, attended, residual, rs_mid, mid_even, mid_odd
+
+    kept, probs, attended, residual, rs_mid, mid_even, mid_odd = stage(ready, forward)
+    query_raw, key_raw, rs_q, rs_k, query_b, key_b, value_b, wo = kept
+    mid_planes = lax.all_gather(after(mid_even, cot_planes), "dp", axis=0, axis_index_groups=near_groups)
+
+    def router_probs_of(mid_rows):
+        logits = dot32(router_t, mid_rows.reshape(-1, model), ((1,), (1,)))
+        exponent = jnp.exp(logits - jnp.max(logits, axis=0, keepdims=True))
+        return exponent / jnp.sum(exponent, axis=0, keepdims=True)
+
     def local_probs(array):
         return lax.dynamic_slice_in_dim(array, mine * local, local, 0)
 
@@ -586,123 +609,158 @@
     def by_group(blocks):
         return jnp.stack([blocks[:half], blocks[half:]], axis=1).reshape(n)
 
-    own_out = routed_own(
-        fixed_ids,
-        cap,
-        near,
-        far,
-        after(ranks(0)[:, None], cot_chunks[0]),
-        local_probs(router_probs)[:, None],
-        [mid_even[None], mid_odd[None]],
-        [cot_even[None], cot_odd[None]],
-        expert_gate,
-        expert_up,
-        expert_down,
-        router_probs.transpose(1, 0, 2),
-        router_t,
-    )
+    def backward():
+        own_out = routed_own(
+            fixed_ids,
+            cap,
+            near,
+            far,
+            own_ranks,
+            local_probs(router_probs)[:, None],
+            [mid_even[None], mid_odd[None]],
+            [cot_even[None], cot_odd[None]],
+            expert_gate,
+            expert_up,
+            expert_down,
+            router_probs.transpose(1, 0, 2),
+            router_t,
+        )
+        hidden_own, gate_lin_own, up_lin_own, x_own_cut, d_own_cut = own_out[:5]
+        moe_even, moe_odd, dmid_even, dmid_odd, dlogits = own_out[5:]
+        dmid = scatter_sum(dmid_even, dmid_odd)
+        scaled = dmid * gain_mid
+        mid_grad = jnp.sum(dmid * (residual * rs_mid), axis=0)
+        inner = jnp.mean(scaled * residual, axis=-1, keepdims=True)
+        dres = cotangent.astype(single) + rs_mid * (scaled - residual * (rs_mid * rs_mid * inner))
+        dres_chips = gather_chips(dres.astype(bfloat))
+        dres_even = jnp.stack(dres_chips)
+        dres_odd = swap(dres_even, "expert", 1).reshape(-1, model)
+        dres_even = dres_even.reshape(-1, model)
+        datt_b = jnp.concatenate(
+            [dot32(part, wo, ((1,), (1,))) for part in (dres_even, dres_odd)], axis=0
+        )
+        datt_b = datt_b.astype(bfloat)
+
+        moe_pairs = pair_sums(after(moe_even, dres_odd), after(moe_odd, dres_odd))
+        cot_planes_odd = swap(cot_planes, "expert", 1)
+        gate_tables = [swap(local_probs(router_probs), "dp", kd) for kd in range(1, near)]
+
+        dq_rot, dk_rot, dv = [], [], []
+        for prob, da, q_h, k_h, v_h in zip(
+            probs, per_head(datt_b), per_head(query_b), per_head(key_b), per_head(value_b)
+        ):
+            dprob = dot32(da, v_h, ((1,), (1,)))
+            dsum = jnp.sum(prob * dprob, axis=-1, keepdims=True)
+            dscores = (prob * (dprob - dsum)).astype(bfloat)
+            dv.append(dot32(prob.astype(bfloat), da, ((0,), (0,))))
+            dq_rot.append(dot32(dscores, k_h, ((1,), (0,))) * scale)
+            dk_rot.append(dot32(dscores, q_h, ((0,), (0,))) * scale)
+        dq_un = rotate(jnp.concatenate(dq_rot, axis=-1), True)
+        dk_un = rotate(jnp.concatenate(dk_rot, axis=-1), True)
+        inners = jnp.stack(
+            [
+                jnp.sum(dq_un * own_gain_q * query_raw, axis=-1),
+                jnp.sum(dk_un * own_gain_k * key_raw, axis=-1),
+            ]
+        )
+        inners = sum_rows_over_expert(inners.reshape(2, n, rows)).reshape(2, length)
+        query_gain_grad = jnp.sum(dq_un * query_raw * rs_q, axis=0)
+        key_gain_grad = jnp.sum(dk_un * key_raw * rs_k, axis=0)
+        dq_b = (
+            rs_q * dq_un * own_gain_q - query_raw * (rs_q**3 / model * inners[0][:, None])
+        ).astype(bfloat)
+        dk_b = (
+            rs_k * dk_un * own_gain_k - key_raw * (rs_k**3 / model * inners[1][:, None])
+        ).astype(bfloat)
+        dv_b = jnp.concatenate(dv, axis=-1).astype(bfloat)
+        dnormed_part = [
+                (
+                    dot32(dq_part, w_q, ((1,), (1,)))
+                    + dot32(dk_part, w_k, ((1,), (1,)))
+                    + dot32(dv_part, w_v, ((1,), (1,)))
+                ).astype(bfloat)
+                for dq_part, dk_part, dv_part in zip(halves(dq_b), halves(dk_b), halves(dv_b))
+        ]
+        output_part = dot32(dres_even, attended[: length // 2], ((0,), (0,))) + dot32(
+            dres_odd, attended[length // 2 :], ((0,), (0,))
+        )
+        early = jnp.stack([dot32(normed_b, dv_b, ((0,), (0,))), output_part]).astype(bfloat)
+        late = jnp.stack([dot32(normed_b, part, ((0,), (0,))) for part in (dq_b, dk_b)])
+        late = late.astype(bfloat)
+        return (
+            own_out,
+            dres,
+            dres_even,
+            dres_odd,
+            mid_grad,
+            query_gain_grad,
+            key_gain_grad,
+            dq_b,
+            dk_b,
+            dv_b,
+            dnormed_part,
+            moe_pairs,
+            cot_planes_odd,
+            gate_tables,
+            early,
+            late,
+        )
+
+    (
+        own_out,
+        dres,
+        dres_even,
+        dres_odd,
+        mid_grad,
+        query_gain_grad,
+        key_gain_grad,
+        dq_b,
+        dk_b,
+        dv_b,
+        dnormed_part,
+        moe_pairs,
+        cot_planes_odd,
+        gate_tables,
+        early,
+        late,
+    ) = stage(ready, backward)
     hidden_own, gate_lin_own, up_lin_own, x_own_cut, d_own_cut = own_out[:5]
     moe_even, moe_odd, dmid_even, dmid_odd, dlogits = own_out[5:]
-    dmid = scatter_sum(dmid_even, after(dmid_odd, cot_chunks[1]))
-    scaled = after(dmid, cot_chunks[2]) * gain_mid
-    cot_chunks += [swap(after(chunk, dmid), "expert", 1) for chunk in cot_chunks]
+    dnormed = scatter_sum(*dnormed_part)
+    dnormed_part = dnormed_part[0]
+
     dlogits = dlogits.transpose(1, 0, 2).astype(bfloat)
     router_grad = dot32(
         dlogits[:, :, :rows].reshape(experts, -1), mid_even.reshape(-1, model), ((1,), (0,))
     ) + dot32(dlogits[:, :, rows:].reshape(experts, -1), mid_odd.reshape(-1, model), ((1,), (0,)))
 
-    all_probs = router_probs_of(mid_planes).reshape(experts, near, n, rows)
-    all_probs = jnp.take(local_probs(all_probs), by_group(slots), axis=2)
-
+    mid_planes = [mid_planes, swap(mid_planes, "expert", 1)]
+    cot_planes = [cot_planes, cot_planes_odd]
     def add_sequences(masks, more, *earlier):
         planes = [plane % near ^ kd for kd in masks]
-        tables = [
-            lax.dynamic_index_in_dim(all_probs, there, 1, keepdims=False).reshape(local, half, block)
-            for there in planes
-        ]
         return routed_others(
-            jnp.concatenate([plane[None] % near, jnp.full((1,), len(masks), jnp.int32), jnp.stack(planes), by_group(slots)]),
+            jnp.concatenate([plane[None] % near, jnp.full((1,), len(masks), jnp.int32), jnp.stack(planes)]),
             cap,
             near,
             far,
             after(jnp.stack([ranks(kd) for kd in masks], axis=1), *earlier),
-            jnp.stack(tables, axis=1),
+            jnp.stack([gate_tables[kd - 1] for kd in masks], axis=1),
             mid_planes,
-            cot_chunks,
+            cot_planes,
             expert_gate,
             expert_up,
             expert_down,
             more,
         )
 
-    mid_grad = jnp.sum(dmid * (residual * rs_mid), axis=0)
-    inner = jnp.mean(scaled * residual, axis=-1, keepdims=True)
-    dres = cotangent.astype(single) + rs_mid * (scaled - residual * (rs_mid * rs_mid * inner))
-    dres_chips = gather_chips(dres.astype(bfloat))
-    dres_even = jnp.stack(dres_chips)
-    dres_odd = swap(dres_even, "expert", 1).reshape(-1, model)
-    dres_even = dres_even.reshape(-1, model)
-    datt_b = jnp.concatenate(
-        [dot32(part, wo, ((1,), (1,))) for part in (dres_even, dres_odd)], axis=0
-    )
-    datt_b = after(datt_b, *cot_chunks[3:half]).astype(bfloat)
-
-    moe = scatter_sum(after(moe_even, dres_odd), after(moe_odd, dres_odd))
-    output = (residual + moe).astype(bfloat)
-
-    dq_rot, dk_rot, dv = [], [], []
-    for prob, da, q_h, k_h, v_h in zip(
-        probs, per_head(datt_b), per_head(query_b), per_head(key_b), per_head(value_b)
-    ):
-        dprob = dot32(da, v_h, ((1,), (1,)))
-        dsum = jnp.sum(prob * dprob, axis=-1, keepdims=True)
-        dscores = (prob * (dprob - dsum)).astype(bfloat)
-        dv.append(dot32(prob.astype(bfloat), da, ((0,), (0,))))
-        dq_rot.append(dot32(dscores, k_h, ((1,), (0,))) * scale)
-        dk_rot.append(dot32(dscores, q_h, ((0,), (0,))) * scale)
-    dq_un = rotate(jnp.concatenate(dq_rot, axis=-1), True)
-    dk_un = rotate(jnp.concatenate(dk_rot, axis=-1), True)
-    inners = jnp.stack(
-        [
-            jnp.sum(dq_un * own_gain_q * query_raw, axis=-1),
-            jnp.sum(dk_un * own_gain_k * key_raw, axis=-1),
-        ]
-    )
-    inners = after(inners, moe, mid_planes)
-    inners = sum_rows_over_expert(inners.reshape(2, n, rows)).reshape(2, length)
-    query_gain_grad = jnp.sum(dq_un * query_raw * rs_q, axis=0)
-    key_gain_grad = jnp.sum(dk_un * key_raw * rs_k, axis=0)
-    dq_b = (
-        rs_q * dq_un * own_gain_q - query_raw * (rs_q**3 / model * inners[0][:, None])
-    ).astype(bfloat)
-    dk_b = (
-        rs_k * dk_un * own_gain_k - key_raw * (rs_k**3 / model * inners[1][:, None])
-    ).astype(bfloat)
-    dv_b = jnp.concatenate(dv, axis=-1).astype(bfloat)
-    dnormed_part = [
-            (
-                dot32(dq_part, w_q, ((1,), (1,)))
-                + dot32(dk_part, w_k, ((1,), (1,)))
-                + dot32(dv_part, w_v, ((1,), (1,)))
-            ).astype(bfloat)
-            for dq_part, dk_part, dv_part in zip(halves(dq_b), halves(dk_b), halves(dv_b))
-    ]
-    dnormed = scatter_sum(*dnormed_part)
-    dnormed_part = dnormed_part[0]
-
-    def planes_sum(partials):
-        return lax.psum_scatter(
-            jnp.stack(partials).astype(bfloat), "dp", scatter_dimension=1, tiled=True
-        )
-
-    output_part = dot32(dres_even, attended[: length // 2], ((0,), (0,))) + dot32(
-        dres_odd, attended[length // 2 :], ((0,), (0,))
-    )
-    early = planes_sum([dot32(normed_b, dv_b, ((0,), (0,))), after(output_part, mid_planes)])
-    late = planes_sum([dot32(normed_b, part, ((0,), (0,))) for part in (dq_b, dk_b)])
+    late = lax.psum_scatter(late, "dp", scatter_dimension=1, tiled=True)
+    early = lax.psum_scatter(early, "dp", scatter_dimension=1, tiled=True)
+    moe = sum_chips(moe_pairs)
+    weight_sums = add_sequences(list(range(1, near - 1)), None, dnormed_part)
+    dnormed = after(dnormed, weight_sums[0])
     summed = jnp.concatenate([early[:1], late], axis=0)
     moved = lax.all_to_all(
-        summed.reshape(3, n, shard, width).transpose(1, 0, 2, 3),
+        after(summed, weight_sums[0]).reshape(3, n, shard, width).transpose(1, 0, 2, 3),
         "expert",
         split_axis=0,
         concat_axis=0,
@@ -710,7 +768,7 @@
     )
     moved = moved.transpose(1, 2, 0, 3).reshape(3, shard, model).astype(single)
     value_grad, query_grad, key_grad = moved[0], moved[1], moved[2]
-    output_sum = early[1].reshape(model // m, m, shard).transpose(1, 2, 0)
+    output_sum = after(early[1], weight_sums[0]).reshape(model // m, m, shard).transpose(1, 2, 0)
     pieces_here = []
     for turn in range(m):
         pairs = [(((s % m + turn) % m) * n + s // m, s) for s in range(m * n)]
@@ -722,6 +780,7 @@
     )
     output_grad = output_grad.transpose(1, 0, 2).reshape(shard, model).astype(single)
 
+    output = (residual + moe).astype(bfloat)
     rs_own = rs_in[:rows]
     scaled_in = dnormed * gain_in
     inner_in = jnp.mean(scaled_in * x_own, axis=-1, keepdims=True)
@@ -751,9 +810,8 @@
     for k in range(1, m):
         total = total + swap(small_sum[:, k], "dp", k)
 
-    weight_sums = add_sequences(list(range(1, near - 1)), None, dnormed_part)
     own_rows = [x_own_cut, d_own_cut, hidden_own, gate_lin_own, up_lin_own]
-    weight_sums = add_sequences([near - 1], own_rows + list(weight_sums), dnormed, summed, moved, total)
+    weight_sums = add_sequences([near - 1], own_rows + list(weight_sums), moe)
     gate_grad, up_grad, down_grad = weight_sums
     span = model // m
 

time: 793 us -> 715 us (0.902)
  waiting for transfers between devices: 230 us -> 183 us
  starting transfers between devices: 134 us -> 110 us
  other arithmetic: 101 us -> 85.8 us
  between operations: 31.6 us -> 22.8 us
    ppermute x62 -> x57, waiting for transfers between devices: 212 us -> 178 us  [swap(): return lax.ppermute(values, axis, [(i, i ^ mask) for i in range(count)])]
    ppermute x62 -> x57, starting transfers between devices: 102 us -> 72.7 us  [swap(): return lax.ppermute(values, axis, [(i, i ^ mask) for i in range(count)])]
    add x21 -> x10, other arithmetic: 25.7 us -> 7.64 us  [after(): values = values + zero.astype(values.dtype)]
    cond x0 -> x84, local copies, waits for them, and re-layouts: none -> 17.9 us  [the longest x6 10.3 us: stage(): lax.cond(ready, compute, lambda: jax.tree.map(lambda a: jnp.zeros(a.shape...]
    convert_element_type x7 -> x9, other arithmetic: 5.65 us -> 18.7 us  [the longest x1 8.21 us: backward(): dscores = (prob * (dprob - dsum)).astype(bfloat)]
    another operation x14 -> x12, local copies, waits for them, and re-layouts: 1.18 us -> 12.1 us  [the longest x3 0.63 us: add_sequences(): jnp.stack(tables, axis=1)]
    slice x21 -> x12, local copies, waits for them, and re-layouts: 20.6 us -> 11 us  [after(): zero = jnp.minimum(jnp.abs(result[(-1,) * result.ndim]), 0)]
    unnamed x357 -> x127, local copies, waits for them, and re-layouts: 18.7 us -> 10.8 us
  transfers between devices with their start and end apart: 79 -> 71, of which waited for: 28 -> 32; matrix products, arithmetic and copies ran while one was open for 27% -> 30% of each run, Pallas kernels for 14% -> 22%
where the time goes in v3:
time: 715 us; the launch traced here: 705 us
  waiting for transfers between devices  183 us (26%)
  Pallas kernels  152 us (21%)
  starting transfers between devices  110 us (15%)
  other arithmetic  85.8 us (12%)
  local copies, waits for them, and re-layouts  79.8 us (11%)
  matrix products  68 us (10%)
  between operations  22.8 us (3%)
    ppermute x57, waiting for transfers between devices, swap(): return lax.ppermute(values, axis, [(i, i ^ mask) for i in range(count)])  178 us
    pallas_call x2, Pallas kernels, routed_others(): pl.pallas_call(functools.partial(others_kernel, len(mid), len(cot), group...  93.5 us
    ppermute x57, starting transfers between devices, swap(): return lax.ppermute(values, axis, [(i, i ^ mask) for i in range(count)])  72.7 us
    dot_general x34, matrix products, dot32(): lax.dot_general(left, right, (dims, ((), ())), preferred_element_type=sin...  66.7 us
    pallas_call x1, Pallas kernels, routed_own(): pl.pallas_call(functools.partial(own_kernel, groups, block, cap, near, fa...  58.3 us
  transfers between devices with their start and end apart: 71, of which 32 were waited for; matrix products, arithmetic and copies ran while one was open for 30% of the time, Pallas kernels for 22%

profile of v3, /device:TPU:0, one launch (start us, length us, event | category | flops | bytes accessed | tf_op | source)
XLA Modules:
  0.0 704.7 jit_solution(12357940266759028685)
XLA Ops:
  11.5 5.2 all-to-all-start
  39.5 14.4 %collective-permute-done.38 = bf16[1,3,512,256]{3,2,1,0:T(8,128)(2,1)S(1)} collective-permute-done((bf16[1,3,512,256]{3,2,1,0:T(8,128)(2,1)S(1)}, bf16[1,3,512,256]{3,2,1,0:T(8,128)(2,1)S(1)}, u32[]{:S(2)}, u32[]{:S(2)}) %collective-permute-start.38) | collective-permute-done | bytes 786464 | tf_op jit(solution)/shard_map/ppermute | solution.py:31
  54.1 16.5 %collective-permute-start.44 = (bf16[2,3,512,256]{3,2,1,0:T(8,128)(2,1)S(1)}, bf16[2,3,512,256]{3,2,1,0:T(8,128)(2,1)S(1)}, u32[]{:S(2)}, u32[]{:S(2)}) collective-permute-start(bf16[2,3,512,256]{3,2,1,0:T(8,128)(2,1)S(1)} %pad_maximum_fusion.17), channel_id=1, source_target_pairs={{0,8},{8,0},{16,24},{24,16},{1,9},{9,1},{17,25},{25,17},{2,10},{10... | collective-permute-start | bytes 4718600 | tf_op jit(solution)/shard_map/ppermute | solution.py:31
  71.8 6.8 collective-permute-done.34
  80.9 23.4 %collective-permute-done.44 = bf16[2,3,512,256]{3,2,1,0:T(8,128)(2,1)S(1)} collective-permute-done((bf16[2,3,512,256]{3,2,1,0:T(8,128)(2,1)S(1)}, bf16[2,3,512,256]{3,2,1,0:T(8,128)(2,1)S(1)}, u32[]{:S(2)}, u32[]{:S(2)}) %collective-permute-start.44) | collective-permute-done | bytes 1572896 | tf_op jit(solution)/shard_map/ppermute | solution.py:31
  151.4 122.9 %conditional.2 = (f32[1024,256]{0,1:T(8,128)}, f32[1024,256]{0,1:T(8,128)}, f32[1024,1]{0,1:T(1,128)S(1)}, f32[1024,1]{0,1:T(1,128)S(1)}, bf16[1024,256]{0,1:T(8...) conditional(s32[]{:T(128)} %bitcast.61, () %tuple.42, ...), branch_computations={%region_2.3_spmd, %region_3.0_spmd} | conditional | flops 5424828416 | bytes 173776416 | solution.py:36
  159.8 5.5 collective-permute-start.24
  217.8 10.4 %collective-permute-done.26 = bf16[128,2048]{1,0:T(8,128)(2,1)S(1)} collective-permute-done((bf16[128,2048]{1,0:T(8,128)(2,1)S(1)}, bf16[128,2048]{1,0:T(8,128)(2,1)S(1)}, u32[]{:S(2)}, u32[]{:S(2)}) %collective-permute-start.26) | collective-permute-done | bytes 524320 | tf_op jit(solution)/shard_map/cond/branch_1_fun/ppermute | solution.py:31
  228.3 10.4 %collective-permute-done.27 = bf16[128,2048]{1,0:T(8,128)(2,1)S(1)} collective-permute-done((bf16[128,2048]{1,0:T(8,128)(2,1)S(1)}, bf16[128,2048]{1,0:T(8,128)(2,1)S(1)}, u32[]{:S(2)}, u32[]{:S(2)}) %collective-permute-start.27) | collective-permute-done | bytes 524320 | tf_op jit(solution)/shard_map/cond/branch_1_fun/ppermute | solution.py:31
  244.4 11.2 %collective-permute-done.29 = bf16[128,2048]{1,0:T(8,128)(2,1)S(1)} collective-permute-done((bf16[128,2048]{1,0:T(8,128)(2,1)S(1)}, bf16[128,2048]{1,0:T(8,128)(2,1)S(1)}, u32[]{:S(2)}, u32[]{:S(2)}) %collective-permute-start.29) | collective-permute-done | bytes 524320 | tf_op jit(solution)/shard_map/cond/branch_1_fun/ppermute | solution.py:31
  255.6 10.3 %collective-permute-done.30 = bf16[128,2048]{1,0:T(8,128)(2,1)S(1)} collective-permute-done((bf16[128,2048]{1,0:T(8,128)(2,1)S(1)}, bf16[128,2048]{1,0:T(8,128)(2,1)S(1)}, u32[]{:S(2)}, u32[]{:S(2)}) %collective-permute-start.30) | collective-permute-done | bytes 524320 | tf_op jit(solution)/shard_map/cond/branch_1_fun/ppermute | solution.py:31
  289.5 217.9 %conditional.3 = (bf16[2,576,1024]{2,1,0:T(8,128)(2,1)}, bf16[2,576,1024]{2,1,0:T(8,128)(2,1)}, bf16[2,576,1024]{2,1,0:T(8,128)(2,1)}, bf16[2,576,512]{2,1,0:T(8...) conditional(s32[]{:T(128)} %bitcast.61, () %tuple.44, ...), branch_computations={%region_15.16_spmd, %region_16.25_spmd} | conditional | flops 39786467328 | bytes 419566912 | solution.py:36
  292.2 58.3 %routed_own.1 = (bf16[2,576,1024]{2,1,0:T(8,128)(2,1)}, bf16[2,576,1024]{2,1,0:T(8,128)(2,1)}, bf16[2,576,1024]{2,1,0:T(8,128)(2,1)}, bf16[2,576,512]{2,1,0:T(8,...) custom-call(s32[2]{0:T(128)} %get-tuple-element.131.ids_ref, ...), custom_call_target="tpu_custom_call" | custom-call | flops 28991029248 | bytes 50331648 | tf_op jit(solution)/shard_map/cond/branch_1_fun/routed_own/pallas_call | solution.py:314
  360.4 12.2 %collective-permute-done.1 = bf16[128,2048]{1,0:T(8,128)(2,1)S(1)} collective-permute-done((bf16[128,2048]{1,0:T(8,128)(2,1)S(1)}, bf16[128,2048]{1,0:T(8,128)(2,1)S(1)}, u32[]{:S(2)}, u32[]{:S(2)}) %collective-permute-start.1) | collective-permute-done | bytes 524320 | tf_op jit(solution)/shard_map/cond/branch_1_fun/ppermute | solution.py:31
  372.6 10.4 %collective-permute-done.2 = bf16[128,2048]{1,0:T(8,128)(2,1)S(1)} collective-permute-done((bf16[128,2048]{1,0:T(8,128)(2,1)S(1)}, bf16[128,2048]{1,0:T(8,128)(2,1)S(1)}, u32[]{:S(2)}, u32[]{:S(2)}) %collective-permute-start.2) | collective-permute-done | bytes 524320 | tf_op jit(solution)/shard_map/cond/branch_1_fun/ppermute | solution.py:31
  389.7 11.3 %collective-permute-done.4 = bf16[128,2048]{1,0:T(8,128)(2,1)S(1)} collective-permute-done((bf16[128,2048]{1,0:T(8,128)(2,1)S(1)}, bf16[128,2048]{1,0:T(8,128)(2,1)S(1)}, u32[]{:S(2)}, u32[]{:S(2)}) %collective-permute-start.4) | collective-permute-done | bytes 524320 | tf_op jit(solution)/shard_map/cond/branch_1_fun/ppermute | solution.py:31
  401.0 11.5 %collective-permute-done.5 = bf16[128,2048]{1,0:T(8,128)(2,1)S(1)} collective-permute-done((bf16[128,2048]{1,0:T(8,128)(2,1)S(1)}, bf16[128,2048]{1,0:T(8,128)(2,1)S(1)}, u32[]{:S(2)}, u32[]{:S(2)}) %collective-permute-start.5) | collective-permute-done | bytes 524320 | tf_op jit(solution)/shard_map/cond/branch_1_fun/ppermute | solution.py:31
  433.3 5.1 multiply_reduce_fusion.4
  443.4 8.2 %multiply_convert_fusion = (bf16[1024,1024]{0,1:T(8,128)(2,1)S(1)}, bf16[1024,1024]{0,1:T(8,128)(2,1)S(1)}) fusion(f32[1024,1024]{0,1:T(8,128)} %get-tuple-element.162, f32[1024,1024]{0,1:T(8,128)} %get-tuple-element.960, f32[1024]{0:T(1024)S(1)} %get-tuple-element.959, f32[1024,1024]{0,1:T(8,128)} %get-tuple-element.156, ...), kind=kLoop, calls=%fused_computation.93 | loop fusion | flops 6291456 | bytes 20979712 | tf_op jit(solution)/shard_map/cond/branch_1_fun/convert_element_type | solution.py:654
  530.8 10.6 %collective-permute-done.47 = bf16[128,2048]{1,0:T(8,128)(2,1)} collective-permute-done((bf16[128,2048]{1,0:T(8,128)(2,1)}, bf16[128,2048]{1,0:T(8,128)(2,1)}, u32[]{:S(2)}, u32[]{:S(2)}) %collective-permute-start.47) | collective-permute-done | bytes 524320 | tf_op jit(solution)/shard_map/ppermute | solution.py:31
  553.0 55.2 %routed_others.2 = (f32[2,512,1024]{2,1,0:T(8,128)}, f32[2,512,1024]{2,1,0:T(8,128)}, f32[2,1024,512]{2,1,0:T(8,128)}) custom-call(s32[4]{0:T(128)} %pad_add_fusion.1.ids_ref, f32[2,2,4,256]{3,2,1,0:T(4,128)} %copy.306.rank_ref, f32[2,2,4,256]{3,2,1,0:T(4,128)} %pad_maximum_fusion.22.prob_ref, bf16[4,4,128,2048]{3,2,1,0:T(8,128)(2,1)} %bitcast.424, ...), custom_call_target="tpu_custom_call" | custom-call | flops 38654705664 | bytes 67108864 | tf_op jit(solution)/shard_map/routed_others/pallas_call | solution.py:375
  616.0 5.7 collective-permute-start.55
  629.1 6.8 all-to-all-start.1
  636.6 38.2 %routed_others.3 = (f32[2,512,1024]{2,1,0:T(8,128)}, f32[2,512,1024]{2,1,0:T(8,128)}, f32[2,1024,512]{2,1,0:T(8,128)}) custom-call(s32[3]{0:T(128)} %pad_add_fusion.2.ids_ref, f32[2,1,4,256]{3,2,1,0:T(4,128)} %fusion.111.rank_ref, f32[2,1,4,256]{3,2,1,0:T(4,128)S(1)} %copy-done.60, ...), custom_call_target="tpu_custom_call", output_to_operand_aliasing={{0}: (15, {}), {1}: (16, {}), {2}: (17, {})} | custom-call | flops 19327352832 | bytes 67108864 | tf_op jit(solution)/shard_map/routed_others/pallas_call | solution.py:375
  (586 shorter events, 331.6 us)
Async XLA Ops:
  16.6 262.4 %all-gather.4.cloned.1.call-start = ((), (), s32[]{:S(2)}) async-start(), calls=%async_computation.4 | async-start | bytes 10485760 | tf_op jit(solution)/shard_map/all_gather | solution.py:500
  30.7 40.0 %collective-permute-start.33 = (bf16[2,128,2048]{2,1,0:T(8,128)(2,1)S(1)}, bf16[2,128,2048]{2,1,0:T(8,128)(2,1)S(1)}, u32[]{:S(2)}, u32[]{:S(2)}) collective-permute-start(bf16[2,128,2048]{2,1,0:T(8,128)(2,1)S(1)} %maximum_add_fusion.6), channel_id=1, source_target_pairs={{0,2},{1,3},{2,0},{3,1},{4,6},{5,7},{6,4},{7,5},{8,10},{9,11},{10,... | collective-permute-start | bytes 3145736 | tf_op jit(solution)/shard_map/ppermute | solution.py:31
  32.2 46.4 %collective-permute-start.34 = (bf16[2,128,2048]{2,1,0:T(8,128)(2,1)S(1)}, bf16[2,128,2048]{2,1,0:T(8,128)(2,1)S(1)}, u32[]{:S(2)}, u32[]{:S(2)}) collective-permute-start(bf16[2,128,2048]{2,1,0:T(8,128)(2,1)S(1)} %maximum_add_fusion.6), channel_id=1, source_target_pairs={{0,4},{1,5},{2,6},{3,7},{4,0},{5,1},{6,2},{7,3},{8,12},{9,13},{10,... | collective-permute-start | bytes 3145736 | tf_op jit(solution)/shard_map/ppermute | solution.py:31
  33.7 46.0 %collective-permute-start.35 = (bf16[2,128,2048]{2,1,0:T(8,128)(2,1)S(1)}, bf16[2,128,2048]{2,1,0:T(8,128)(2,1)S(1)}, u32[]{:S(2)}, u32[]{:S(2)}) collective-permute-start(bf16[2,128,2048]{2,1,0:T(8,128)(2,1)S(1)} %maximum_add_fusion.6), channel_id=1, source_target_pairs={{0,6},{1,7},{2,4},{3,5},{4,2},{5,3},{6,0},{7,1},{8,14},{9,15},{10,... | collective-permute-start | bytes 3145736 | tf_op jit(solution)/shard_map/ppermute | solution.py:31
  54.1 50.2 %collective-permute-start.44 = (bf16[2,3,512,256]{3,2,1,0:T(8,128)(2,1)S(1)}, bf16[2,3,512,256]{3,2,1,0:T(8,128)(2,1)S(1)}, u32[]{:S(2)}, u32[]{:S(2)}) collective-permute-start(bf16[2,3,512,256]{3,2,1,0:T(8,128)(2,1)S(1)} %pad_maximum_fusion.17), channel_id=1, source_target_pairs={{0,8},{8,0},{16,24},{24,16},{1,9},{9,1},{17,25},{25,17},{2,10},{10... | collective-permute-start | bytes 4718600 | tf_op jit(solution)/shard_map/ppermute | solution.py:31
  108.4 399.1 %all-gather.6.cloned.1.call-start = ((), (), s32[]{:S(2)}) async-start(), calls=%async_computation.7 | async-start | bytes 10485760 | tf_op jit(solution)/shard_map/all_gather | solution.py:591
  151.4 50.0 %collective-permute-start.21 = (bf16[64,2048]{1,0:T(8,128)(2,1)}, bf16[64,2048]{1,0:T(8,128)(2,1)S(1)}, u32[]{:S(2)}, u32[]{:S(2)}) collective-permute-start(bf16[64,2048]{1,0:T(8,128)(2,1)} %get-tuple-element.282), channel_id=1, source_target_pairs={{0,0},{1,8},{2,16},{3,24},{4,1},{5,9},{6,17},{7,25},{8,2},{9,10},{... | collective-permute-start | bytes 786440 | tf_op jit(solution)/shard_map/cond/branch_1_fun/ppermute | solution.py:551
  153.0 50.3 %collective-permute-start.22 = (bf16[64,2048]{1,0:T(8,128)(2,1)}, bf16[64,2048]{1,0:T(8,128)(2,1)S(1)}, u32[]{:S(2)}, u32[]{:S(2)}) collective-permute-start(bf16[64,2048]{1,0:T(8,128)(2,1)} %get-tuple-element.282), channel_id=1, source_target_pairs={{0,8},{1,16},{2,24},{3,0},{4,9},{5,17},{6,25},{7,1},{8,10},{9,18},... | collective-permute-start | bytes 786440 | tf_op jit(solution)/shard_map/cond/branch_1_fun/ppermute | solution.py:551
  157.1 46.9 %collective-permute-start.23 = (bf16[64,2048]{1,0:T(8,128)(2,1)}, bf16[64,2048]{1,0:T(8,128)(2,1)S(1)}, u32[]{:S(2)}, u32[]{:S(2)}) collective-permute-start(bf16[64,2048]{1,0:T(8,128)(2,1)} %get-tuple-element.282), channel_id=1, source_target_pairs={{0,16},{1,24},{2,0},{3,8},{4,17},{5,25},{6,1},{7,9},{8,18},{9,26},... | collective-permute-start | bytes 786440 | tf_op jit(solution)/shard_map/cond/branch_1_fun/ppermute | solution.py:551
  159.8 44.9 %collective-permute-start.24 = (bf16[64,2048]{1,0:T(8,128)(2,1)}, bf16[64,2048]{1,0:T(8,128)(2,1)S(1)}, u32[]{:S(2)}, u32[]{:S(2)}) collective-permute-start(bf16[64,2048]{1,0:T(8,128)(2,1)} %get-tuple-element.282), channel_id=1, source_target_pairs={{0,24},{1,0},{2,8},{3,16},{4,25},{5,1},{6,9},{7,17},{8,26},{9,2},{... | collective-permute-start | bytes 786440 | tf_op jit(solution)/shard_map/cond/branch_1_fun/ppermute | solution.py:551
  282.5 331.6 %reduce-scatter.3.cloned.1.call-start = ((), (), s32[]{:S(2)}) async-start(), calls=%async_computation.5 | async-start | bytes 2621440 | tf_op jit(solution)/shard_map/reduce_scatter | solution.py:757
  419.5 87.8 %collective-permute-start.13 = (bf16[4,4,128,2048]{3,2,1,0:T(8,128)(2,1)}, bf16[4,4,128,2048]{3,2,1,0:T(8,128)(2,1)}, u32[]{:S(2)}, u32[]{:S(2)}) collective-permute-start(bf16[4,4,128,2048]{3,2,1,0:T(8,128)(2,1)} %get-tuple-element.174), channel_id=1, source_target_pairs={{0,1},{1,0},{2,3},{3,2},{4,5},{5,4},{6,7},{7,6},{8,9},{9,8},{10,11... | collective-permute-start | bytes 25165832 | tf_op jit(solution)/shard_map/cond/branch_1_fun/ppermute | solution.py:31
  469.4 34.3 %collective-permute-start.12 = (bf16[512,2048]{1,0:T(8,128)(2,1)}, bf16[512,2048]{1,0:T(8,128)(2,1)}, u32[]{:S(2)}, u32[]{:S(2)}) collective-permute-start(bf16[512,2048]{1,0:T(8,128)(2,1)} %broadcast_add_fusion), channel_id=1, source_target_pairs={{0,1},{1,0},{2,3},{3,2},{4,5},{5,4},{6,7},{7,6},{8,9},{9,8},{10,11... | collective-permute-start | bytes 6291464 | tf_op jit(solution)/shard_map/cond/branch_1_fun/ppermute | solution.py:31
  507.5 45.5 %collective-permute-start.53 = (bf16[4,4,128,2048]{3,2,1,0:T(8,128)(2,1)}, bf16[4,4,128,2048]{3,2,1,0:T(8,128)(2,1)}, u32[]{:S(2)}, u32[]{:S(2)}) collective-permute-start(bf16[4,4,128,2048]{3,2,1,0:T(8,128)(2,1)} %bitcast.423), channel_id=1, source_target_pairs={{0,1},{1,0},{2,3},{3,2},{4,5},{5,4},{6,7},{7,6},{8,9},{9,8},{10,11... | collective-permute-start | bytes 25165832 | tf_op jit(solution)/shard_map/ppermute | solution.py:31
  511.5 115.5 %reduce-scatter.5.cloned.1.call-start = ((), (), s32[]{:S(2)}) async-start(), calls=%async_computation.6 | async-start | bytes 2621440 | tf_op jit(solution)/shard_map/reduce_scatter | solution.py:756
  549.5 60.7 %collective-permute-start.50 = (bf16[128,2048]{1,0:T(8,128)(2,1)}, bf16[128,2048]{1,0:T(8,128)(2,1)S(1)}, u32[]{:S(2)}, u32[]{:S(2)}) collective-permute-start(bf16[128,2048]{1,0:T(8,128)(2,1)} %get-tuple-element.963), channel_id=1, source_target_pairs={{0,6},{1,7},{2,4},{3,5},{4,2},{5,3},{6,0},{7,1},{8,14},{9,15},{10,... | collective-permute-start | bytes 1572872 | tf_op jit(solution)/shard_map/ppermute | solution.py:31
  550.7 59.4 %collective-permute-start.51 = (bf16[128,2048]{1,0:T(8,128)(2,1)S(1)}, bf16[128,2048]{1,0:T(8,128)(2,1)S(1)}, u32[]{:S(2)}, u32[]{:S(2)}) collective-permute-start(bf16[128,2048]{1,0:T(8,128)(2,1)S(1)} %get-tuple-element.965), channel_id=1, source_target_pairs={{0,4},{1,5},{2,6},{3,7},{4,0},{5,1},{6,2},{7,3},{8,12},{9,13},{10,... | collective-permute-start | bytes 1572872 | tf_op jit(solution)/shard_map/ppermute | solution.py:31
  551.6 58.6 %collective-permute-start.52 = (bf16[128,2048]{1,0:T(8,128)(2,1)S(1)}, bf16[128,2048]{1,0:T(8,128)(2,1)S(1)}, u32[]{:S(2)}, u32[]{:S(2)}) collective-permute-start(bf16[128,2048]{1,0:T(8,128)(2,1)S(1)} %get-tuple-element.964), channel_id=1, source_target_pairs={{0,2},{1,3},{2,0},{3,1},{4,6},{5,7},{6,4},{7,5},{8,10},{9,11},{10,... | collective-permute-start | bytes 1572872 | tf_op jit(solution)/shard_map/ppermute | solution.py:31
  613.9 63.5 %collective-permute-start.58 = (f32[20,4,4,64]{3,1,0,2:T(4,128)S(1)}, f32[20,4,4,64]{3,1,0,2:T(4,128)S(1)}, u32[]{:S(2)}, u32[]{:S(2)}) collective-permute-start(f32[20,4,4,64]{3,1,0,2:T(4,128)S(1)} %slice.703), channel_id=1, source_target_pairs={{0,1},{1,0},{2,3},{3,2},{4,5},{5,4},{6,7},{7,6},{8,9},{9,8},{10,11... | collective-permute-start | bytes 245768 | tf_op jit(solution)/shard_map/ppermute | solution.py:31
  615.3 64.3 %collective-permute-start.54 = (bf16[64,512]{1,0:T(8,128)(2,1)S(1)}, bf16[64,512]{1,0:T(8,128)(2,1)S(1)}, u32[]{:S(2)}, u32[]{:S(2)}) collective-permute-start(bf16[64,512]{1,0:T(8,128)(2,1)S(1)} %get-tuple-element.991), channel_id=1, source_target_pairs={{0,0},{8,1},{16,2},{24,3},{1,4},{9,5},{17,6},{25,7},{2,8},{10,9},{... | collective-permute-start | bytes 196616 | tf_op jit(solution)/shard_map/ppermute | solution.py:776
  616.0 65.1 %collective-permute-start.55 = (bf16[64,512]{1,0:T(8,128)(2,1)S(1)}, bf16[64,512]{1,0:T(8,128)(2,1)S(1)}, u32[]{:S(2)}, u32[]{:S(2)}) collective-permute-start(bf16[64,512]{1,0:T(8,128)(2,1)S(1)} %get-tuple-element.994), channel_id=1, source_target_pairs={{8,0},{16,1},{24,2},{0,3},{9,4},{17,5},{25,6},{1,7},{10,8},{18,9},... | collective-permute-start | bytes 196616 | tf_op jit(solution)/shard_map/ppermute | solution.py:776
  621.6 59.5 %collective-permute-start.56 = (bf16[64,512]{1,0:T(8,128)(2,1)S(1)}, bf16[64,512]{1,0:T(8,128)(2,1)S(1)}, u32[]{:S(2)}, u32[]{:S(2)}) collective-permute-start(bf16[64,512]{1,0:T(8,128)(2,1)S(1)} %get-tuple-element.993), channel_id=1, source_target_pairs={{16,0},{24,1},{0,2},{8,3},{17,4},{25,5},{1,6},{9,7},{18,8},{26,9},... | collective-permute-start | bytes 196616 | tf_op jit(solution)/shard_map/ppermute | solution.py:776
  622.3 58.8 %collective-permute-start.57 = (bf16[64,512]{1,0:T(8,128)(2,1)S(1)}, bf16[64,512]{1,0:T(8,128)(2,1)S(1)}, u32[]{:S(2)}, u32[]{:S(2)}) collective-permute-start(bf16[64,512]{1,0:T(8,128)(2,1)S(1)} %get-tuple-element.992), channel_id=1, source_target_pairs={{24,0},{0,1},{8,2},{16,3},{25,4},{1,5},{9,6},{17,7},{26,8},{2,9},{... | collective-permute-start | bytes 196616 | tf_op jit(solution)/shard_map/ppermute | solution.py:776
  629.1 65.7 %all-to-all-start.1 = ((bf16[8,3,64,256]{3,2,1,0:T(8,128)(2,1)}), bf16[8,3,64,256]{3,2,1,0:T(8,128)(2,1)S(1)}, u32[]{:S(2)}, u32[]{:S(2)}) async-start(bf16[8,3,64,256]{3,2,1,0:T(8,128)(2,1)} %copy.309), calls=%async_computation.3 | async-start | bytes 1572864 | tf_op jit(solution)/shard_map/all_to_all | solution.py:762
  (143 other events, 1433.4 us)
Sparse Core Ops, SparseCore 0:
  108.5 170.5 all-gather.3
  282.6 152.5 all-gather.5
  511.6 44.4 reduce-scatter.2
  558.3 43.1 reduce-scatter.4

commit v4 on v3

--- a/solution.py
+++ b/solution.py
@@ -402,6 +402,81 @@
     )(ids, *args)
 
 
+def masked_scores(scale, q, k, place_q, place_k, piece_q, piece_k):
+    allowed = (place_k <= place_q) | ((piece_q == piece_k) & (piece_q > 0))
+    return jnp.where(allowed, dot32(q, k, ((1,), (1,))) * scale, -1e30)
+
+
+def attend_kernel(scale, q_ref, k_ref, v_ref, pq_ref, pk_ref, cq_ref, ck_ref, out_ref, mass_ref):
+    scores = masked_scores(
+        scale, q_ref[...], k_ref[...], pq_ref[...], pk_ref[...], cq_ref[...], ck_ref[...]
+    )
+    highest = jnp.max(scores, axis=-1, keepdims=True)
+    exponent = jnp.exp(scores - highest)
+    total = jnp.sum(exponent, axis=-1, keepdims=True)
+    probs = (exponent / total).astype(bfloat)
+    out_ref[...] = dot32(probs, v_ref[...], ((1,), (0,))).astype(bfloat)
+    mass_ref[0] = highest + jnp.log(total)
+
+
+def attend_back_kernel(
+    scale, q_ref, k_ref, v_ref, da_ref, mass_ref, pq_ref, pk_ref, cq_ref, ck_ref, dq_ref, dk_ref, dv_ref
+):
+    q, k, v, da = q_ref[...], k_ref[...], v_ref[...], da_ref[...]
+    scores = masked_scores(scale, q, k, pq_ref[...], pk_ref[...], cq_ref[...], ck_ref[...])
+    probs = jnp.exp(scores - mass_ref[0])
+    dprob = dot32(da, v, ((1,), (1,)))
+    dsum = jnp.sum(probs * dprob, axis=-1, keepdims=True)
+    dscores = (probs * (dprob - dsum)).astype(bfloat)
+    dq_ref[...] = dot32(dscores, k, ((1,), (0,))) * scale
+    dk = dot32(dscores, q, ((0,), (0,))) * scale
+    dv = dot32(probs.astype(bfloat), da, ((0,), (0,)))
+
+    @pl.when(pl.program_id(1) == 0)
+    def _():
+        dk_ref[...] = dk
+        dv_ref[...] = dv
+
+    @pl.when(pl.program_id(1) > 0)
+    def _():
+        dk_ref[...] += dk
+        dv_ref[...] += dv
+
+
+def attention_call(kernel, name, arrays, masses, marks, out_kinds, products):
+    length, width = arrays[0][1].shape
+    heads = width // HEAD
+    span = min(256, length)
+    by_query = pl.BlockSpec((span, HEAD), lambda h, i: (i, h))
+    by_head = pl.BlockSpec((length, HEAD), lambda h, i: (0, h))
+    mass = pl.BlockSpec((1, span, 1), lambda h, i: (h, i, 0))
+    column = pl.BlockSpec((span, 1), lambda h, i: (i, 0))
+    row = pl.BlockSpec((1, length), lambda h, i: (0, 0))
+    specs = {"query": by_query, "head": by_head, "mass": mass}
+    shapes = {"query": (length, width), "head": (length, width), "mass": (heads, length, 1)}
+    mark_args = []
+    for mark in marks:
+        mark_args += [mark[:, None], mark[None, :]]
+    return pl.pallas_call(
+        kernel,
+        grid=(heads, length // span),
+        in_specs=[specs[kind] for kind, _ in arrays]
+        + [mass] * len(masses)
+        + [column, row] * len(marks),
+        out_specs=[specs[kind] for kind, _ in out_kinds],
+        out_shape=[jax.ShapeDtypeStruct(shapes[kind], dtype) for kind, dtype in out_kinds],
+        compiler_params=pltpu.CompilerParams(
+            dimension_semantics=("arbitrary",) * 2, vmem_limit_bytes=32 * 1024 * 1024
+        ),
+        cost_estimate=pl.CostEstimate(
+            flops=2 * products * heads * length * length * HEAD,
+            bytes_accessed=8 * length * width,
+            transcendentals=heads * length * length,
+        ),
+        name=name,
+    )(*[array for _, array in arrays], *masses, *mark_args)
+
+
 def per_device(
     tokens,
     attn_query,
@@ -517,9 +592,6 @@
 
     own_gain_q = lax.dynamic_slice_in_dim(gain_query, mine * width, width)
     own_gain_k = lax.dynamic_slice_in_dim(gain_key, mine * width, width)
-    def per_head(array):
-        return [array[:, h * HEAD : (h + 1) * HEAD] for h in range(heads)]
-
     def halves(array):
         return array[: length // 2], array[length // 2 :]
 
@@ -540,6 +612,8 @@
     own_ranks = after(ranks(0)[:, None], cot_odd)
 
     x_own = tokens.astype(single)
+
+    marks = [place, piece_row.astype(jnp.int32)]
 
     def forward():
         query_raw = dot32(normed_b, w_q, ((1,), (0,)))
@@ -565,18 +639,15 @@
         query_b = rotate(query_raw * rs_q * own_gain_q, False).astype(bfloat)
         key_b = rotate(key_raw * rs_k * own_gain_k, False).astype(bfloat)
 
-        allowed = (place[None, :] <= place[:, None]) | (
-            (piece_row[:, None] == piece_row[None, :]) & (piece_row[:, None] > 0)
-        )
-        probs = []
-        mixed = []
-        for q_h, k_h, v_h in zip(per_head(query_b), per_head(key_b), per_head(value_b)):
-            scores = jnp.where(allowed, dot32(q_h, k_h, ((1,), (1,))) * scale, -1e30)
-            exponent = jnp.exp(scores - jnp.max(scores, axis=-1, keepdims=True))
-            prob = exponent / jnp.sum(exponent, axis=-1, keepdims=True)
-            probs.append(prob)
-            mixed.append(dot32(prob.astype(bfloat), v_h, ((1,), (0,))))
-        attended = jnp.concatenate(mixed, axis=-1).astype(bfloat)
+        attended, masses = attention_call(
+            functools.partial(attend_kernel, scale),
+            "attend",
+            [("query", query_b), ("head", key_b), ("head", value_b)],
+            [],
+            marks,
+            [("query", bfloat), ("mass", single)],
+            2,
+        )
 
         projected = [dot32(part, wo, ((1,), (0,))).astype(bfloat) for part in halves(attended)]
         residual = x_own + scatter_sum(*projected)
@@ -584,9 +655,9 @@
         mid = after(residual * rs_mid * gain_mid, own_ranks).astype(bfloat)
         mid_even, mid_odd = gather_halves(mid)
         kept = (query_raw, key_raw, rs_q, rs_k, query_b, key_b, value_b, wo)
-        return kept, probs, attended, residual, rs_mid, mid_even, mid_odd
-
-    kept, probs, attended, residual, rs_mid, mid_even, mid_odd = stage(ready, forward)
+        return kept, masses, attended, residual, rs_mid, mid_even, mid_odd
+
+    kept, masses, attended, residual, rs_mid, mid_even, mid_odd = stage(ready, forward)
     query_raw, key_raw, rs_q, rs_k, query_b, key_b, value_b, wo = kept
     mid_planes = lax.all_gather(after(mid_even, cot_planes), "dp", axis=0, axis_index_groups=near_groups)
 
@@ -645,18 +716,17 @@
         cot_planes_odd = swap(cot_planes, "expert", 1)
         gate_tables = [swap(local_probs(router_probs), "dp", kd) for kd in range(1, near)]
 
-        dq_rot, dk_rot, dv = [], [], []
-        for prob, da, q_h, k_h, v_h in zip(
-            probs, per_head(datt_b), per_head(query_b), per_head(key_b), per_head(value_b)
-        ):
-            dprob = dot32(da, v_h, ((1,), (1,)))
-            dsum = jnp.sum(prob * dprob, axis=-1, keepdims=True)
-            dscores = (prob * (dprob - dsum)).astype(bfloat)
-            dv.append(dot32(prob.astype(bfloat), da, ((0,), (0,))))
-            dq_rot.append(dot32(dscores, k_h, ((1,), (0,))) * scale)
-            dk_rot.append(dot32(dscores, q_h, ((0,), (0,))) * scale)
-        dq_un = rotate(jnp.concatenate(dq_rot, axis=-1), True)
-        dk_un = rotate(jnp.concatenate(dk_rot, axis=-1), True)
+        dq_rot, dk_rot, dv = attention_call(
+            functools.partial(attend_back_kernel, scale),
+            "attend_back",
+            [("query", query_b), ("head", key_b), ("head", value_b), ("query", datt_b)],
+            [masses],
+            marks,
+            [("query", single), ("head", single), ("head", single)],
+            5,
+        )
+        dq_un = rotate(dq_rot, True)
+        dk_un = rotate(dk_rot, True)
         inners = jnp.stack(
             [
                 jnp.sum(dq_un * own_gain_q * query_raw, axis=-1),
@@ -672,7 +742,7 @@
         dk_b = (
             rs_k * dk_un * own_gain_k - key_raw * (rs_k**3 / model * inners[1][:, None])
         ).astype(bfloat)
-        dv_b = jnp.concatenate(dv, axis=-1).astype(bfloat)
+        dv_b = dv.astype(bfloat)
         dnormed_part = [
                 (
                     dot32(dq_part, w_q, ((1,), (1,)))

time: 715 us -> 701 us (0.980)
  matrix products: 68 us -> 40.4 us
  Pallas kernels: 152 us -> 175 us
  other arithmetic: 85.8 us -> 73.1 us
  starting transfers between devices: 110 us -> 118 us
    dot_general x34 -> x22, matrix products: 66.7 us -> 39.2 us  [dot32(): lax.dot_general(left, right, (dims, ((), ())), preferred_element_type=sin...]
    pallas_call x0 -> x2, Pallas kernels: none -> 22.6 us  [attention_call(): pl.pallas_call(kernel, grid=(heads, length // span), in_specs=[specs[kind...]
    ppermute x57, starting transfers between devices: 72.7 us -> 81.5 us  [swap(): return lax.ppermute(values, axis, [(i, i ^ mask) for i in range(count)])]
    convert_element_type x2, other arithmetic: 8.29 us -> 0.78 us  [the longest x1 0.73 us: per_device(): marks = [place, piece_row.astype(jnp.int32)]]
  transfers between devices with their start and end apart: 71 -> 71, of which waited for: 32 -> 31; matrix products, arithmetic and copies ran while one was open for 30% -> 25% of each run, Pallas kernels for 22% -> 25%
where the time goes in v4:
time: 701 us; the launch traced here: 692 us
  waiting for transfers between devices  176 us (25%)
  Pallas kernels  175 us (25%)
  starting transfers between devices  118 us (17%)
  local copies, waits for them, and re-layouts  83 us (12%)
  other arithmetic  73.1 us (10%)
  matrix products  40.4 us (6%)
  between operations  22.9 us (3%)
    ppermute x57, waiting for transfers between devices, swap(): return lax.ppermute(values, axis, [(i, i ^ mask) for i in range(count)])  173 us
    pallas_call x2, Pallas kernels, routed_others(): pl.pallas_call(functools.partial(others_kernel, len(mid), len(cot), group...  93.5 us
    ppermute x57, starting transfers between devices, swap(): return lax.ppermute(values, axis, [(i, i ^ mask) for i in range(count)])  81.5 us
    pallas_call x1, Pallas kernels, routed_own(): pl.pallas_call(functools.partial(own_kernel, groups, block, cap, near, fa...  58.8 us
    dot_general x22, matrix products, dot32(): lax.dot_general(left, right, (dims, ((), ())), preferred_element_type=sin...  39.2 us
    pallas_call x2, Pallas kernels, attention_call(): pl.pallas_call(kernel, grid=(heads, length // span), in_specs=[specs[kind...  22.6 us
  transfers between devices with their start and end apart: 71, of which 31 were waited for; matrix products, arithmetic and copies ran while one was open for 25% of the time, Pallas kernels for 25%

profile of v4, /device:TPU:0, one launch (start us, length us, event | category | flops | bytes accessed | tf_op | source)
XLA Modules:
  0.0 691.9 jit_solution(8459523323630879576)
XLA Ops:
  11.4 5.2 all-to-all-start
  40.5 14.4 %collective-permute-done.38 = bf16[1,3,512,256]{3,2,1,0:T(8,128)(2,1)S(1)} collective-permute-done((bf16[1,3,512,256]{3,2,1,0:T(8,128)(2,1)S(1)}, bf16[1,3,512,256]{3,2,1,0:T(8,128)(2,1)S(1)}, u32[]{:S(2)}, u32[]{:S(2)}) %collective-permute-start.38) | collective-permute-done | bytes 786464 | tf_op jit(solution)/shard_map/ppermute | solution.py:31
  55.1 16.5 %collective-permute-start.44 = (bf16[2,3,512,256]{3,2,1,0:T(8,128)(2,1)S(1)}, bf16[2,3,512,256]{3,2,1,0:T(8,128)(2,1)S(1)}, u32[]{:S(2)}, u32[]{:S(2)}) collective-permute-start(bf16[2,3,512,256]{3,2,1,0:T(8,128)(2,1)S(1)} %pad_maximum_fusion.12), channel_id=1, source_target_pairs={{0,8},{8,0},{16,24},{24,16},{1,9},{9,1},{17,25},{25,17},{2,10},{10... | collective-permute-start | bytes 4718600 | tf_op jit(solution)/shard_map/ppermute | solution.py:31
  72.8 6.8 collective-permute-done.34
  81.9 23.4 %collective-permute-done.44 = bf16[2,3,512,256]{3,2,1,0:T(8,128)(2,1)S(1)} collective-permute-done((bf16[2,3,512,256]{3,2,1,0:T(8,128)(2,1)S(1)}, bf16[2,3,512,256]{3,2,1,0:T(8,128)(2,1)S(1)}, u32[]{:S(2)}, u32[]{:S(2)}) %collective-permute-start.44) | collective-permute-done | bytes 1572896 | tf_op jit(solution)/shard_map/ppermute | solution.py:31
  147.3 130.5 %conditional.2 = (f32[1024,256]{0,1:T(8,128)S(1)}, f32[1024,256]{0,1:T(8,128)}, f32[1024,1]{0,1:T(1,128)S(1)}, f32[1024,1]{0,1:T(1,128)S(1)}, bf16[1024,256]{1,0...) conditional(s32[]{:T(128)} %bitcast.65, () %tuple.42, ...), branch_computations={%region_2.3_spmd, %region_3.7_spmd} | conditional | flops 5391013888 | bytes 126745144 | solution.py:36
  185.4 9.7 %attend.1 = (bf16[1024,256]{1,0:T(8,128)(2,1)}, f32[2,1024,1]{2,1,0:T(8,128)}) custom-call(bf16[1024,256]{1,0:T(8,128)(2,1)} %pad_maximum_fusion.1.q_ref, bf16[1024,256]{1,0:T(8,128)(2,1)} %pad_maximum_fusion.2.k_ref, bf16[1024,256]{1,0:T(8,128)(2,1)} %convolution_convert_fusion.2.v_ref, s32[1024,1]{1,0:T(8,128)S(1)} %copy.306.pq_ref, ...), custom_call_target="tpu_custom_call" | custom-call | flops 1073741824 | bytes 2097152 | tf_op jit(solution)/shard_map/cond/branch_1_fun/attend/pallas_call | solution.py:460
  210.8 6.6 collective-permute-start.27
  220.0 5.6 collective-permute-done.26
  225.5 14.5 %collective-permute-done.27 = bf16[128,2048]{1,0:T(8,128)(2,1)S(1)} collective-permute-done((bf16[128,2048]{1,0:T(8,128)(2,1)S(1)}, bf16[128,2048]{1,0:T(8,128)(2,1)S(1)}, u32[]{:S(2)}, u32[]{:S(2)}) %collective-permute-start.27) | collective-permute-done | bytes 524320 | tf_op jit(solution)/shard_map/cond/branch_1_fun/ppermute | solution.py:31
  246.5 11.2 %collective-permute-done.29 = bf16[128,2048]{1,0:T(8,128)(2,1)S(1)} collective-permute-done((bf16[128,2048]{1,0:T(8,128)(2,1)S(1)}, bf16[128,2048]{1,0:T(8,128)(2,1)S(1)}, u32[]{:S(2)}, u32[]{:S(2)}) %collective-permute-start.29) | collective-permute-done | bytes 524320 | tf_op jit(solution)/shard_map/cond/branch_1_fun/ppermute | solution.py:31
  257.7 10.3 %collective-permute-done.30 = bf16[128,2048]{1,0:T(8,128)(2,1)S(1)} collective-permute-done((bf16[128,2048]{1,0:T(8,128)(2,1)S(1)}, bf16[128,2048]{1,0:T(8,128)(2,1)S(1)}, u32[]{:S(2)}, u32[]{:S(2)}) %collective-permute-start.30) | collective-permute-done | bytes 524320 | tf_op jit(solution)/shard_map/cond/branch_1_fun/ppermute | solution.py:31
  291.1 198.5 %conditional.3 = (bf16[2,576,1024]{2,1,0:T(8,128)(2,1)}, bf16[2,576,1024]{2,1,0:T(8,128)(2,1)}, bf16[2,576,1024]{2,1,0:T(8,128)(2,1)}, bf16[2,576,512]{2,1,0:T(8...) conditional(s32[]{:T(128)} %bitcast.65, () %tuple.44, ...), branch_computations={%region_11.12_spmd, %region_12.19_spmd} | conditional | flops 40307089408 | bytes 371322048 | solution.py:36
  291.8 58.8 %routed_own.1 = (bf16[2,576,1024]{2,1,0:T(8,128)(2,1)}, bf16[2,576,1024]{2,1,0:T(8,128)(2,1)}, bf16[2,576,1024]{2,1,0:T(8,128)(2,1)}, bf16[2,576,512]{2,1,0:T(8,...) custom-call(s32[2]{0:T(128)S(1)} %get-tuple-element.130.ids_ref, ...), custom_call_target="tpu_custom_call" | custom-call | flops 28991029248 | bytes 50331648 | tf_op jit(solution)/shard_map/cond/branch_1_fun/routed_own/pallas_call | solution.py:314
  360.5 12.2 %collective-permute-done.1 = bf16[128,2048]{1,0:T(8,128)(2,1)S(1)} collective-permute-done((bf16[128,2048]{1,0:T(8,128)(2,1)S(1)}, bf16[128,2048]{1,0:T(8,128)(2,1)S(1)}, u32[]{:S(2)}, u32[]{:S(2)}) %collective-permute-start.1) | collective-permute-done | bytes 524320 | tf_op jit(solution)/shard_map/cond/branch_1_fun/ppermute | solution.py:31
  372.8 10.4 %collective-permute-done.2 = bf16[128,2048]{1,0:T(8,128)(2,1)S(1)} collective-permute-done((bf16[128,2048]{1,0:T(8,128)(2,1)S(1)}, bf16[128,2048]{1,0:T(8,128)(2,1)S(1)}, u32[]{:S(2)}, u32[]{:S(2)}) %collective-permute-start.2) | collective-permute-done | bytes 524320 | tf_op jit(solution)/shard_map/cond/branch_1_fun/ppermute | solution.py:31
  389.7 11.3 %collective-permute-done.4 = bf16[128,2048]{1,0:T(8,128)(2,1)S(1)} collective-permute-done((bf16[128,2048]{1,0:T(8,128)(2,1)S(1)}, bf16[128,2048]{1,0:T(8,128)(2,1)S(1)}, u32[]{:S(2)}, u32[]{:S(2)}) %collective-permute-start.4) | collective-permute-done | bytes 524320 | tf_op jit(solution)/shard_map/cond/branch_1_fun/ppermute | solution.py:31
  401.0 11.4 %collective-permute-done.5 = bf16[128,2048]{1,0:T(8,128)(2,1)S(1)} collective-permute-done((bf16[128,2048]{1,0:T(8,128)(2,1)S(1)}, bf16[128,2048]{1,0:T(8,128)(2,1)S(1)}, u32[]{:S(2)}, u32[]{:S(2)}) %collective-permute-start.5) | collective-permute-done | bytes 524320 | tf_op jit(solution)/shard_map/cond/branch_1_fun/ppermute | solution.py:31
  414.0 6.6 collective-permute-start.14
  435.1 12.9 %attend_back.1 = (f32[1024,256]{1,0:T(8,128)S(1)}, f32[1024,256]{1,0:T(8,128)S(1)}, f32[1024,256]{1,0:T(8,128)S(1)}) custom-call(bf16[1024,256]{1,0:T(8,128)(2,1)} %get-tuple-element.155.q_ref, bf16[1024,256]{1,0:T(8,128)(2,1)} %get-tuple-element.156.k_ref, bf16[1024,256]{1,0:T(8,128)(2,1)} %get-tuple-element.157.v_ref, ...), custom_call_target="tpu_custom_call" | custom-call | flops 2684354560 | bytes 2097152 | tf_op jit(solution)/shard_map/cond/branch_1_fun/attend_back/pallas_call | solution.py:460
  517.2 7.2 %collective-permute-done.47 = bf16[128,2048]{1,0:T(8,128)(2,1)} collective-permute-done((bf16[128,2048]{1,0:T(8,128)(2,1)}, bf16[128,2048]{1,0:T(8,128)(2,1)}, u32[]{:S(2)}, u32[]{:S(2)}) %collective-permute-start.47) | collective-permute-done | bytes 524320 | tf_op jit(solution)/shard_map/ppermute | solution.py:31
  536.0 55.3 %routed_others.2 = (f32[2,512,1024]{2,1,0:T(8,128)}, f32[2,512,1024]{2,1,0:T(8,128)}, f32[2,1024,512]{2,1,0:T(8,128)}) custom-call(s32[4]{0:T(128)} %pad_add_fusion.1.ids_ref, f32[2,2,4,256]{3,2,1,0:T(4,128)} %copy.327.rank_ref, f32[2,2,4,256]{3,2,1,0:T(4,128)} %pad_maximum_fusion.17.prob_ref, bf16[4,4,128,2048]{3,2,1,0:T(8,128)(2,1)} %bitcast.418, ...), custom_call_target="tpu_custom_call" | custom-call | flops 38654705664 | bytes 67108864 | tf_op jit(solution)/shard_map/routed_others/pallas_call | solution.py:375
  615.7 6.5 all-to-all-start.1
  622.9 38.2 %routed_others.3 = (f32[2,512,1024]{2,1,0:T(8,128)}, f32[2,512,1024]{2,1,0:T(8,128)}, f32[2,1024,512]{2,1,0:T(8,128)}) custom-call(s32[3]{0:T(128)} %pad_add_fusion.2.ids_ref, f32[2,1,4,256]{3,2,1,0:T(4,128)} %fusion.43.rank_ref, f32[2,1,4,256]{3,2,1,0:T(4,128)S(1)} %copy-done.57, ...), custom_call_target="tpu_custom_call", output_to_operand_aliasing={{0}: (15, {}), {1}: (16, {}), {2}: (17, {})} | custom-call | flops 19327352832 | bytes 67108864 | tf_op jit(solution)/shard_map/routed_others/pallas_call | solution.py:375
  (576 shorter events, 311.0 us)
Async XLA Ops:
  16.6 263.8 %all-gather.4.cloned.1.call-start = ((), (), s32[]{:S(2)}) async-start(), calls=%async_computation.4 | async-start | bytes 10485760 | tf_op jit(solution)/shard_map/all_gather | solution.py:575
  31.7 40.0 %collective-permute-start.33 = (bf16[2,128,2048]{2,1,0:T(8,128)(2,1)S(1)}, bf16[2,128,2048]{2,1,0:T(8,128)(2,1)S(1)}, u32[]{:S(2)}, u32[]{:S(2)}) collective-permute-start(bf16[2,128,2048]{2,1,0:T(8,128)(2,1)S(1)} %maximum_add_fusion.6), channel_id=1, source_target_pairs={{0,2},{1,3},{2,0},{3,1},{4,6},{5,7},{6,4},{7,5},{8,10},{9,11},{10,... | collective-permute-start | bytes 3145736 | tf_op jit(solution)/shard_map/ppermute | solution.py:31
  33.2 46.4 %collective-permute-start.34 = (bf16[2,128,2048]{2,1,0:T(8,128)(2,1)S(1)}, bf16[2,128,2048]{2,1,0:T(8,128)(2,1)S(1)}, u32[]{:S(2)}, u32[]{:S(2)}) collective-permute-start(bf16[2,128,2048]{2,1,0:T(8,128)(2,1)S(1)} %maximum_add_fusion.6), channel_id=1, source_target_pairs={{0,4},{1,5},{2,6},{3,7},{4,0},{5,1},{6,2},{7,3},{8,12},{9,13},{10,... | collective-permute-start | bytes 3145736 | tf_op jit(solution)/shard_map/ppermute | solution.py:31
  34.7 46.0 %collective-permute-start.35 = (bf16[2,128,2048]{2,1,0:T(8,128)(2,1)S(1)}, bf16[2,128,2048]{2,1,0:T(8,128)(2,1)S(1)}, u32[]{:S(2)}, u32[]{:S(2)}) collective-permute-start(bf16[2,128,2048]{2,1,0:T(8,128)(2,1)S(1)} %maximum_add_fusion.6), channel_id=1, source_target_pairs={{0,6},{1,7},{2,4},{3,5},{4,2},{5,3},{6,0},{7,1},{8,14},{9,15},{10,... | collective-permute-start | bytes 3145736 | tf_op jit(solution)/shard_map/ppermute | solution.py:31
  55.1 50.2 %collective-permute-start.44 = (bf16[2,3,512,256]{3,2,1,0:T(8,128)(2,1)S(1)}, bf16[2,3,512,256]{3,2,1,0:T(8,128)(2,1)S(1)}, u32[]{:S(2)}, u32[]{:S(2)}) collective-permute-start(bf16[2,3,512,256]{3,2,1,0:T(8,128)(2,1)S(1)} %pad_maximum_fusion.12), channel_id=1, source_target_pairs={{0,8},{8,0},{16,24},{24,16},{1,9},{9,1},{17,25},{25,17},{2,10},{10... | collective-permute-start | bytes 4718600 | tf_op jit(solution)/shard_map/ppermute | solution.py:31
  109.7 379.9 %all-gather.6.cloned.1.call-start = ((), (), s32[]{:S(2)}) async-start(), calls=%async_computation.7 | async-start | bytes 10485760 | tf_op jit(solution)/shard_map/all_gather | solution.py:662
  151.7 43.4 %collective-permute-start.21 = (bf16[64,2048]{1,0:T(8,128)(2,1)}, bf16[64,2048]{1,0:T(8,128)(2,1)}, u32[]{:S(2)}, u32[]{:S(2)}) collective-permute-start(bf16[64,2048]{1,0:T(8,128)(2,1)} %get-tuple-element.283), channel_id=1, source_target_pairs={{0,0},{1,8},{2,16},{3,24},{4,1},{5,9},{6,17},{7,25},{8,2},{9,10},{... | collective-permute-start | bytes 786440 | tf_op jit(solution)/shard_map/cond/branch_1_fun/ppermute | solution.py:625
  155.3 42.7 %collective-permute-start.22 = (bf16[64,2048]{1,0:T(8,128)(2,1)}, bf16[64,2048]{1,0:T(8,128)(2,1)}, u32[]{:S(2)}, u32[]{:S(2)}) collective-permute-start(bf16[64,2048]{1,0:T(8,128)(2,1)} %get-tuple-element.283), channel_id=1, source_target_pairs={{0,8},{1,16},{2,24},{3,0},{4,9},{5,17},{6,25},{7,1},{8,10},{9,18},... | collective-permute-start | bytes 786440 | tf_op jit(solution)/shard_map/cond/branch_1_fun/ppermute | solution.py:625
  157.4 42.2 %collective-permute-start.23 = (bf16[64,2048]{1,0:T(8,128)(2,1)}, bf16[64,2048]{1,0:T(8,128)(2,1)}, u32[]{:S(2)}, u32[]{:S(2)}) collective-permute-start(bf16[64,2048]{1,0:T(8,128)(2,1)} %get-tuple-element.283), channel_id=1, source_target_pairs={{0,16},{1,24},{2,0},{3,8},{4,17},{5,25},{6,1},{7,9},{8,18},{9,26},... | collective-permute-start | bytes 786440 | tf_op jit(solution)/shard_map/cond/branch_1_fun/ppermute | solution.py:625
  160.0 41.2 %collective-permute-start.24 = (bf16[64,2048]{1,0:T(8,128)(2,1)}, bf16[64,2048]{1,0:T(8,128)(2,1)}, u32[]{:S(2)}, u32[]{:S(2)}) collective-permute-start(bf16[64,2048]{1,0:T(8,128)(2,1)} %get-tuple-element.283), channel_id=1, source_target_pairs={{0,24},{1,0},{2,8},{3,16},{4,25},{5,1},{6,9},{7,17},{8,26},{9,2},{... | collective-permute-start | bytes 786440 | tf_op jit(solution)/shard_map/cond/branch_1_fun/ppermute | solution.py:625
  285.5 312.7 %reduce-scatter.3.cloned.1.call-start = ((), (), s32[]{:S(2)}) async-start(), calls=%async_computation.5 | async-start | bytes 2621440 | tf_op jit(solution)/shard_map/reduce_scatter | solution.py:827
  422.9 66.5 %collective-permute-start.13 = (bf16[4,4,128,2048]{3,2,1,0:T(8,128)(2,1)}, bf16[4,4,128,2048]{3,2,1,0:T(8,128)(2,1)}, u32[]{:S(2)}, u32[]{:S(2)}) collective-permute-start(bf16[4,4,128,2048]{3,2,1,0:T(8,128)(2,1)} %get-tuple-element.177), channel_id=1, source_target_pairs={{0,1},{1,0},{2,3},{3,2},{4,5},{5,4},{6,7},{7,6},{8,9},{9,8},{10,11... | collective-permute-start | bytes 25165832 | tf_op jit(solution)/shard_map/cond/branch_1_fun/ppermute | solution.py:31
  489.7 46.3 %collective-permute-start.53 = (bf16[4,4,128,2048]{3,2,1,0:T(8,128)(2,1)}, bf16[4,4,128,2048]{3,2,1,0:T(8,128)(2,1)}, u32[]{:S(2)}, u32[]{:S(2)}) collective-permute-start(bf16[4,4,128,2048]{3,2,1,0:T(8,128)(2,1)} %bitcast.417), channel_id=1, source_target_pairs={{0,1},{1,0},{2,3},{3,2},{4,5},{5,4},{6,7},{7,6},{8,9},{9,8},{10,11... | collective-permute-start | bytes 25165832 | tf_op jit(solution)/shard_map/ppermute | solution.py:31
  493.8 119.7 %reduce-scatter.5.cloned.1.call-start = ((), (), s32[]{:S(2)}) async-start(), calls=%async_computation.6 | async-start | bytes 2621440 | tf_op jit(solution)/shard_map/reduce_scatter | solution.py:826
  495.8 33.2 %collective-permute-start.49 = (bf16[512,2048]{1,0:T(8,128)(2,1)}, bf16[512,2048]{1,0:T(8,128)(2,1)}, u32[]{:S(2)}, u32[]{:S(2)}) collective-permute-start(bf16[512,2048]{1,0:T(8,128)(2,1)} %get-tuple-element.260), channel_id=1, source_target_pairs={{0,1},{1,0},{2,3},{3,2},{4,5},{5,4},{6,7},{7,6},{8,9},{9,8},{10,11... | collective-permute-start | bytes 6291464 | tf_op jit(solution)/shard_map/ppermute | solution.py:31
  532.5 60.7 %collective-permute-start.50 = (bf16[128,2048]{1,0:T(8,128)(2,1)}, bf16[128,2048]{1,0:T(8,128)(2,1)S(1)}, u32[]{:S(2)}, u32[]{:S(2)}) collective-permute-start(bf16[128,2048]{1,0:T(8,128)(2,1)} %get-tuple-element.818), channel_id=1, source_target_pairs={{0,6},{1,7},{2,4},{3,5},{4,2},{5,3},{6,0},{7,1},{8,14},{9,15},{10,... | collective-permute-start | bytes 1572872 | tf_op jit(solution)/shard_map/ppermute | solution.py:31
  534.1 59.1 %collective-permute-start.51 = (bf16[128,2048]{1,0:T(8,128)(2,1)}, bf16[128,2048]{1,0:T(8,128)(2,1)S(1)}, u32[]{:S(2)}, u32[]{:S(2)}) collective-permute-start(bf16[128,2048]{1,0:T(8,128)(2,1)} %get-tuple-element.820), channel_id=1, source_target_pairs={{0,4},{1,5},{2,6},{3,7},{4,0},{5,1},{6,2},{7,3},{8,12},{9,13},{10,... | collective-permute-start | bytes 1572872 | tf_op jit(solution)/shard_map/ppermute | solution.py:31
  535.1 59.0 %collective-permute-start.52 = (bf16[128,2048]{1,0:T(8,128)(2,1)S(1)}, bf16[128,2048]{1,0:T(8,128)(2,1)}, u32[]{:S(2)}, u32[]{:S(2)}) collective-permute-start(bf16[128,2048]{1,0:T(8,128)(2,1)S(1)} %get-tuple-element.819), channel_id=1, source_target_pairs={{0,2},{1,3},{2,0},{3,1},{4,6},{5,7},{6,4},{7,5},{8,10},{9,11},{10,... | collective-permute-start | bytes 1572872 | tf_op jit(solution)/shard_map/ppermute | solution.py:31
  598.1 64.5 %collective-permute-start.58 = (f32[20,4,4,64]{3,1,0,2:T(4,128)S(1)}, f32[20,4,4,64]{3,1,0,2:T(4,128)}, u32[]{:S(2)}, u32[]{:S(2)}) collective-permute-start(f32[20,4,4,64]{3,1,0,2:T(4,128)S(1)} %slice.665), channel_id=1, source_target_pairs={{0,1},{1,0},{2,3},{3,2},{4,5},{5,4},{6,7},{7,6},{8,9},{9,8},{10,11... | collective-permute-start | bytes 245768 | tf_op jit(solution)/shard_map/ppermute | solution.py:31
  601.8 63.8 %collective-permute-start.54 = (bf16[64,512]{1,0:T(8,128)(2,1)}, bf16[64,512]{1,0:T(8,128)(2,1)S(1)}, u32[]{:S(2)}, u32[]{:S(2)}) collective-permute-start(bf16[64,512]{1,0:T(8,128)(2,1)} %get-tuple-element.846), channel_id=1, source_target_pairs={{0,0},{8,1},{16,2},{24,3},{1,4},{9,5},{17,6},{25,7},{2,8},{10,9},{... | collective-permute-start | bytes 196616 | tf_op jit(solution)/shard_map/ppermute | solution.py:846
  603.3 63.8 %collective-permute-start.55 = (bf16[64,512]{1,0:T(8,128)(2,1)}, bf16[64,512]{1,0:T(8,128)(2,1)S(1)}, u32[]{:S(2)}, u32[]{:S(2)}) collective-permute-start(bf16[64,512]{1,0:T(8,128)(2,1)} %get-tuple-element.849), channel_id=1, source_target_pairs={{8,0},{16,1},{24,2},{0,3},{9,4},{17,5},{25,6},{1,7},{10,8},{18,9},... | collective-permute-start | bytes 196616 | tf_op jit(solution)/shard_map/ppermute | solution.py:846
  608.2 58.9 %collective-permute-start.56 = (bf16[64,512]{1,0:T(8,128)(2,1)S(1)}, bf16[64,512]{1,0:T(8,128)(2,1)S(1)}, u32[]{:S(2)}, u32[]{:S(2)}) collective-permute-start(bf16[64,512]{1,0:T(8,128)(2,1)S(1)} %get-tuple-element.848), channel_id=1, source_target_pairs={{16,0},{24,1},{0,2},{8,3},{17,4},{25,5},{1,6},{9,7},{18,8},{26,9},... | collective-permute-start | bytes 196616 | tf_op jit(solution)/shard_map/ppermute | solution.py:846
  608.9 58.2 %collective-permute-start.57 = (bf16[64,512]{1,0:T(8,128)(2,1)S(1)}, bf16[64,512]{1,0:T(8,128)(2,1)S(1)}, u32[]{:S(2)}, u32[]{:S(2)}) collective-permute-start(bf16[64,512]{1,0:T(8,128)(2,1)S(1)} %get-tuple-element.847), channel_id=1, source_target_pairs={{24,0},{0,1},{8,2},{16,3},{25,4},{1,5},{9,6},{17,7},{26,8},{2,9},{... | collective-permute-start | bytes 196616 | tf_op jit(solution)/shard_map/ppermute | solution.py:846
  615.7 65.3 %all-to-all-start.1 = ((bf16[8,3,64,256]{3,2,1,0:T(8,128)(2,1)}), bf16[8,3,64,256]{3,2,1,0:T(8,128)(2,1)}, u32[]{:S(2)}, u32[]{:S(2)}) async-start(bf16[8,3,64,256]{3,2,1,0:T(8,128)(2,1)} %copy.330), calls=%async_computation.3 | async-start | bytes 1572864 | tf_op jit(solution)/shard_map/all_to_all | solution.py:832
  (145 other events, 1451.5 us)
Sparse Core Ops, SparseCore 0:
  109.8 170.5 all-gather.3
  285.6 153.5 all-gather.5
  493.9 44.4 reduce-scatter.2
  540.7 43.1 reduce-scatter.4

commit v5 on v4

--- a/solution.py
+++ b/solution.py
@@ -712,7 +712,7 @@
         )
         datt_b = datt_b.astype(bfloat)
 
-        moe_pairs = pair_sums(after(moe_even, dres_odd), after(moe_odd, dres_odd))
+        moe_pairs = jnp.stack(pair_sums(moe_even, moe_odd))
         cot_planes_odd = swap(cot_planes, "expert", 1)
         gate_tables = [swap(local_probs(router_probs), "dp", kd) for kd in range(1, near)]
 
@@ -825,9 +825,16 @@
 
     late = lax.psum_scatter(late, "dp", scatter_dimension=1, tiled=True)
     early = lax.psum_scatter(early, "dp", scatter_dimension=1, tiled=True)
-    moe = sum_chips(moe_pairs)
+    cut = half // 2
+    moe_arrived = swap(moe_pairs[cut:], "expert", 2 * cut)
     weight_sums = add_sequences(list(range(1, near - 1)), None, dnormed_part)
     dnormed = after(dnormed, weight_sums[0])
+    moe_sums = moe_pairs[:cut].astype(single) + after(moe_arrived, weight_sums[0]).astype(single)
+    while moe_sums.shape[0] > 1:
+        cut = moe_sums.shape[0] // 2
+        arrived = swap(moe_sums[cut:].astype(bfloat), "expert", 2 * cut)
+        moe_sums = moe_sums[:cut] + arrived.astype(single)
+    output = (residual + moe_sums[0]).astype(bfloat)
     summed = jnp.concatenate([early[:1], late], axis=0)
     moved = lax.all_to_all(
         after(summed, weight_sums[0]).reshape(3, n, shard, width).transpose(1, 0, 2, 3),
@@ -850,7 +857,6 @@
     )
     output_grad = output_grad.transpose(1, 0, 2).reshape(shard, model).astype(single)
 
-    output = (residual + moe).astype(bfloat)
     rs_own = rs_in[:rows]
     scaled_in = dnormed * gain_in
     inner_in = jnp.mean(scaled_in * x_own, axis=-1, keepdims=True)
@@ -881,7 +887,7 @@
         total = total + swap(small_sum[:, k], "dp", k)
 
     own_rows = [x_own_cut, d_own_cut, hidden_own, gate_lin_own, up_lin_own]
-    weight_sums = add_sequences([near - 1], own_rows + list(weight_sums), moe)
+    weight_sums = add_sequences([near - 1], own_rows + list(weight_sums))
     gate_grad, up_grad, down_grad = weight_sums
     span = model // m
 

time: 701 us -> 691 us (0.986)
  waiting for transfers between devices: 176 us -> 160 us
  matrix products: 40.4 us -> 48.4 us
    ppermute x57 -> x56, waiting for transfers between devices: 173 us -> 157 us  [swap(): return lax.ppermute(values, axis, [(i, i ^ mask) for i in range(count)])]
    dot_general x22, matrix products: 39.2 us -> 47.2 us  [dot32(): lax.dot_general(left, right, (dims, ((), ())), preferred_element_type=sin...]
    ppermute x57 -> x56, starting transfers between devices: 81.5 us -> 86.4 us  [swap(): return lax.ppermute(values, axis, [(i, i ^ mask) for i in range(count)])]
  transfers between devices with their start and end apart: 71 -> 70, of which waited for: 31 -> 31; matrix products, arithmetic and copies ran while one was open for 25% -> 27% of each run, Pallas kernels for 25% -> 25%
where the time goes in v5:
time: 691 us; the launch traced here: 682 us
  Pallas kernels  174 us (25%)
  waiting for transfers between devices  160 us (23%)
  starting transfers between devices  120 us (17%)
  local copies, waits for them, and re-layouts  84.2 us (12%)
  other arithmetic  70.9 us (10%)
  matrix products  48.4 us (7%)
  between operations  21.9 us (3%)
    ppermute x56, waiting for transfers between devices, swap(): return lax.ppermute(values, axis, [(i, i ^ mask) for i in range(count)])  157 us
    pallas_call x2, Pallas kernels, routed_others(): pl.pallas_call(functools.partial(others_kernel, len(mid), len(cot), group...  93.3 us
    ppermute x56, starting transfers between devices, swap(): return lax.ppermute(values, axis, [(i, i ^ mask) for i in range(count)])  86.4 us
    pallas_call x1, Pallas kernels, routed_own(): pl.pallas_call(functools.partial(own_kernel, groups, block, cap, near, fa...  58 us
    dot_general x22, matrix products, dot32(): lax.dot_general(left, right, (dims, ((), ())), preferred_element_type=sin...  47.2 us
    pallas_call x2, Pallas kernels, attention_call(): pl.pallas_call(kernel, grid=(heads, length // span), in_specs=[specs[kind...  22.7 us
  transfers between devices with their start and end apart: 70, of which 31 were waited for; matrix products, arithmetic and copies ran while one was open for 27% of the time, Pallas kernels for 25%

profile of v5, /device:TPU:0, one launch (start us, length us, event | category | flops | bytes accessed | tf_op | source)
XLA Modules:
  0.0 682.1 jit_solution(14108453306140973360)
XLA Ops:
  11.5 5.2 all-to-all-start
  42.9 10.9 %collective-permute-done.38 = bf16[1,3,512,256]{3,2,1,0:T(8,128)(2,1)S(1)} collective-permute-done((bf16[1,3,512,256]{3,2,1,0:T(8,128)(2,1)S(1)}, bf16[1,3,512,256]{3,2,1,0:T(8,128)(2,1)S(1)}, u32[]{:S(2)}, u32[]{:S(2)}) %collective-permute-start.38) | collective-permute-done | bytes 786464 | tf_op jit(solution)/shard_map/ppermute | solution.py:31
  54.0 16.5 %collective-permute-start.44 = (bf16[2,3,512,256]{3,2,1,0:T(8,128)(2,1)S(1)}, bf16[2,3,512,256]{3,2,1,0:T(8,128)(2,1)S(1)}, u32[]{:S(2)}, u32[]{:S(2)}) collective-permute-start(bf16[2,3,512,256]{3,2,1,0:T(8,128)(2,1)S(1)} %pad_maximum_fusion.13), channel_id=1, source_target_pairs={{0,8},{8,0},{16,24},{24,16},{1,9},{9,1},{17,25},{25,17},{2,10},{10... | collective-permute-start | bytes 4718600 | tf_op jit(solution)/shard_map/ppermute | solution.py:31
  79.5 24.7 %collective-permute-done.44 = bf16[2,3,512,256]{3,2,1,0:T(8,128)(2,1)S(1)} collective-permute-done((bf16[2,3,512,256]{3,2,1,0:T(8,128)(2,1)S(1)}, bf16[2,3,512,256]{3,2,1,0:T(8,128)(2,1)S(1)}, u32[]{:S(2)}, u32[]{:S(2)}) %collective-permute-start.44) | collective-permute-done | bytes 1572896 | tf_op jit(solution)/shard_map/ppermute | solution.py:31
  144.9 132.0 %conditional.2 = (f32[1024,256]{0,1:T(8,128)S(1)}, f32[1024,256]{0,1:T(8,128)}, f32[1024,1]{0,1:T(1,128)S(1)}, f32[1024,1]{0,1:T(1,128)S(1)}, bf16[1024,256]{1,0...) conditional(s32[]{:T(128)} %bitcast.68, () %tuple.40, ...), branch_computations={%region_2.3_spmd, %region_3.7_spmd} | conditional | flops 5391013888 | bytes 126745144 | solution.py:36
  160.4 4.8 collective-permute-start.24
  184.4 9.7 %attend.1 = (bf16[1024,256]{1,0:T(8,128)(2,1)}, f32[2,1024,1]{2,1,0:T(8,128)}) custom-call(bf16[1024,256]{1,0:T(8,128)(2,1)} %pad_maximum_fusion.1.q_ref, bf16[1024,256]{1,0:T(8,128)(2,1)} %pad_maximum_fusion.2.k_ref, bf16[1024,256]{1,0:T(8,128)(2,1)} %convolution_convert_fusion.2.v_ref, s32[1024,1]{1,0:T(8,128)S(1)} %copy.306.pq_ref, ...), custom_call_target="tpu_custom_call" | custom-call | flops 1073741824 | bytes 2097152 | tf_op jit(solution)/shard_map/cond/branch_1_fun/attend/pallas_call | solution.py:460
  210.5 5.7 collective-permute-start.27
  218.8 4.8 collective-permute-done.28
  223.6 15.3 %collective-permute-done.27 = bf16[128,2048]{1,0:T(8,128)(2,1)S(1)} collective-permute-done((bf16[128,2048]{1,0:T(8,128)(2,1)S(1)}, bf16[128,2048]{1,0:T(8,128)(2,1)S(1)}, u32[]{:S(2)}, u32[]{:S(2)}) %collective-permute-start.27) | collective-permute-done | bytes 524320 | tf_op jit(solution)/shard_map/cond/branch_1_fun/ppermute | solution.py:31
  245.3 12.1 %collective-permute-done.31 = bf16[128,2048]{1,0:T(8,128)(2,1)S(1)} collective-permute-done((bf16[128,2048]{1,0:T(8,128)(2,1)S(1)}, bf16[128,2048]{1,0:T(8,128)(2,1)S(1)}, u32[]{:S(2)}, u32[]{:S(2)}) %collective-permute-start.31) | collective-permute-done | bytes 524320 | tf_op jit(solution)/shard_map/cond/branch_1_fun/ppermute | solution.py:31
  257.5 9.6 %collective-permute-done.30 = bf16[128,2048]{1,0:T(8,128)(2,1)S(1)} collective-permute-done((bf16[128,2048]{1,0:T(8,128)(2,1)S(1)}, bf16[128,2048]{1,0:T(8,128)(2,1)S(1)}, u32[]{:S(2)}, u32[]{:S(2)}) %collective-permute-start.30) | collective-permute-done | bytes 524320 | tf_op jit(solution)/shard_map/cond/branch_1_fun/ppermute | solution.py:31
  289.7 198.2 %conditional.3 = (bf16[2,576,1024]{2,1,0:T(8,128)(2,1)}, bf16[2,576,1024]{2,1,0:T(8,128)(2,1)}, bf16[2,576,1024]{2,1,0:T(8,128)(2,1)}, bf16[2,576,512]{2,1,0:T(8...) conditional(s32[]{:T(128)} %bitcast.68, () %tuple.42, ...), branch_computations={%region_11.12_spmd, %region_12.19_spmd} | conditional | flops 40307875840 | bytes 324660192 | solution.py:36
  290.3 58.0 %routed_own.1 = (bf16[2,576,1024]{2,1,0:T(8,128)(2,1)}, bf16[2,576,1024]{2,1,0:T(8,128)(2,1)}, bf16[2,576,1024]{2,1,0:T(8,128)(2,1)}, bf16[2,576,512]{2,1,0:T(8,...) custom-call(s32[2]{0:T(128)S(1)} %get-tuple-element.129.ids_ref, ...), custom_call_target="tpu_custom_call" | custom-call | flops 28991029248 | bytes 50331648 | tf_op jit(solution)/shard_map/cond/branch_1_fun/routed_own/pallas_call | solution.py:314
  358.3 11.3 %collective-permute-done.3 = bf16[128,2048]{1,0:T(8,128)(2,1)S(1)} collective-permute-done((bf16[128,2048]{1,0:T(8,128)(2,1)S(1)}, bf16[128,2048]{1,0:T(8,128)(2,1)S(1)}, u32[]{:S(2)}, u32[]{:S(2)}) %collective-permute-start.3) | collective-permute-done | bytes 524320 | tf_op jit(solution)/shard_map/cond/branch_1_fun/ppermute | solution.py:31
  369.6 11.4 %collective-permute-done.2 = bf16[128,2048]{1,0:T(8,128)(2,1)S(1)} collective-permute-done((bf16[128,2048]{1,0:T(8,128)(2,1)S(1)}, bf16[128,2048]{1,0:T(8,128)(2,1)S(1)}, u32[]{:S(2)}, u32[]{:S(2)}) %collective-permute-start.2) | collective-permute-done | bytes 524320 | tf_op jit(solution)/shard_map/cond/branch_1_fun/ppermute | solution.py:31
  387.5 12.3 %collective-permute-done.6 = bf16[128,2048]{1,0:T(8,128)(2,1)S(1)} collective-permute-done((bf16[128,2048]{1,0:T(8,128)(2,1)S(1)}, bf16[128,2048]{1,0:T(8,128)(2,1)S(1)}, u32[]{:S(2)}, u32[]{:S(2)}) %collective-permute-start.6) | collective-permute-done | bytes 524320 | tf_op jit(solution)/shard_map/cond/branch_1_fun/ppermute | solution.py:31
  399.8 9.4 %collective-permute-done.5 = bf16[128,2048]{1,0:T(8,128)(2,1)S(1)} collective-permute-done((bf16[128,2048]{1,0:T(8,128)(2,1)S(1)}, bf16[128,2048]{1,0:T(8,128)(2,1)S(1)}, u32[]{:S(2)}, u32[]{:S(2)}) %collective-permute-start.5) | collective-permute-done | bytes 524320 | tf_op jit(solution)/shard_map/cond/branch_1_fun/ppermute | solution.py:31
  410.9 7.3 %collective-permute-start.14 = (f32[2,4,256]{2,0,1:T(2,128)S(1)}, f32[2,4,256]{2,0,1:T(2,128)S(1)}, u32[]{:S(2)}, u32[]{:S(2)}) collective-permute-start(f32[2,4,256]{2,0,1:T(2,128)S(1)} %constant_dynamic-slice_fusion), channel_id=1, source_target_pairs={{0,8},{8,0},{16,24},{24,16},{1,9},{9,1},{17,25},{25,17},{2,10},{10... | collective-permute-start | bytes 24584 | tf_op jit(solution)/shard_map/cond/branch_1_fun/ppermute | solution.py:31
  436.2 12.9 %attend_back.1 = (f32[1024,256]{1,0:T(8,128)S(1)}, f32[1024,256]{1,0:T(8,128)S(1)}, f32[1024,256]{1,0:T(8,128)S(1)}) custom-call(bf16[1024,256]{1,0:T(8,128)(2,1)} %get-tuple-element.154.q_ref, bf16[1024,256]{1,0:T(8,128)(2,1)} %get-tuple-element.155.k_ref, bf16[1024,256]{1,0:T(8,128)(2,1)} %get-tuple-element.156.v_ref, ...), custom_call_target="tpu_custom_call" | custom-call | flops 2684354560 | bytes 2097152 | tf_op jit(solution)/shard_map/cond/branch_1_fun/attend_back/pallas_call | solution.py:460
  518.6 55.1 %routed_others.2 = (f32[2,512,1024]{2,1,0:T(8,128)}, f32[2,512,1024]{2,1,0:T(8,128)}, f32[2,1024,512]{2,1,0:T(8,128)}) custom-call(s32[4]{0:T(128)} %pad_add_fusion.1.ids_ref, f32[2,2,4,256]{3,2,1,0:T(4,128)} %copy.327.rank_ref, f32[2,2,4,256]{3,2,1,0:T(4,128)} %pad_maximum_fusion.18.prob_ref, bf16[4,4,128,2048]{3,2,1,0:T(8,128)(2,1)} %bitcast.426, ...), custom_call_target="tpu_custom_call" | custom-call | flops 38654705664 | bytes 67108864 | tf_op jit(solution)/shard_map/routed_others/pallas_call | solution.py:375
  595.0 6.4 collective-permute-start.54
  606.9 38.1 %routed_others.3 = (f32[2,512,1024]{2,1,0:T(8,128)}, f32[2,512,1024]{2,1,0:T(8,128)}, f32[2,1024,512]{2,1,0:T(8,128)}) custom-call(s32[3]{0:T(128)} %pad_add_fusion.2.ids_ref, f32[2,1,4,256]{3,2,1,0:T(4,128)} %fusion.45.rank_ref, f32[2,1,4,256]{3,2,1,0:T(4,128)S(1)} %get-tuple-element.696.prob_ref, ...), custom_call_target="tpu_custom_call", output_to_operand_aliasing={{0}: (15, {}), {1}: (16, {}), {2}: (17, {})} | custom-call | flops 19327352832 | bytes 67108864 | tf_op jit(solution)/shard_map/routed_others/pallas_call | solution.py:375
  648.4 6.9 %collective-permute-start.60 = (f32[20,4,64]{2,1,0:T(4,128)S(1)}, f32[20,4,64]{2,1,0:T(4,128)S(1)}, u32[]{:S(2)}, u32[]{:S(2)}) collective-permute-start(f32[20,4,64]{2,1,0:T(4,128)S(1)} %get-tuple-element.846), channel_id=1, source_target_pairs={{0,6},{1,7},{2,4},{3,5},{4,2},{5,3},{6,0},{7,1},{8,14},{9,15},{10,... | collective-permute-start | bytes 61448 | tf_op jit(solution)/shard_map/ppermute | solution.py:31
  (510 shorter events, 309.3 us)
Async XLA Ops:
  16.6 262.5 %all-gather.4.cloned.1.call-start = ((), (), s32[]{:S(2)}) async-start(), calls=%async_computation.4 | async-start | bytes 10485760 | tf_op jit(solution)/shard_map/all_gather | solution.py:575
  30.7 40.7 %collective-permute-start.35 = (bf16[2,128,2048]{2,1,0:T(8,128)(2,1)S(1)}, bf16[2,128,2048]{2,1,0:T(8,128)(2,1)S(1)}, u32[]{:S(2)}, u32[]{:S(2)}) collective-permute-start(bf16[2,128,2048]{2,1,0:T(8,128)(2,1)S(1)} %maximum_add_fusion.6), channel_id=1, source_target_pairs={{0,6},{1,7},{2,4},{3,5},{4,2},{5,3},{6,0},{7,1},{8,14},{9,15},{10,... | collective-permute-start | bytes 3145736 | tf_op jit(solution)/shard_map/ppermute | solution.py:31
  33.1 44.1 %collective-permute-start.34 = (bf16[2,128,2048]{2,1,0:T(8,128)(2,1)S(1)}, bf16[2,128,2048]{2,1,0:T(8,128)(2,1)S(1)}, u32[]{:S(2)}, u32[]{:S(2)}) collective-permute-start(bf16[2,128,2048]{2,1,0:T(8,128)(2,1)S(1)} %maximum_add_fusion.6), channel_id=1, source_target_pairs={{0,4},{1,5},{2,6},{3,7},{4,0},{5,1},{6,2},{7,3},{8,12},{9,13},{10,... | collective-permute-start | bytes 3145736 | tf_op jit(solution)/shard_map/ppermute | solution.py:31
  33.7 44.6 %collective-permute-start.33 = (bf16[2,128,2048]{2,1,0:T(8,128)(2,1)S(1)}, bf16[2,128,2048]{2,1,0:T(8,128)(2,1)S(1)}, u32[]{:S(2)}, u32[]{:S(2)}) collective-permute-start(bf16[2,128,2048]{2,1,0:T(8,128)(2,1)S(1)} %maximum_add_fusion.6), channel_id=1, source_target_pairs={{0,2},{1,3},{2,0},{3,1},{4,6},{5,7},{6,4},{7,5},{8,10},{9,11},{10,... | collective-permute-start | bytes 3145736 | tf_op jit(solution)/shard_map/ppermute | solution.py:31
  54.0 50.2 %collective-permute-start.44 = (bf16[2,3,512,256]{3,2,1,0:T(8,128)(2,1)S(1)}, bf16[2,3,512,256]{3,2,1,0:T(8,128)(2,1)S(1)}, u32[]{:S(2)}, u32[]{:S(2)}) collective-permute-start(bf16[2,3,512,256]{3,2,1,0:T(8,128)(2,1)S(1)} %pad_maximum_fusion.13), channel_id=1, source_target_pairs={{0,8},{8,0},{16,24},{24,16},{1,9},{9,1},{17,25},{25,17},{2,10},{10... | collective-permute-start | bytes 4718600 | tf_op jit(solution)/shard_map/ppermute | solution.py:31
  108.4 379.5 %all-gather.6.cloned.1.call-start = ((), (), s32[]{:S(2)}) async-start(), calls=%async_computation.7 | async-start | bytes 10485760 | tf_op jit(solution)/shard_map/all_gather | solution.py:662
  152.0 42.1 %collective-permute-start.21 = (bf16[64,2048]{1,0:T(8,128)(2,1)}, bf16[64,2048]{1,0:T(8,128)(2,1)}, u32[]{:S(2)}, u32[]{:S(2)}) collective-permute-start(bf16[64,2048]{1,0:T(8,128)(2,1)} %get-tuple-element.276), channel_id=1, source_target_pairs={{0,0},{1,8},{2,16},{3,24},{4,1},{5,9},{6,17},{7,25},{8,2},{9,10},{... | collective-permute-start | bytes 786440 | tf_op jit(solution)/shard_map/cond/branch_1_fun/ppermute | solution.py:625
  155.6 41.3 %collective-permute-start.22 = (bf16[64,2048]{1,0:T(8,128)(2,1)}, bf16[64,2048]{1,0:T(8,128)(2,1)}, u32[]{:S(2)}, u32[]{:S(2)}) collective-permute-start(bf16[64,2048]{1,0:T(8,128)(2,1)} %get-tuple-element.276), channel_id=1, source_target_pairs={{0,8},{1,16},{2,24},{3,0},{4,9},{5,17},{6,25},{7,1},{8,10},{9,18},... | collective-permute-start | bytes 786440 | tf_op jit(solution)/shard_map/cond/branch_1_fun/ppermute | solution.py:625
  157.9 40.7 %collective-permute-start.23 = (bf16[64,2048]{1,0:T(8,128)(2,1)}, bf16[64,2048]{1,0:T(8,128)(2,1)}, u32[]{:S(2)}, u32[]{:S(2)}) collective-permute-start(bf16[64,2048]{1,0:T(8,128)(2,1)} %get-tuple-element.276), channel_id=1, source_target_pairs={{0,16},{1,24},{2,0},{3,8},{4,17},{5,25},{6,1},{7,9},{8,18},{9,26},... | collective-permute-start | bytes 786440 | tf_op jit(solution)/shard_map/cond/branch_1_fun/ppermute | solution.py:625
  160.4 39.8 %collective-permute-start.24 = (bf16[64,2048]{1,0:T(8,128)(2,1)}, bf16[64,2048]{1,0:T(8,128)(2,1)}, u32[]{:S(2)}, u32[]{:S(2)}) collective-permute-start(bf16[64,2048]{1,0:T(8,128)(2,1)} %get-tuple-element.276), channel_id=1, source_target_pairs={{0,24},{1,0},{2,8},{3,16},{4,25},{5,1},{6,9},{7,17},{8,26},{9,2},{... | collective-permute-start | bytes 786440 | tf_op jit(solution)/shard_map/cond/branch_1_fun/ppermute | solution.py:625
  284.1 298.6 %reduce-scatter.3.cloned.1.call-start = ((), (), s32[]{:S(2)}) async-start(), calls=%async_computation.5 | async-start | bytes 2621440 | tf_op jit(solution)/shard_map/reduce_scatter | solution.py:827
  358.3 67.9 %collective-permute-start.12 = (bf16[512,2048]{1,0:T(8,128)(2,1)}, bf16[512,2048]{1,0:T(8,128)(2,1)}, u32[]{:S(2)}, u32[]{:S(2)}) collective-permute-start(bf16[512,2048]{1,0:T(8,128)(2,1)} %get-tuple-element.175), channel_id=1, source_target_pairs={{0,1},{1,0},{2,3},{3,2},{4,5},{5,4},{6,7},{7,6},{8,9},{9,8},{10,11... | collective-permute-start | bytes 6291464 | tf_op jit(solution)/shard_map/cond/branch_1_fun/ppermute | solution.py:31
  424.9 62.8 %collective-permute-start.13 = (bf16[4,4,128,2048]{3,2,1,0:T(8,128)(2,1)}, bf16[4,4,128,2048]{3,2,1,0:T(8,128)(2,1)}, u32[]{:S(2)}, u32[]{:S(2)}) collective-permute-start(bf16[4,4,128,2048]{3,2,1,0:T(8,128)(2,1)} %get-tuple-element.176), channel_id=1, source_target_pairs={{0,1},{1,0},{2,3},{3,2},{4,5},{5,4},{6,7},{7,6},{8,9},{9,8},{10,11... | collective-permute-start | bytes 25165832 | tf_op jit(solution)/shard_map/cond/branch_1_fun/ppermute | solution.py:31
  492.0 91.8 %reduce-scatter.5.cloned.1.call-start = ((), (), s32[]{:S(2)}) async-start(), calls=%async_computation.6 | async-start | bytes 2621440 | tf_op jit(solution)/shard_map/reduce_scatter | solution.py:826
  497.9 77.8 %collective-permute-start.46 = (bf16[2,128,2048]{2,1,0:T(8,128)(2,1)}, bf16[2,128,2048]{2,1,0:T(8,128)(2,1)S(1)}, u32[]{:S(2)}, u32[]{:S(2)}) collective-permute-start(bf16[2,128,2048]{2,1,0:T(8,128)(2,1)} %slice.647), channel_id=1, source_target_pairs={{0,4},{1,5},{2,6},{3,7},{4,0},{5,1},{6,2},{7,3},{8,12},{9,13},{10,... | collective-permute-start | bytes 3145736 | tf_op jit(solution)/shard_map/ppermute | solution.py:31
  515.1 64.5 %collective-permute-start.52 = (bf16[128,2048]{1,0:T(8,128)(2,1)}, bf16[128,2048]{1,0:T(8,128)(2,1)}, u32[]{:S(2)}, u32[]{:S(2)}) collective-permute-start(bf16[128,2048]{1,0:T(8,128)(2,1)} %get-tuple-element.810), channel_id=1, source_target_pairs={{0,2},{1,3},{2,0},{3,1},{4,6},{5,7},{6,4},{7,5},{8,10},{9,11},{10,... | collective-permute-start | bytes 1572872 | tf_op jit(solution)/shard_map/ppermute | solution.py:31
  516.5 63.2 %collective-permute-start.51 = (bf16[128,2048]{1,0:T(8,128)(2,1)}, bf16[128,2048]{1,0:T(8,128)(2,1)}, u32[]{:S(2)}, u32[]{:S(2)}) collective-permute-start(bf16[128,2048]{1,0:T(8,128)(2,1)} %get-tuple-element.811), channel_id=1, source_target_pairs={{0,4},{1,5},{2,6},{3,7},{4,0},{5,1},{6,2},{7,3},{8,12},{9,13},{10,... | collective-permute-start | bytes 1572872 | tf_op jit(solution)/shard_map/ppermute | solution.py:31
  517.1 62.5 %collective-permute-start.50 = (bf16[128,2048]{1,0:T(8,128)(2,1)}, bf16[128,2048]{1,0:T(8,128)(2,1)}, u32[]{:S(2)}, u32[]{:S(2)}) collective-permute-start(bf16[128,2048]{1,0:T(8,128)(2,1)} %get-tuple-element.809), channel_id=1, source_target_pairs={{0,6},{1,7},{2,4},{3,5},{4,2},{5,3},{6,0},{7,1},{8,14},{9,15},{10,... | collective-permute-start | bytes 1572872 | tf_op jit(solution)/shard_map/ppermute | solution.py:31
  578.3 90.5 %collective-permute-start.48 = (bf16[1,128,2048]{2,1,0:T(8,128)(2,1)}, bf16[1,128,2048]{2,1,0:T(8,128)(2,1)}, u32[]{:S(2)}, u32[]{:S(2)}) collective-permute-start(bf16[1,128,2048]{2,1,0:T(8,128)(2,1)} %slice.1045), channel_id=1, source_target_pairs={{0,2},{1,3},{2,0},{3,1},{4,6},{5,7},{6,4},{7,5},{8,10},{9,11},{10,... | collective-permute-start | bytes 1572872 | tf_op jit(solution)/shard_map/ppermute | solution.py:31
  585.9 85.2 %all-to-all-start.1 = ((bf16[8,3,64,256]{3,2,1,0:T(8,128)(2,1)}), bf16[8,3,64,256]{3,2,1,0:T(8,128)(2,1)}, u32[]{:S(2)}, u32[]{:S(2)}) async-start(bf16[8,3,64,256]{3,2,1,0:T(8,128)(2,1)} %copy.330), calls=%async_computation.3 | async-start | bytes 1572864 | tf_op jit(solution)/shard_map/all_to_all | solution.py:839
  591.1 57.2 %collective-permute-start.56 = (bf16[64,512]{1,0:T(8,128)(2,1)}, bf16[64,512]{1,0:T(8,128)(2,1)}, u32[]{:S(2)}, u32[]{:S(2)}) collective-permute-start(bf16[64,512]{1,0:T(8,128)(2,1)} %get-tuple-element.838), channel_id=1, source_target_pairs={{24,0},{0,1},{8,2},{16,3},{25,4},{1,5},{9,6},{17,7},{26,8},{2,9},{... | collective-permute-start | bytes 196616 | tf_op jit(solution)/shard_map/ppermute | solution.py:853
  593.4 61.8 %collective-permute-start.55 = (bf16[64,512]{1,0:T(8,128)(2,1)}, bf16[64,512]{1,0:T(8,128)(2,1)}, u32[]{:S(2)}, u32[]{:S(2)}) collective-permute-start(bf16[64,512]{1,0:T(8,128)(2,1)} %get-tuple-element.839), channel_id=1, source_target_pairs={{16,0},{24,1},{0,2},{8,3},{17,4},{25,5},{1,6},{9,7},{18,8},{26,9},... | collective-permute-start | bytes 196616 | tf_op jit(solution)/shard_map/ppermute | solution.py:853
  595.0 60.3 %collective-permute-start.54 = (bf16[64,512]{1,0:T(8,128)(2,1)}, bf16[64,512]{1,0:T(8,128)(2,1)}, u32[]{:S(2)}, u32[]{:S(2)}) collective-permute-start(bf16[64,512]{1,0:T(8,128)(2,1)} %get-tuple-element.840), channel_id=1, source_target_pairs={{8,0},{16,1},{24,2},{0,3},{9,4},{17,5},{25,6},{1,7},{10,8},{18,9},... | collective-permute-start | bytes 196616 | tf_op jit(solution)/shard_map/ppermute | solution.py:853
  606.8 40.8 %collective-permute-start.57 = (f32[20,4,4,64]{3,1,0,2:T(4,128)S(1)}, f32[20,4,4,64]{3,1,0,2:T(4,128)S(1)}, u32[]{:S(2)}, u32[]{:S(2)}) collective-permute-start(f32[20,4,4,64]{3,1,0,2:T(4,128)S(1)} %slice.676), channel_id=1, source_target_pairs={{0,1},{1,0},{2,3},{3,2},{4,5},{5,4},{6,7},{7,6},{8,9},{9,8},{10,11... | collective-permute-start | bytes 245768 | tf_op jit(solution)/shard_map/ppermute | solution.py:31
  (112 other events, 1023.0 us)
Sparse Core Ops, SparseCore 0:
  108.5 170.6 all-gather.3
  284.2 155.3 all-gather.5
  492.1 43.7 reduce-scatter.2
  538.1 43.2 reduce-scatter.4
